TPU v7x, 32 devices: a whole 2x2x4 slice. The times are simulated.
32 devices in a mesh: groups: 2 (over y), blk: 16 (over z, x, core).
Axes of the slice: x: 2, y: 2, z: 4, core: 2. Of those that a mesh axis runs over, the one named last changes fastest.
Arguments:
- snapshots: bfloat16 [64, 64, 16, 128], P(None, ('groups', 'blk')), parts along dimension 1, may hold values from -200 to 200
- old_modes: bfloat16 [192, 64, 16, 128], P(None, ('groups', 'blk')), parts along dimension 1, may hold values from -60 to 60
- mode_scales: float32 [384], P('groups'), parts along dimension 0, may hold values from 0.3 to 3
- plane_counts: int32 [32], P(('groups', 'blk')), parts along dimension 0, may hold values from 1 to 2, 20 in all
- links: int32 [32, 2], P(('groups', 'blk')), parts along dimension 0, may hold values from 0 to 1, as said below
Outputs:
- new_modes: bfloat16 [256, 64, 16, 128], P(None, ('groups', 'blk')), parts along dimension 1
- factor: float32 [512, 256], P('groups'), parts along dimension 0
There are 2 independent parts, one for each index of `groups`. A program takes and returns all parts, laid end to end along the dimension named above; each array names one. Nothing has to cross between parts.
Inputs may be any that keep to these rules, and one draw needn't show every extreme that they name: links[b, 1] equals links[b + 1 mod 16, 0]; 1 joins two blocks, 0 is a wall.
All inputs are finite; a program needn't handle non-finite values. No bound on the sum of `plane_counts` on one device may be relied on, other than what follows from the above.
Results may differ from a plain program's by a relative error of at most 0.0095.
Values may be sent and summed in bfloat16 or wider, within the bound.
No kernel may reach another device: no remote copies, remote signals or barrier semaphores. Data moves between devices by JAX's collectives and lax.ppermute only.
A program may use at most 128 MiB of HBM per device.

v0:
```python
import jax
import jax.numpy as jnp
from jax import lax
from jax.sharding import PartitionSpec as P


def with_halo(x, sides, width):
    for axis, dim in sides:
        peers, length = (lax.axis_size(axis), x.shape[dim])
        up = [(i, (i + 1) % peers) for i in range(peers)]
        down = [(j, i) for i, j in up]
        last = lax.slice_in_dim(x, length - width, length, axis=dim)
        leading = lax.slice_in_dim(x, 0, width, axis=dim)
        before = lax.ppermute(last, axis, up)
        after = lax.ppermute(leading, axis, down)
        x = jnp.concatenate([before, x, after], axis=dim)
    return x


def smooth_along(field, along):
    widths = [(0, 0)] * field.ndim
    widths[along] = (1, 1)
    padded = jnp.pad(field, widths)
    length = field.shape[along]
    lower = lax.slice_in_dim(padded, 0, length, axis=along)
    upper = lax.slice_in_dim(padded, 2, length + 2, axis=along)
    return 0.25 * lower + 0.5 * field + 0.25 * upper


def gram_term(left_rows, right_rows):
    return lax.dot_general(
        left_rows, right_rows, (((1,), (1,)), ((), ())), preferred_element_type=jnp.float32
    )


def exact_dot(left_mat, right_mat):
    return jnp.dot(left_mat, right_mat, precision=lax.Precision.HIGHEST)


def leaf_factor(matrix):
    order = matrix.shape[0]
    row_ids = lax.iota(jnp.int32, order)
    lower = jnp.zeros((order, order), jnp.float32)
    for column in range(order):
        residue = matrix[:, column] - exact_dot(lower, lower[column, :])
        pivot = jnp.sqrt(residue[column])
        lower = lower.at[:, column].set(jnp.where(row_ids >= column, residue / pivot, 0.0))
    inverse = jnp.zeros((order, order), jnp.float32)
    for row in range(order):
        target = jnp.zeros((order,), jnp.float32).at[row].set(1.0)
        solved = (target - exact_dot(lower[row, :], inverse)) / lower[row, row]
        inverse = inverse.at[row, :].set(solved)
    return (lower, inverse)


def lower_factor(matrix):
    order = matrix.shape[0]
    if order <= 8:
        return leaf_factor(matrix)
    half = order // 2
    lower_one, inverse_one = lower_factor(matrix[:half, :half])
    below = exact_dot(matrix[half:, :half], inverse_one.T)
    rest = matrix[half:, half:] - exact_dot(below, below.T)
    lower_two, inverse_two = lower_factor(rest)
    corner = -exact_dot(inverse_two, exact_dot(below, inverse_one))
    top_zero = jnp.zeros((half, order - half), jnp.float32)
    lower = jnp.concatenate(
        [
            jnp.concatenate([lower_one, top_zero], axis=1),
            jnp.concatenate([below, lower_two], axis=1),
        ],
        axis=0,
    )
    inverse = jnp.concatenate(
        [
            jnp.concatenate([inverse_one, top_zero], axis=1),
            jnp.concatenate([corner, inverse_two], axis=1),
        ],
        axis=0,
    )
    return (lower, inverse)


def shards(snapshots, old_modes, mode_scales, plane_counts, links):
    new_count, plane_slots, rows_y, rows_z = snapshots.shape
    keep_count = old_modes.shape[0]
    columns = new_count + keep_count
    plane_count = plane_counts[0]
    plane_ids = lax.iota(jnp.int32, plane_slots)
    alive_mask = (plane_ids < plane_count).astype(jnp.float32)[None, :, None, None]
    last_pick = (plane_ids == plane_count - 1).astype(jnp.float32)[None, :, None, None]
    masked = snapshots.astype(jnp.float32) * alive_mask
    first_plane = masked[:, 0]
    last_plane = jnp.sum(masked * last_pick, axis=1)
    edge_planes = jnp.stack([first_plane, last_plane], axis=1).astype(jnp.bfloat16)
    widened = with_halo(edge_planes, (("blk", 1),), 1)
    left_halo = widened[:, 0].astype(jnp.float32) * links[0, 0].astype(jnp.float32)
    right_halo = widened[:, 3].astype(jnp.float32) * links[0, 1].astype(jnp.float32)
    behind = jnp.concatenate([left_halo[:, None], masked[:, :-1]], axis=1)
    forward = jnp.concatenate([masked[:, 1:], jnp.zeros_like(masked[:, :1])], axis=1)
    forward = forward + last_pick * right_halo[:, None]
    along_planes = 0.25 * behind + 0.5 * masked + 0.25 * forward
    filtered = (smooth_along(smooth_along(along_planes, 2), 3) * alive_mask).astype(jnp.bfloat16)
    scaled = (mode_scales[:, None, None, None] * old_modes.astype(jnp.float32) * alive_mask).astype(
        jnp.bfloat16
    )
    stacked = jnp.concatenate([filtered, scaled], axis=0).reshape(
        columns, plane_slots * rows_y * rows_z
    )
    cell_total = lax.axis_size("blk") * stacked.shape[1]
    local_gram = gram_term(stacked, stacked)
    gram = lax.psum(local_gram, "blk") / cell_total
    lower, inverse_lower = lower_factor(gram)
    factor = lower.T
    inverse_high = inverse_lower.astype(jnp.bfloat16)
    inverse_low = (inverse_lower - inverse_high.astype(jnp.float32)).astype(jnp.bfloat16)
    result = jnp.dot(inverse_high, stacked, preferred_element_type=jnp.float32)
    result = result + jnp.dot(inverse_low, stacked, preferred_element_type=jnp.float32)
    return (result.reshape(columns, plane_slots, rows_y, rows_z).astype(jnp.bfloat16), factor)


def solution(mesh):
    return jax.shard_map(
        shards,
        mesh=mesh,
        in_specs=(
            P(None, ("groups", "blk"), None, None),
            P(None, ("groups", "blk"), None, None),
            P("groups"),
            P(("groups", "blk")),
            P(("groups", "blk"), None),
        ),
        out_specs=(P(None, ("groups", "blk"), None, None), P("groups", None)),
        check_vma=False,
    )
```

profile of v0, /device:TPU:0, one launch (start us, length us, event | category | flops | bytes accessed | tf_op | source)
XLA Modules:
  0.0 922.3 jit_solution(12888956410553050702)
XLA Ops:
  7.9 1.4 multiply_reduce_fusion
  9.4 5.5 collective-permute-start.1
  22.4 1.0 collective-permute-done
  24.7 1.4 convolution_bitcast_fusion
  26.1 1.5 pad_maximum_fusion
  27.7 2.9 copy.589
  30.6 84.6 %all-reduce.131.cloned.1.call-done = f32[256,256]{1,0:T(8,128)} async-done(((f32[256,256]{1,0:T(8,128)}), f32[256,256]{1,0:T(8,128)}) %all-reduce.131.cloned.1.call-update) | async-done | bytes 262160 | tf_op jit(solution)/shard_map/psum | solution.py:112
  115.3 1.0 broadcast_multiply_fusion
  139.7 0.8 fusion.32
  161.8 0.8 fusion.54
  163.5 0.8 fusion.60
  188.8 0.8 fusion.94
  213.1 0.8 fusion.122
  213.9 0.8 fusion.125
  238.8 0.8 fusion.156
  260.9 0.8 fusion.178
  261.8 0.8 fusion.181
  287.9 0.8 fusion.218
  311.1 0.8 fusion.243
  312.8 0.8 fusion.249
  337.2 0.8 fusion.277
  338.1 0.8 fusion.280
  360.2 0.8 fusion.302
  361.9 0.8 fusion.308
  387.2 0.8 fusion.342
  411.9 0.8 fusion.373
  436.7 0.8 fusion.404
  459.1 0.8 fusion.426
  486.1 0.8 fusion.466
  511.1 0.8 fusion.497
  536.7 0.8 fusion.528
  558.8 0.8 fusion.550
  586.2 0.8 fusion.590
  610.9 0.8 fusion.621
  635.7 0.8 fusion.652
  657.9 0.8 fusion.674
  684.9 0.8 fusion.714
  709.9 0.8 fusion.745
  735.0 0.8 fusion.776
  757.2 0.8 fusion.798
  784.2 0.8 fusion.838
  808.9 0.8 fusion.869
  834.1 0.8 fusion.900
  856.2 0.8 fusion.922
  883.4 0.8 fusion.962
  908.8 0.8 fusion.993
  910.0 0.8 copy.591
  913.4 1.8 copy.625
  (2228 shorter events, 611.1 us)
Async XLA Ops:
  7.2 7.7 copy-start.3
  7.2 108.1 %all-reduce.131.cloned.1.call-start = ((), (), s32[]{:S(2)}) async-start(), calls=%async_computation | async-start | bytes 524288 | tf_op jit(solution)/shard_map/psum | solution.py:112
  7.9 7.0 copy-start.1
  9.4 13.0 %collective-permute-start.1 = (bf16[64,1,16,128]{3,0,2,1:T(8,128)(2,1)S(1)}, bf16[64,1,16,128]{3,0,2,1:T(8,128)(2,1)S(1)}, u32[]{:S(2)}, u32[]{:S(2)}) collective-permute-start(bf16[64,1,16,128]{3,0,2,1:T(8,128)(2,1)S(1)} %slice.17541), channel_id=1, source_target_pairs={{1,0},{2,1},{3,2},{4,3},{5,4},{6,5},{7,6},{8,7},{9,8},{10,9},{11,1... | collective-permute-start | bytes 786440 | tf_op jit(solution)/shard_map/ppermute | solution.py:15
  14.8 0.9 copy-start.2
  14.8 8.5 collective-permute-start
  15.6 7.8 copy-start
  27.6 106.5 %copy-start.11 = (f32[8]{0:T(128)S(1)}, f32[8]{0:T(128)}, u32[]{:S(2)}) copy-start(f32[8]{0:T(128)} %constant.13709.clone.1) | copy-start | bytes 100
  27.6 107.3 %copy-start.10 = (f32[8]{0:T(128)S(1)}, f32[8]{0:T(128)}, u32[]{:S(2)}) copy-start(f32[8]{0:T(128)} %constant.13724.clone.1) | copy-start | bytes 100
  27.6 108.1 %copy-start.9 = (f32[8]{0:T(128)S(1)}, f32[8]{0:T(128)}, u32[]{:S(2)}) copy-start(f32[8]{0:T(128)} %constant.13725.clone.1) | copy-start | bytes 100
  27.6 108.9 %copy-start.8 = (f32[8]{0:T(128)S(1)}, f32[8]{0:T(128)}, u32[]{:S(2)}) copy-start(f32[8]{0:T(128)} %constant.13726.clone.1) | copy-start | bytes 100
  27.6 109.7 %copy-start.7 = (f32[8]{0:T(128)S(1)}, f32[8]{0:T(128)}, u32[]{:S(2)}) copy-start(f32[8]{0:T(128)} %constant.13727.clone.1) | copy-start | bytes 100
  27.6 110.4 %copy-start.6 = (f32[8]{0:T(128)S(1)}, f32[8]{0:T(128)}, u32[]{:S(2)}) copy-start(f32[8]{0:T(128)} %constant.13728.clone.1) | copy-start | bytes 100
  27.7 111.2 %copy-start.5 = (f32[8]{0:T(128)S(1)}, f32[8]{0:T(128)}, u32[]{:S(2)}) copy-start(f32[8]{0:T(128)} %constant.13729.clone.1) | copy-start | bytes 100
  27.7 112.0 %copy-start.4 = (f32[8]{0:T(128)S(1)}, f32[8]{0:T(128)}, u32[]{:S(2)}) copy-start(f32[8]{0:T(128)} %constant.13730.clone.1) | copy-start | bytes 100
Sparse Core Ops, SparseCore 0:
  26.2 88.9 all-reduce.130
where the time goes:
time: 937 us; the launch traced here: 922 us
  matrix products  245 us (26%)
  local copies, waits for them, and re-layouts  242 us (26%)
  between operations  178 us (19%)
  other arithmetic  166 us (18%)
  waiting for transfers between devices  85.6 us (9%)
    dot_general x605, matrix products, exact_dot(): return jnp.dot(left_mat, right_mat, precision=lax.Precision.HIGHEST)  243 us
    another operation x423, other arithmetic  157 us
    slice x224, local copies, waits for them, and re-layouts, leaf_factor(): pivot = jnp.sqrt(residue[column])  134 us
    psum x1, waiting for transfers between devices, shards(): gram = lax.psum(local_gram, 'blk') / cell_total  84.6 us
    slice x64, local copies, waits for them, and re-layouts, leaf_factor(): solved = (target - exact_dot(lower[row, :], inverse)) / lower[row, row]  42.5 us
    scatter x256, local copies, waits for them, and re-layouts, leaf_factor(): lower.at[:, column].set(jnp.where(row_ids >= column, residue / pivot, 0.0))  21.1 us
    another operation x256, local copies, waits for them, and re-layouts  20.9 us
  transfers between devices with their start and end apart: 3, of which 2 were waited for; matrix products, arithmetic and copies ran while one was open for 1% of the time, Pallas kernels for 0%

commit v1 on v0

--- a/solution.py
+++ b/solution.py
@@ -1,7 +1,13 @@
 import jax
 import jax.numpy as jnp
 from jax import lax
+from jax.experimental import pallas as pl
+from jax.experimental.pallas import tpu as pltpu
 from jax.sharding import PartitionSpec as P
+
+PANEL = 16
+LANES = 128
+SUBS = 8
 
 
 def with_halo(x, sides, width):
@@ -33,52 +39,118 @@
     )
 
 
-def exact_dot(left_mat, right_mat):
-    return jnp.dot(left_mat, right_mat, precision=lax.Precision.HIGHEST)
-
-
-def leaf_factor(matrix):
-    order = matrix.shape[0]
-    row_ids = lax.iota(jnp.int32, order)
-    lower = jnp.zeros((order, order), jnp.float32)
-    for column in range(order):
-        residue = matrix[:, column] - exact_dot(lower, lower[column, :])
-        pivot = jnp.sqrt(residue[column])
-        lower = lower.at[:, column].set(jnp.where(row_ids >= column, residue / pivot, 0.0))
-    inverse = jnp.zeros((order, order), jnp.float32)
-    for row in range(order):
-        target = jnp.zeros((order,), jnp.float32).at[row].set(1.0)
-        solved = (target - exact_dot(lower[row, :], inverse)) / lower[row, row]
-        inverse = inverse.at[row, :].set(solved)
-    return (lower, inverse)
-
-
-def lower_factor(matrix):
-    order = matrix.shape[0]
-    if order <= 8:
-        return leaf_factor(matrix)
-    half = order // 2
-    lower_one, inverse_one = lower_factor(matrix[:half, :half])
-    below = exact_dot(matrix[half:, :half], inverse_one.T)
-    rest = matrix[half:, half:] - exact_dot(below, below.T)
-    lower_two, inverse_two = lower_factor(rest)
-    corner = -exact_dot(inverse_two, exact_dot(below, inverse_one))
-    top_zero = jnp.zeros((half, order - half), jnp.float32)
-    lower = jnp.concatenate(
-        [
-            jnp.concatenate([lower_one, top_zero], axis=1),
-            jnp.concatenate([below, lower_two], axis=1),
+def factor_panel(tile, tiles, panel, t_ref, f_ref, x_ref, cols, rows, vpad):
+    first = pl.multiple_of(panel * PANEL, PANEL)
+    off = pl.multiple_of(first - tile * LANES, PANEL)
+    here = pl.ds(first, PANEL)
+    lane = lax.broadcasted_iota(jnp.int32, (PANEL, LANES), 1)
+    sub = lax.broadcasted_iota(jnp.int32, (PANEL, LANES), 0)
+    inside = (lane >= off) & (lane < off + PANEL)
+    own = t_ref[here, tile * LANES:(tile + 1) * LANES]
+    for s in range(tiles):
+        if s == tile:
+            block = jnp.where(inside, jnp.where(lane - off == sub, 1.0, 0.0), own)
+        else:
+            block = t_ref[here, s * LANES:(s + 1) * LANES]
+        rows[pl.ds(s, PANEL, stride=SUBS), :] = block
+    rows[pl.ds(tiles, PANEL, stride=SUBS), :] = own
+    turned = pltpu.roll(own, lax.rem(LANES - off, LANES), axis=1)
+    for j in range(PANEL):
+        cols[j] = jnp.broadcast_to(turned[:, j:j + 1], (PANEL, LANES))
+    entry = [
+        [jnp.broadcast_to(cols[j, i:i + 1, :], (SUBS, LANES)) for j in range(i + 1)]
+        for i in range(PANEL)
+    ]
+    y = [rows[i * SUBS:(i + 1) * SUBS, :] for i in range(PANEL)]
+    unit = [[None] * PANEL for _ in range(PANEL)]
+    recip = []
+    for k in range(PANEL):
+        recip.append(1.0 / entry[k][k])
+        for i in range(k + 1, PANEL):
+            unit[i][k] = entry[i][k] * recip[k]
+        for j in range(k + 1, PANEL):
+            for i in range(j, PANEL):
+                entry[i][j] = entry[i][j] - unit[i][k] * entry[j][k]
+        for i in range(k + 1, PANEL):
+            y[i] = y[i] - unit[i][k] * y[k]
+    v = [recip[i] * y[i] for i in range(PANEL)]
+    for j in reversed(range(PANEL)):
+        for i in range(j):
+            v[i] = v[i] - unit[j][i] * v[j]
+    for i in range(PANEL):
+        rows[i * SUBS:(i + 1) * SUBS, :] = v[i]
+    for s in range(tiles):
+        vpad[pl.ds(off, PANEL), s * LANES:(s + 1) * LANES] = rows[pl.ds(s, PANEL, stride=SUBS), :]
+    for i in range(PANEL):
+        rows[i * SUBS:(i + 1) * SUBS, :] = jnp.sqrt(recip[i]) * y[i]
+    zero = jnp.zeros((PANEL, LANES), jnp.float32)
+    for s in range(tiles):
+        span = slice(s * LANES, (s + 1) * LANES)
+        part = rows[pl.ds(s, PANEL, stride=SUBS), :]
+        if s == tile:
+            whole = rows[pl.ds(tiles, PANEL, stride=SUBS), :]
+            f_ref[here, span] = jnp.where(lane >= off + sub, whole, 0.0)
+            x_ref[here, span] = jnp.where(lane <= off + sub, part, 0.0)
+        else:
+            f_ref[here, span] = part if s > tile else zero
+            x_ref[here, span] = part if s < tile else zero
+    low = tile * LANES
+    order = t_ref.shape[0]
+    update = jnp.dot(
+        t_ref[low:, low:low + LANES],
+        vpad[...],
+        precision=lax.Precision.HIGHEST,
+        preferred_element_type=jnp.float32,
+    )
+    row_id = lax.broadcasted_iota(jnp.int32, (order - low, LANES), 0) + low
+    lane_id = lax.broadcasted_iota(jnp.int32, (order - low, LANES), 1)
+    below = row_id >= first + PANEL
+    mine = (lane_id >= off) & (lane_id < off + PANEL)
+    for s in range(tiles):
+        span = slice(s * LANES, (s + 1) * LANES)
+        held = t_ref[low:, span]
+        base = jnp.where(mine, 0.0, held) if s == tile else held
+        t_ref[low:, span] = jnp.where(below, base - update[:, span], held)
+    vpad[pl.ds(off, PANEL), :] = jnp.zeros((PANEL, order), jnp.float32)
+
+
+def factor_kernel(scale, gram_ref, f_ref, high_ref, low_ref, t_ref, x_ref, cols, rows, vpad):
+    order = gram_ref.shape[0]
+    tiles = order // LANES
+    t_ref[...] = gram_ref[...] * scale
+    vpad[...] = jnp.zeros(vpad.shape, jnp.float32)
+    per_tile = LANES // PANEL
+    rows[...] = jnp.zeros(rows.shape, jnp.float32)
+    for tile in range(tiles):
+        @pl.loop(tile * per_tile, (tile + 1) * per_tile)
+        def _(panel):
+            factor_panel(tile, tiles, panel, t_ref, f_ref, x_ref, cols, rows, vpad)
+    whole = x_ref[...]
+    high = whole.astype(jnp.bfloat16)
+    high_ref[...] = high
+    low_ref[...] = (whole - high.astype(jnp.float32)).astype(jnp.bfloat16)
+
+
+def factor_and_inverse(gram_sum, cell_total):
+    order = gram_sum.shape[0]
+    square = (order, order)
+    return pl.pallas_call(
+        lambda *refs: factor_kernel(1.0 / cell_total, *refs),
+        out_shape=[
+            jax.ShapeDtypeStruct(square, jnp.float32),
+            jax.ShapeDtypeStruct(square, jnp.bfloat16),
+            jax.ShapeDtypeStruct(square, jnp.bfloat16),
         ],
-        axis=0,
-    )
-    inverse = jnp.concatenate(
-        [
-            jnp.concatenate([inverse_one, top_zero], axis=1),
-            jnp.concatenate([corner, inverse_two], axis=1),
+        scratch_shapes=[
+            pltpu.VMEM(square, jnp.float32),
+            pltpu.VMEM(square, jnp.float32),
+            pltpu.VMEM((PANEL, PANEL, LANES), jnp.float32),
+            pltpu.VMEM((PANEL * SUBS, LANES), jnp.float32),
+            pltpu.VMEM((LANES, order), jnp.float32),
         ],
-        axis=0,
-    )
-    return (lower, inverse)
+        compiler_params=pltpu.CompilerParams(vmem_limit_bytes=32 * 1024 * 1024),
+        name="factor",
+    )(gram_sum)
 
 
 def shards(snapshots, old_modes, mode_scales, plane_counts, links):
@@ -109,11 +181,8 @@
     )
     cell_total = lax.axis_size("blk") * stacked.shape[1]
     local_gram = gram_term(stacked, stacked)
-    gram = lax.psum(local_gram, "blk") / cell_total
-    lower, inverse_lower = lower_factor(gram)
-    factor = lower.T
-    inverse_high = inverse_lower.astype(jnp.bfloat16)
-    inverse_low = (inverse_lower - inverse_high.astype(jnp.float32)).astype(jnp.bfloat16)
+    gram_sum = lax.psum(local_gram, "blk")
+    factor, inverse_high, inverse_low = factor_and_inverse(gram_sum, cell_total)
     result = jnp.dot(inverse_high, stacked, preferred_element_type=jnp.float32)
     result = result + jnp.dot(inverse_low, stacked, preferred_element_type=jnp.float32)
     return (result.reshape(columns, plane_slots, rows_y, rows_z).astype(jnp.bfloat16), factor)

time: 937 us -> 138 us (0.15); the launches traced: 922 us -> 137 us
  matrix products: 245 us -> 2.93 us
  local copies, waits for them, and re-layouts: 242 us -> 6.36 us
  between operations: 178 us -> 16.2 us
  other arithmetic: 166 us -> 4.86 us
  Pallas kernels: 0 us -> 13.7 us
    dot_general x605 -> x0, matrix products: 243 us -> none  [exact_dot(): return jnp.dot(left_mat, right_mat, precision=lax.Precision.HIGHEST)]
    slice x320 -> x0, local copies, waits for them, and re-layouts: 187 us -> none  [the longest x224 134 us: leaf_factor(): pivot = jnp.sqrt(residue[column])]
    another operation x423 -> x0, other arithmetic: 157 us -> none
    scatter x512 -> x0, local copies, waits for them, and re-layouts: 27.1 us -> none  [the longest x256 21.1 us: leaf_factor(): lower.at[:, column].set(jnp.where(row_ids >= column, residue / pivot, 0.0))]
    another operation x256 -> x0, local copies, waits for them, and re-layouts: 20.9 us -> none
    pallas_call x0 -> x1, Pallas kernels: none -> 13.7 us  [factor_and_inverse(): pl.pallas_call(lambda *refs: factor_kernel(1.0 / cell_total, *refs), out_...]
  transfers between devices with their start and end apart: 3 -> 3, of which waited for: 2 -> 3; matrix products, arithmetic and copies ran while one was open for 1% -> 4% of each run, Pallas kernels for 0% -> 0%
where the time goes in v1:
time: 138 us; the launch traced here: 137 us
  waiting for transfers between devices  87.7 us (64%)
  between operations  16.2 us (12%)
  Pallas kernels  13.7 us (10%)
  local copies, waits for them, and re-layouts  6.36 us (5%)
  starting transfers between devices  5.51 us (4%)
  other arithmetic  4.86 us (4%)
  matrix products  2.93 us (2%)
    psum x1, waiting for transfers between devices, shards(): gram_sum = lax.psum(local_gram, 'blk')  82.1 us
    pallas_call x1, Pallas kernels, factor_and_inverse(): pl.pallas_call(lambda *refs: factor_kernel(1.0 / cell_total, *refs), out_...  13.7 us
    ppermute x1, starting transfers between devices, with_halo(): after = lax.ppermute(leading, axis, down)  5.47 us
    ppermute x1, waiting for transfers between devices, with_halo(): before = lax.ppermute(last, axis, up)  4.56 us
    concatenate x1, local copies, waits for them, and re-layouts, shards(): jnp.concatenate([filtered, scaled], axis=0)  2.86 us
    unnamed x11, local copies, waits for them, and re-layouts  2.77 us
  transfers between devices with their start and end apart: 3, of which 3 were waited for; matrix products, arithmetic and copies ran while one was open for 4% of the time, Pallas kernels for 0%

profile of v1, /device:TPU:0, one launch (start us, length us, event | category | flops | bytes accessed | tf_op | source)
XLA Modules:
  0.0 137.3 jit_solution(8012813069154270579)
XLA Ops:
  7.2 0.0 copy-start.4
  7.2 0.0 copy-start.2
  7.2 0.0 all-reduce.5.cloned.1.call-start
  8.0 1.3 multiply_reduce_fusion
  9.4 5.5 %collective-permute-start.1 = (bf16[64,1,16,128]{3,0,2,1:T(8,128)(2,1)S(1)}, bf16[64,1,16,128]{3,0,2,1:T(8,128)(2,1)S(1)}, u32[]{:S(2)}, u32[]{:S(2)}) collective-permute-start(bf16[64,1,16,128]{3,0,2,1:T(8,128)(2,1)S(1)} %slice.70), channel_id=1, source_target_pairs={{1,0},{2,1},{3,2},{4,3},{5,4},{6,5},{7,6},{8,7},{9,8},{10,9},{11,1... | collective-permute-start | bytes 786440 | tf_op jit(solution)/shard_map/ppermute | solution.py:21
  14.8 0.0 copy-start.3
  14.8 0.0 collective-permute-start
  14.8 0.0 copy-done.4
  14.8 0.0 copy-done.2
  14.8 0.8 multiply_convert_fusion
  15.6 0.0 copy-start.1
  15.6 0.1 fusion.14
  15.7 0.0 copy-done.3
  15.8 0.6 fusion.15
  17.6 1.1 collective-permute-done.1
  18.8 4.6 %collective-permute-done = bf16[64,1,16,128]{3,0,2,1:T(8,128)(2,1)S(1)} collective-permute-done((bf16[64,1,16,128]{3,0,2,1:T(8,128)(2,1)S(1)}, bf16[64,1,16,128]{3,0,2,1:T(8,128)(2,1)S(1)}, u32[]{:S(2)}, u32[]{:S(2)}) %collective-permute-start) | collective-permute-done | bytes 262176 | tf_op jit(solution)/shard_map/ppermute | solution.py:20
  23.4 0.0 copy-done.1
  23.4 0.4 fusion.13
  23.8 0.2 fusion.4
  24.0 0.6 fusion.10
  24.6 1.4 %convolution_bitcast_fusion = f32[256,256]{1,0:T(8,128)} fusion(bf16[192,2,16,128]{3,0,2,1:T(8,128)(2,1)S(1)} %multiply_convert_fusion, bf16[64,2,16,128]{3,0,2,1:T(8,128)(2,1)S(1)} %fusion.10), kind=kOutput, calls=%fused_computation.9 | convolution fusion | flops 541065216 | bytes 2359296 | tf_op jit(solution)/shard_map/dot_general | solution.py:37
  26.0 0.0 all-reduce.5.cloned.1.call-update
  26.1 1.5 %pad_maximum_fusion = bf16[256,2,16,128]{3,0,2,1:T(8,128)(2,1)} fusion(bf16[192,2,16,128]{3,0,2,1:T(8,128)(2,1)S(1)} %multiply_convert_fusion, bf16[64,2,16,128]{3,0,2,1:T(8,128)(2,1)S(1)} %fusion.10), kind=kLoop, calls=%fused_computation.5 | loop fusion | flops 4194304 | bytes 4194304 | tf_op jit(solution)/shard_map/concatenate | solution.py:179
  27.6 2.9 %copy.11 = bf16[256,2,16,128]{0,3,2,1:T(8,128)(2,1)S(1)} copy(bf16[256,2,16,128]{3,0,2,1:T(8,128)(2,1)} %pad_maximum_fusion) | data formatting | bytes 4194304 | tf_op jit(solution)/shard_map/concatenate | solution.py:179
  30.4 82.1 %all-reduce.5.cloned.1.call-done.refs_0_ = f32[256,256]{1,0:T(8,128)} async-done(((f32[256,256]{1,0:T(8,128)}), f32[256,256]{1,0:T(8,128)}) %all-reduce.5.cloned.1.call-update) | async-done | bytes 262160 | tf_op jit(solution)/shard_map/psum | solution.py:184
  112.5 0.0 copy-start
  112.5 0.9 copy-done
  113.5 13.7 %factor.1 = (f32[256,256]{1,0:T(8,128)}, bf16[256,256]{1,0:T(8,128)(2,1)S(1)}, bf16[256,256]{1,0:T(8,128)(2,1)S(1)}) custom-call(f32[256,256]{1,0:T(8,128)S(1)} %copy-done), custom_call_target="tpu_custom_call" | custom-call | tf_op jit(solution)/shard_map/factor/pallas_call | solution.py:137
  127.1 0.7 fusion.16
  127.9 0.7 fusion.1
  128.6 1.8 %copy.13 = bf16[32,8,32,128]{3,2,1,0:T(8,128)(2,1)} copy(bf16[32,8,32,128]{3,1,2,0:T(8,128)(2,1)S(1)} %fusion.1) | data formatting | bytes 4194304
  (4 shorter events, 0.1 us)
Async XLA Ops:
  7.2 7.7 %copy-start.4 = (f32[192]{0:T(256)S(1)}, f32[192]{0:T(256)}, u32[]{:S(2)}) copy-start(f32[192]{0:T(256)} %param.7) | copy-start | bytes 2308
  7.2 7.7 %copy-start.2 = (bf16[192,2,16,128]{3,2,1,0:T(8,128)(2,1)S(1)}, bf16[192,2,16,128]{3,2,1,0:T(8,128)(2,1)}, u32[]{:S(2)}) copy-start(bf16[192,2,16,128]{3,2,1,0:T(8,128)(2,1)} %param.6) | copy-start | bytes 4718596
  7.2 105.3 %all-reduce.5.cloned.1.call-start = ((), (), s32[]{:S(2)}) async-start(), calls=%async_computation | async-start | bytes 524288 | tf_op jit(solution)/shard_map/psum | solution.py:184
  9.4 9.4 %collective-permute-start.1 = (bf16[64,1,16,128]{3,0,2,1:T(8,128)(2,1)S(1)}, bf16[64,1,16,128]{3,0,2,1:T(8,128)(2,1)S(1)}, u32[]{:S(2)}, u32[]{:S(2)}) collective-permute-start(bf16[64,1,16,128]{3,0,2,1:T(8,128)(2,1)S(1)} %slice.70), channel_id=1, source_target_pairs={{1,0},{2,1},{3,2},{4,3},{5,4},{6,5},{7,6},{8,7},{9,8},{10,9},{11,1... | collective-permute-start | bytes 786440 | tf_op jit(solution)/shard_map/ppermute | solution.py:21
  14.8 0.9 copy-start.3
  14.8 8.5 %collective-permute-start = (bf16[64,1,16,128]{3,0,2,1:T(8,128)(2,1)S(1)}, bf16[64,1,16,128]{3,0,2,1:T(8,128)(2,1)S(1)}, u32[]{:S(2)}, u32[]{:S(2)}) collective-permute-start(bf16[64,1,16,128]{3,0,2,1:T(8,128)(2,1)S(1)} %bitcast.26), channel_id=1, source_target_pairs={{0,1},{1,2},{2,3},{3,4},{4,5},{5,6},{6,7},{7,8},{8,9},{9,10},{10,1... | collective-permute-start | bytes 786440 | tf_op jit(solution)/shard_map/ppermute | solution.py:20
  15.6 7.8 %copy-start.1 = (bf16[64,2,16,128]{3,2,1,0:T(8,128)(2,1)S(1)}, bf16[64,2,16,128]{3,2,1,0:T(8,128)(2,1)}, u32[]{:S(2)}) copy-start(bf16[64,2,16,128]{3,2,1,0:T(8,128)(2,1)} %param.5) | copy-start | bytes 1572868
  112.5 0.9 copy-start
Sparse Core Ops, SparseCore 0:
  26.2 86.2 all-reduce.4

commit v2 on v1

--- a/solution.py
+++ b/solution.py
@@ -37,6 +37,16 @@
     return lax.dot_general(
         left_rows, right_rows, (((1,), (1,)), ((), ())), preferred_element_type=jnp.float32
     )
+
+
+def sum_over(matrix, axis):
+    peers = lax.axis_size(axis)
+    order = matrix.shape[0]
+    chunks = matrix.reshape(peers, order // peers, order)
+    arrived = lax.all_to_all(chunks, axis, 0, 0)
+    own = jnp.sum(arrived, axis=0, keepdims=True)
+    sums = lax.all_to_all(jnp.broadcast_to(own, chunks.shape), axis, 0, 0)
+    return sums.reshape(order, order)
 
 
 def factor_panel(tile, tiles, panel, t_ref, f_ref, x_ref, cols, rows, vpad):
@@ -181,7 +191,7 @@
     )
     cell_total = lax.axis_size("blk") * stacked.shape[1]
     local_gram = gram_term(stacked, stacked)
-    gram_sum = lax.psum(local_gram, "blk")
+    gram_sum = sum_over(local_gram, "blk")
     factor, inverse_high, inverse_low = factor_and_inverse(gram_sum, cell_total)
     result = jnp.dot(inverse_high, stacked, preferred_element_type=jnp.float32)
     result = result + jnp.dot(inverse_low, stacked, preferred_element_type=jnp.float32)

time: 138 us -> 69.3 us (0.50)
  waiting for transfers between devices: 87.7 us -> 5.4 us
  blocking collectives: 0 us -> 25.5 us
  between operations: 16.2 us -> 2.84 us
  matrix products: 2.93 us -> 5.16 us
    psum x1 -> x0, waiting for transfers between devices: 82.1 us -> none  [shards(): gram_sum = lax.psum(local_gram, 'blk')]
    all_to_all x0 -> x2, blocking collectives: none -> 25.5 us  [the longest x1 12.8 us: sum_over(): sums = lax.all_to_all(jnp.broadcast_to(own, chunks.shape), axis, 0, 0)]
    concatenate x1 -> x0, local copies, waits for them, and re-layouts: 2.86 us -> none  [shards(): jnp.concatenate([filtered, scaled], axis=0)]
    reshape x0 -> x1, local copies, waits for them, and re-layouts: none -> 2.29 us  [shards(): jnp.concatenate([filtered, scaled], axis=0)]
    dot_general x0 -> x1, local copies, waits for them, and re-layouts: none -> 2.27 us  [gram_term(): lax.dot_general(left_rows, right_rows, (((1,), (1,)), ((), ())), preferre...]
    dot_general x1, matrix products: 1.45 us -> 2.96 us  [gram_term(): lax.dot_general(left_rows, right_rows, (((1,), (1,)), ((), ())), preferre...]
    unnamed x11 -> x9, local copies, waits for them, and re-layouts: 2.77 us -> 1.83 us
  transfers between devices with their start and end apart: 3 -> 2, of which waited for: 3 -> 2; matrix products, arithmetic and copies ran while one was open for 4% -> 3% of each run, Pallas kernels for 0% -> 0%
where the time goes in v2:
time: 69.3 us; the launch traced here: 69.1 us
  blocking collectives  25.5 us (37%)
  Pallas kernels  13.7 us (20%)
  local copies, waits for them, and re-layouts  7.11 us (10%)
  starting transfers between devices  5.47 us (8%)
  waiting for transfers between devices  5.4 us (8%)
  matrix products  5.16 us (7%)
  other arithmetic  3.95 us (6%)
  between operations  2.84 us (4%)
    pallas_call x1, Pallas kernels, factor_and_inverse(): pl.pallas_call(lambda *refs: factor_kernel(1.0 / cell_total, *refs), out_...  13.7 us
    all_to_all x1, blocking collectives, sum_over(): sums = lax.all_to_all(jnp.broadcast_to(own, chunks.shape), axis, 0, 0)  12.8 us
    all_to_all x1, blocking collectives, sum_over(): arrived = lax.all_to_all(chunks, axis, 0, 0)  12.6 us
    ppermute x1, starting transfers between devices, with_halo(): after = lax.ppermute(leading, axis, down)  5.47 us
    ppermute x1, waiting for transfers between devices, with_halo(): before = lax.ppermute(last, axis, up)  4.56 us
    dot_general x1, matrix products, gram_term(): lax.dot_general(left_rows, right_rows, (((1,), (1,)), ((), ())), preferre...  2.96 us
    reshape x1, local copies, waits for them, and re-layouts, shards(): jnp.concatenate([filtered, scaled], axis=0)  2.29 us
    dot_general x1, local copies, waits for them, and re-layouts, gram_term(): lax.dot_general(left_rows, right_rows, (((1,), (1,)), ((), ())), preferre...  2.27 us
  transfers between devices with their start and end apart: 2, of which 2 were waited for; matrix products, arithmetic and copies ran while one was open for 3% of the time, Pallas kernels for 0%

profile of v2, /device:TPU:0, one launch (start us, length us, event | category | flops | bytes accessed | tf_op | source)
XLA Modules:
  0.0 69.1 jit_solution(11280919301440712497)
XLA Ops:
  0.6 0.0 copy-start.3
  0.6 0.0 copy-start.1
  1.4 1.3 %multiply_reduce_fusion = (bf16[64,16,128]{2,1,0:T(8,128)(2,1)S(1)}, f32[64,2,16,128]{3,2,1,0:T(8,128)S(1)}) fusion(f32[2]{0:T(128)S(1)} %get-tuple-element.14, f32[2]{0:T(128)S(1)} %get-tuple-element.15, bf16[64,2,16,128]{3,2,1,0:T(8,128)(2,1)} %param.5), kind=kLoop, calls=%fused_computation.27 | loop fusion | flops 917504 | bytes 1835024 | tf_op jit(solution)/shard_map/reduce_sum | solution.py:176
  2.8 0.1 slice.70
  2.8 5.5 %collective-permute-start.1 = (bf16[64,1,16,128]{3,2,1,0:T(8,128)(2,1)S(1)}, bf16[64,1,16,128]{3,2,1,0:T(8,128)(2,1)S(1)}, u32[]{:S(2)}, u32[]{:S(2)}) collective-permute-start(bf16[64,1,16,128]{3,2,1,0:T(8,128)(2,1)S(1)} %slice.70), channel_id=1, source_target_pairs={{1,0},{2,1},{3,2},{4,3},{5,4},{6,5},{7,6},{8,7},{9,8},{10,9},{11,1... | collective-permute-start | bytes 786440 | tf_op jit(solution)/shard_map/ppermute | solution.py:21
  8.3 0.0 copy-start.2
  8.3 0.0 collective-permute-start
  8.3 0.0 copy-done.3
  8.3 0.0 copy-done.1
  8.3 1.0 %multiply_convert_fusion = bf16[192,2,16,128]{3,2,1,0:T(8,128)(2,1)S(1)} fusion(bf16[192,2,16,128]{3,2,1,0:T(8,128)(2,1)S(1)} %copy-done.1, f32[2]{0:T(128)S(1)} %get-tuple-element.15, f32[192]{0:T(256)S(1)} %copy-done.3), kind=kLoop, calls=%fused_computation.2 | loop fusion | flops 3145728 | bytes 3146504 | tf_op jit(solution)/shard_map/convert_element_type | solution.py:186
  9.3 0.0 copy-start
  9.4 0.1 fusion.21
  9.4 0.0 copy-done.2
  9.4 0.6 fusion.22
  11.3 0.8 %collective-permute-done.1 = bf16[64,1,16,128]{3,2,1,0:T(8,128)(2,1)S(1)} collective-permute-done((bf16[64,1,16,128]{3,2,1,0:T(8,128)(2,1)S(1)}, bf16[64,1,16,128]{3,2,1,0:T(8,128)(2,1)S(1)}, u32[]{:S(2)}, u32[]{:S(2)}) %collective-permute-start.1) | collective-permute-done | bytes 262176 | tf_op jit(solution)/shard_map/ppermute | solution.py:21
  12.2 4.6 %collective-permute-done = bf16[64,1,16,128]{3,2,1,0:T(8,128)(2,1)S(1)} collective-permute-done((bf16[64,1,16,128]{3,2,1,0:T(8,128)(2,1)S(1)}, bf16[64,1,16,128]{3,2,1,0:T(8,128)(2,1)S(1)}, u32[]{:S(2)}, u32[]{:S(2)}) %collective-permute-start) | collective-permute-done | bytes 262176 | tf_op jit(solution)/shard_map/ppermute | solution.py:20
  16.8 0.0 copy-done
  16.8 0.4 fusion.20
  17.2 0.3 fusion.11
  17.5 0.6 fusion.17
  18.1 0.2 pad_maximum_fusion
  18.3 2.3 %reshape.31 = bf16[256,4096,1]{1,0,2:T(8,128)(2,1)} reshape(bf16[256,2,16,128]{3,2,1,0:T(8,128)(2,1)S(1)} %pad_maximum_fusion) | data formatting | bytes 4194304 | tf_op jit(solution)/shard_map/reshape | solution.py:189
  20.6 2.3 %dot_general.11 = bf16[16,16,4096]{2,1,0:T(8,128)(2,1)} reshape(bf16[256,2,16,128]{3,2,1,0:T(8,128)(2,1)S(1)} %pad_maximum_fusion) | data formatting | bytes 4194304 | tf_op jit(solution)/shard_map/dot_general | solution.py:37
  22.9 3.0 %fusion.23 = f32[16,16,256]{2,1,0:T(8,128)S(1)} fusion(bf16[16,16,4096]{2,1,0:T(8,128)(2,1)} %dot_general.11, bf16[256,4096,1]{1,0,2:T(8,128)(2,1)} %reshape.31), kind=kOutput, calls=%fused_computation.37 | convolution fusion | flops 536870912 | bytes 4456448 | tf_op jit(solution)/shard_map/dot_general | solution.py:37
  25.9 12.6 %all_to_all.10 = f32[16,16,256]{2,1,0:T(8,128)S(1)} all-to-all(f32[16,16,256]{2,1,0:T(8,128)S(1)} %fusion.23), channel_id=1, replica_groups=mesh['groups'=2,'blk'=16] {'blk'}, dimensions={0} | all-to-all | bytes 524288 | tf_op jit(solution)/shard_map/all_to_all | solution.py:46
  38.6 12.8 %all_to_all.11 = f32[16,16,256]{2,1,0:T(8,128)S(1)} all-to-all(f32[16,16,256]{2,1,0:T(8,128)S(1)} %broadcast_in_dim.2), channel_id=1, replica_groups=mesh['groups'=2,'blk'=16] {'blk'}, dimensions={0} | all-to-all | bytes 524288 | tf_op jit(solution)/shard_map/all_to_all | solution.py:48
  51.4 13.7 %factor.1 = (f32[256,256]{1,0:T(8,128)}, bf16[256,256]{1,0:T(8,128)(2,1)S(1)}, bf16[256,256]{1,0:T(8,128)(2,1)S(1)}) custom-call(f32[256,256]{1,0:T(8,128)S(1)} %bitcast.32), custom_call_target="tpu_custom_call" | custom-call | tf_op jit(solution)/shard_map/factor/pallas_call | solution.py:147
  65.1 1.0 %fusion.1 = f32[256,4096]{1,0:T(8,128)S(1)} fusion(bf16[256,256]{1,0:T(8,128)(2,1)S(1)} %get-tuple-element.5, bf16[32,8,32,128]{3,2,1,0:T(8,128)(2,1)S(1)} %bitcast.33), kind=kOutput, calls=%fused_computation.5 | convolution fusion | flops 536870912 | bytes 6422528 | tf_op jit(solution)/shard_map/dot_general | solution.py:196
  66.1 1.2 %fusion.6 = bf16[32,8,32,128]{3,1,2,0:T(8,128)(2,1)S(1)} fusion(f32[256,4096]{1,0:T(8,128)S(1)} %fusion.1, bf16[256,256]{1,0:T(8,128)(2,1)S(1)} %get-tuple-element.6, bf16[32,8,32,128]{3,2,1,0:T(8,128)(2,1)S(1)} %bitcast.34), kind=kOutput, calls=%fused_computation.13 | convolution fusion | flops 538968064 | bytes 8519680 | tf_op jit(solution)/shard_map/dot_general | solution.py:197
  67.3 1.8 %copy.8 = bf16[32,8,32,128]{3,2,1,0:T(8,128)(2,1)} copy(bf16[32,8,32,128]{3,1,2,0:T(8,128)(2,1)S(1)} %fusion.6) | data formatting | bytes 4194304
  (5 shorter events, 0.1 us)
Async XLA Ops:
  0.6 7.7 %copy-start.3 = (f32[192]{0:T(256)S(1)}, f32[192]{0:T(256)}, u32[]{:S(2)}) copy-start(f32[192]{0:T(256)} %param.7) | copy-start | bytes 2308
  0.6 7.7 %copy-start.1 = (bf16[192,2,16,128]{3,2,1,0:T(8,128)(2,1)S(1)}, bf16[192,2,16,128]{3,2,1,0:T(8,128)(2,1)}, u32[]{:S(2)}) copy-start(bf16[192,2,16,128]{3,2,1,0:T(8,128)(2,1)} %param.6) | copy-start | bytes 4718596
  2.8 9.4 %collective-permute-start.1 = (bf16[64,1,16,128]{3,2,1,0:T(8,128)(2,1)S(1)}, bf16[64,1,16,128]{3,2,1,0:T(8,128)(2,1)S(1)}, u32[]{:S(2)}, u32[]{:S(2)}) collective-permute-start(bf16[64,1,16,128]{3,2,1,0:T(8,128)(2,1)S(1)} %slice.70), channel_id=1, source_target_pairs={{1,0},{2,1},{3,2},{4,3},{5,4},{6,5},{7,6},{8,7},{9,8},{10,9},{11,1... | collective-permute-start | bytes 786440 | tf_op jit(solution)/shard_map/ppermute | solution.py:21
  8.3 1.2 %copy-start.2 = (s32[1,2]{1,0:T(1,128)S(1)}, s32[1,2]{1,0:T(1,128)}, u32[]{:S(2)}) copy-start(s32[1,2]{1,0:T(1,128)} %param.9) | copy-start | bytes 28
  8.3 8.5 %collective-permute-start = (bf16[64,1,16,128]{3,2,1,0:T(8,128)(2,1)S(1)}, bf16[64,1,16,128]{3,2,1,0:T(8,128)(2,1)S(1)}, u32[]{:S(2)}, u32[]{:S(2)}) collective-permute-start(bf16[64,1,16,128]{3,2,1,0:T(8,128)(2,1)S(1)} %bitcast.36), channel_id=1, source_target_pairs={{0,1},{1,2},{2,3},{3,4},{4,5},{5,6},{6,7},{7,8},{8,9},{9,10},{10,1... | collective-permute-start | bytes 786440 | tf_op jit(solution)/shard_map/ppermute | solution.py:20
  9.3 7.5 %copy-start = (bf16[64,2,16,128]{3,2,1,0:T(8,128)(2,1)S(1)}, bf16[64,2,16,128]{3,2,1,0:T(8,128)(2,1)}, u32[]{:S(2)}) copy-start(bf16[64,2,16,128]{3,2,1,0:T(8,128)(2,1)} %param.5) | copy-start | bytes 1572868

commit v3 on v1

v3 whole, which is shorter than its diff:
```python
import functools

import jax
import jax.numpy as jnp
from jax import lax
from jax.experimental import pallas as pl
from jax.experimental.pallas import tpu as pltpu
from jax.sharding import PartitionSpec as P

PANEL = 16
LANES = 128
SUBS = 8
SPREAD = 4
VMEM_BYTES = 40 * 1024 * 1024


def nt_dot(left_rows, right_rows):
    return lax.dot_general(
        left_rows, right_rows, (((1,), (1,)), ((), ())), preferred_element_type=jnp.float32
    )


def swap(x, axis, flip):
    peers = lax.axis_size(axis)
    return lax.ppermute(x, axis, [(i, i ^ flip) for i in range(peers)])


def relay(tall, s_ref, plane, rows_y):
    rows = s_ref.shape[0]
    for y in range(rows_y):
        column = (plane * rows_y + y) * LANES
        part = tall[pl.ds(y, rows, stride=rows_y), :]
        s_ref[:, column:column + LANES] = part.astype(jnp.bfloat16)


def scale_kernel(scales_ref, count_ref, old_ref, s_ref, gram_ref, tall):
    rows, planes, rows_y, _ = old_ref.shape
    for plane in range(planes):
        alive = jnp.where(plane < count_ref[0], 1.0, 0.0)

        @pl.loop(0, rows, unroll=8)
        def _(row):
            weight = scales_ref[row]
            at = pl.multiple_of(row * rows_y, rows_y)
            tall[pl.ds(at, rows_y), :] = old_ref[row, plane].astype(jnp.float32) * weight * alive

        relay(tall, s_ref, plane, rows_y)
    gram_ref[...] = nt_dot(s_ref[...], s_ref[...])


def scaled_rows(old_modes, mode_scales, plane_counts):
    rows, planes, rows_y, rows_z = old_modes.shape
    cells = planes * rows_y * rows_z
    smem = pl.BlockSpec(memory_space=pltpu.SMEM)
    vmem = pl.BlockSpec(memory_space=pltpu.VMEM)
    return pl.pallas_call(
        scale_kernel,
        out_shape=[
            jax.ShapeDtypeStruct((rows, cells), jnp.bfloat16),
            jax.ShapeDtypeStruct((rows, rows), jnp.float32),
        ],
        in_specs=[smem, smem, vmem],
        out_specs=[vmem, vmem],
        scratch_shapes=[pltpu.VMEM((rows * rows_y, rows_z), jnp.float32)],
        compiler_params=pltpu.CompilerParams(vmem_limit_bytes=VMEM_BYTES),
        cost_estimate=pl.CostEstimate(
            flops=2 * rows * rows * cells, bytes_accessed=8 * rows * cells, transcendentals=0
        ),
        name="scale_gram",
    )(mode_scales, plane_counts, old_modes)


def smooth(field, axis, place, length):
    lower = jnp.where(place == 0, 0.0, pltpu.roll(field, 1, axis=axis))
    upper = jnp.where(place == length - 1, 0.0, pltpu.roll(field, length - 1, axis=axis))
    return 0.25 * lower + 0.5 * field + 0.25 * upper


def packed_rows(order):
    chunk = -(-(order + SUBS) // (SPREAD * SUBS)) * SUBS
    return SPREAD * chunk


def filter_kernel(
    count_ref, links_ref, snap_ref, before_ref, after_ref, old_ref, oldgram_ref, s_ref, *rest
):
    chunk_refs, (tall, packed) = rest[:SPREAD], rest[SPREAD:]
    rows, planes, rows_y, rows_z = snap_ref.shape
    count = count_ref[0]
    join_low = links_ref[0, 0].astype(jnp.float32)
    join_high = links_ref[0, 1].astype(jnp.float32)
    place_y = lax.broadcasted_iota(jnp.int32, (rows_y, rows_z), 0)
    place_z = lax.broadcasted_iota(jnp.int32, (rows_y, rows_z), 1)
    for plane in range(planes):
        alive = jnp.where(plane < count, 1.0, 0.0)
        is_last = plane == count - 1

        @pl.loop(0, rows, unroll=8)
        def _(row):
            own = snap_ref[row, plane].astype(jnp.float32)
            if plane == 0:
                behind = before_ref[row, 0].astype(jnp.float32) * join_low
            else:
                behind = snap_ref[row, plane - 1].astype(jnp.float32)
            forward = after_ref[row, 0].astype(jnp.float32) * join_high
            if plane < planes - 1:
                forward = jnp.where(is_last, forward, snap_ref[row, plane + 1].astype(jnp.float32))
            field = 0.25 * behind + 0.5 * own + 0.25 * forward
            field = smooth(smooth(field, 0, place_y, rows_y), 1, place_z, rows_z) * alive
            at = pl.multiple_of(row * rows_y, rows_y)
            tall[pl.ds(at, rows_y), :] = field

        relay(tall, s_ref, plane, rows_y)
    fresh = s_ref[...]
    new_new = nt_dot(fresh, fresh)
    new_old = nt_dot(fresh, old_ref[...])
    split = LANES - rows
    old_old = oldgram_ref[...]
    top = jnp.concatenate([new_new, new_old[:, :split]], axis=1)
    hidden = jnp.zeros((split, rows), jnp.float32)
    middle = jnp.concatenate([hidden, old_old[:split, :split]], axis=1)
    upper_left = jnp.concatenate([top, middle], axis=0)
    upper_right = jnp.concatenate([new_old[:, split:], old_old[:split, split:]], axis=0)
    lower_right = old_old[split:, split:]
    i = lax.broadcasted_iota(jnp.int32, (LANES, LANES), 0)
    j = lax.broadcasted_iota(jnp.int32, (LANES, LANES), 1)
    packed[:LANES, :] = jnp.where(j >= i, upper_left, lower_right)
    packed[LANES:2 * LANES, :] = upper_right
    packed[2 * LANES:, :] = jnp.zeros((packed.shape[0] - 2 * LANES, LANES), jnp.float32)
    packed[2 * LANES:2 * LANES + 1, :] = jnp.sum(
        jnp.where(i == j, lower_right, 0.0), axis=0, keepdims=True
    )
    share = lax.axis_index("blk") % SPREAD
    height = packed.shape[0] // SPREAD
    for flip in range(SPREAD):
        at = pl.multiple_of((share ^ flip) * height, SUBS)
        chunk_refs[flip][...] = packed[pl.ds(at, height), :]


def filtered_rows(snapshots, before, after, plane_counts, links, s_old, old_gram):
    rows, planes, rows_y, rows_z = snapshots.shape
    cells = planes * rows_y * rows_z
    order = rows + s_old.shape[0]
    height = packed_rows(order)
    smem = pl.BlockSpec(memory_space=pltpu.SMEM)
    vmem = pl.BlockSpec(memory_space=pltpu.VMEM)
    chunk = jax.ShapeDtypeStruct((height // SPREAD, LANES), jnp.float32)
    return pl.pallas_call(
        filter_kernel,
        out_shape=[jax.ShapeDtypeStruct((rows, cells), jnp.bfloat16)] + [chunk] * SPREAD,
        in_specs=[smem, smem] + [vmem] * 5,
        out_specs=[vmem] * (1 + SPREAD),
        scratch_shapes=[
            pltpu.VMEM((rows * rows_y, rows_z), jnp.float32),
            pltpu.VMEM((height, LANES), jnp.float32),
        ],
        compiler_params=pltpu.CompilerParams(vmem_limit_bytes=VMEM_BYTES),
        cost_estimate=pl.CostEstimate(
            flops=2 * rows * order * cells, bytes_accessed=2 * order * cells, transcendentals=0
        ),
        name="filter_gram",
    )(plane_counts, links, snapshots, before, after, s_old, old_gram)


def sum_chunks(chunks, axis):
    peers = lax.axis_size(axis)
    arrived = [chunks[0]] + [swap(chunks[d], axis, d) for d in range(1, SPREAD)]
    total = (arrived[0] + arrived[1]) + (arrived[2] + arrived[3])
    step = SPREAD
    while step < peers:
        if step * 4 <= peers:
            one, two, three = (swap(total, axis, d * step) for d in (1, 2, 3))
            total = (total + one) + (two + three)
            step *= 4
        else:
            total = total + swap(total, axis, step)
            step *= 2
    return [total] + [swap(total, axis, d) for d in range(1, SPREAD)]


def factor_panel(tile, tiles, panel, t_ref, f_ref, x_ref, cols, rows, vpad):
    first = pl.multiple_of(panel * PANEL, PANEL)
    off = pl.multiple_of(first - tile * LANES, PANEL)
    here = pl.ds(first, PANEL)
    lane = lax.broadcasted_iota(jnp.int32, (PANEL, LANES), 1)
    sub = lax.broadcasted_iota(jnp.int32, (PANEL, LANES), 0)
    inside = (lane >= off) & (lane < off + PANEL)
    own = t_ref[here, tile * LANES:(tile + 1) * LANES]
    for s in range(tiles):
        if s == tile:
            block = jnp.where(inside, jnp.where(lane - off == sub, 1.0, 0.0), own)
        else:
            block = t_ref[here, s * LANES:(s + 1) * LANES]
        rows[pl.ds(s, PANEL, stride=SUBS), :] = block
    rows[pl.ds(tiles, PANEL, stride=SUBS), :] = own
    turned = pltpu.roll(own, lax.rem(LANES - off, LANES), axis=1)
    for j in range(PANEL):
        cols[j] = jnp.broadcast_to(turned[:, j:j + 1], (PANEL, LANES))
    entry = [
        [jnp.broadcast_to(cols[j, i:i + 1, :], (SUBS, LANES)) for j in range(i + 1)]
        for i in range(PANEL)
    ]
    y = [rows[i * SUBS:(i + 1) * SUBS, :] for i in range(PANEL)]
    unit = [[None] * PANEL for _ in range(PANEL)]
    recip = []
    for k in range(PANEL):
        recip.append(1.0 / entry[k][k])
        for i in range(k + 1, PANEL):
            unit[i][k] = entry[i][k] * recip[k]
        for j in range(k + 1, PANEL):
            for i in range(j, PANEL):
                entry[i][j] = entry[i][j] - unit[i][k] * entry[j][k]
        for i in range(k + 1, PANEL):
            y[i] = y[i] - unit[i][k] * y[k]
    v = [recip[i] * y[i] for i in range(PANEL)]
    for j in reversed(range(PANEL)):
        for i in range(j):
            v[i] = v[i] - unit[j][i] * v[j]
    for i in range(PANEL):
        rows[i * SUBS:(i + 1) * SUBS, :] = v[i]
    for s in range(tiles):
        vpad[pl.ds(off, PANEL), s * LANES:(s + 1) * LANES] = rows[pl.ds(s, PANEL, stride=SUBS), :]
    for i in range(PANEL):
        rows[i * SUBS:(i + 1) * SUBS, :] = jnp.sqrt(recip[i]) * y[i]
    zero = jnp.zeros((PANEL, LANES), jnp.float32)
    for s in range(tiles):
        span = slice(s * LANES, (s + 1) * LANES)
        part = rows[pl.ds(s, PANEL, stride=SUBS), :]
        if s == tile:
            whole = rows[pl.ds(tiles, PANEL, stride=SUBS), :]
            f_ref[here, span] = jnp.where(lane >= off + sub, whole, 0.0)
            x_ref[here, span] = jnp.where(lane <= off + sub, part, 0.0)
        else:
            f_ref[here, span] = part if s > tile else zero
            x_ref[here, span] = part if s < tile else zero
    low = tile * LANES
    order = t_ref.shape[0]
    update = jnp.dot(
        t_ref[low:, low:low + LANES],
        vpad[...],
        precision=lax.Precision.HIGHEST,
        preferred_element_type=jnp.float32,
    )
    row_id = lax.broadcasted_iota(jnp.int32, (order - low, LANES), 0) + low
    lane_id = lax.broadcasted_iota(jnp.int32, (order - low, LANES), 1)
    below = row_id >= first + PANEL
    mine = (lane_id >= off) & (lane_id < off + PANEL)
    for s in range(tiles):
        span = slice(s * LANES, (s + 1) * LANES)
        held = t_ref[low:, span]
        base = jnp.where(mine, 0.0, held) if s == tile else held
        t_ref[low:, span] = jnp.where(below, base - update[:, span], held)
    vpad[pl.ds(off, PANEL), :] = jnp.zeros((PANEL, order), jnp.float32)


def factor_kernel(scale, *refs):
    chunk_refs, refs = refs[:SPREAD], refs[SPREAD:]
    new_ref, old_ref, f_ref, out_ref, refs = *refs[:4], refs[4:]
    packed, t_ref, x_ref, cols, rows, vpad, stack, tall, staged, in_sem, out_sem = refs
    order = t_ref.shape[0]
    tiles = order // LANES
    new_count = new_ref.shape[0]
    load_new = pltpu.make_async_copy(new_ref, stack.at[pl.ds(0, new_count)], in_sem.at[0])
    load_old = pltpu.make_async_copy(
        old_ref, stack.at[pl.ds(new_count, order - new_count)], in_sem.at[1]
    )
    load_new.start()
    load_old.start()
    share = lax.axis_index("blk") % SPREAD
    height = packed.shape[0] // SPREAD
    for flip in range(SPREAD):
        at = pl.multiple_of((share ^ flip) * height, SUBS)
        packed[pl.ds(at, height), :] = chunk_refs[flip][...] * scale
    i = lax.broadcasted_iota(jnp.int32, (LANES, LANES), 0)
    j = lax.broadcasted_iota(jnp.int32, (LANES, LANES), 1)
    shared = packed[:LANES, :]
    right = packed[LANES:2 * LANES, :]
    upper = jnp.where(j >= i, shared, 0.0)
    lower = jnp.where(j < i, shared, 0.0)
    diagonal = packed[2 * LANES:2 * LANES + 1, :]
    t_ref[:LANES, :LANES] = jnp.where(j >= i, shared, upper.T)
    t_ref[:LANES, LANES:] = right
    t_ref[LANES:, :LANES] = right.T
    corner = jnp.where(j < i, shared, lower.T)
    t_ref[LANES:, LANES:] = jnp.where(i == j, diagonal, corner)
    vpad[...] = jnp.zeros(vpad.shape, jnp.float32)
    rows[...] = jnp.zeros(rows.shape, jnp.float32)
    per_tile = LANES // PANEL
    for tile in range(tiles):
        @pl.loop(tile * per_tile, (tile + 1) * per_tile)
        def _(panel):
            factor_panel(tile, tiles, panel, t_ref, f_ref, x_ref, cols, rows, vpad)
    inverse = x_ref[...]
    high = inverse.astype(jnp.bfloat16)
    low = (inverse - high.astype(jnp.float32)).astype(jnp.bfloat16)
    load_new.wait()
    load_old.wait()
    _, planes, rows_y, rows_z = out_ref.shape
    stores = []
    for plane in range(planes):
        for pair in range(0, rows_y, 2):
            column = (plane * rows_y + pair) * LANES
            block = stack[:, column:column + 2 * LANES]
            sums = jnp.dot(high, block, preferred_element_type=jnp.float32)
            sums = sums + jnp.dot(low, block, preferred_element_type=jnp.float32)
            for y in (0, 1):
                tall[pl.ds(pair + y, order, stride=rows_y), :] = sums[:, y * LANES:(y + 1) * LANES]

        @pl.loop(0, order, unroll=8)
        def _(row):
            at = pl.multiple_of(row * rows_y, rows_y)
            staged[plane, row] = tall[pl.ds(at, rows_y), :].astype(jnp.bfloat16)

        store = pltpu.make_async_copy(staged.at[plane], out_ref.at[:, plane], out_sem.at[plane])
        store.start()
        stores.append(store)
    for store in stores:
        store.wait()


def factor_and_modes(chunks, s_new, s_old, shape, cell_total):
    order, planes, rows_y, rows_z = shape
    height = chunks[0].shape[0] * SPREAD
    vmem = pl.BlockSpec(memory_space=pltpu.VMEM)
    hbm = pl.BlockSpec(memory_space=pl.ANY)
    square = (order, order)
    return pl.pallas_call(
        functools.partial(factor_kernel, 1.0 / cell_total),
        out_shape=[
            jax.ShapeDtypeStruct(square, jnp.float32),
            jax.ShapeDtypeStruct(shape, jnp.bfloat16),
        ],
        in_specs=[vmem] * SPREAD + [hbm, hbm],
        out_specs=[vmem, hbm],
        scratch_shapes=[
            pltpu.VMEM((height, LANES), jnp.float32),
            pltpu.VMEM(square, jnp.float32),
            pltpu.VMEM(square, jnp.float32),
            pltpu.VMEM((PANEL, PANEL, LANES), jnp.float32),
            pltpu.VMEM((PANEL * SUBS, LANES), jnp.float32),
            pltpu.VMEM((LANES, order), jnp.float32),
            pltpu.VMEM((order, planes * rows_y * rows_z), jnp.bfloat16),
            pltpu.VMEM((order * rows_y, rows_z), jnp.float32),
            pltpu.VMEM((planes, order, rows_y, rows_z), jnp.bfloat16),
            pltpu.SemaphoreType.DMA((2,)),
            pltpu.SemaphoreType.DMA((planes,)),
        ],
        compiler_params=pltpu.CompilerParams(vmem_limit_bytes=VMEM_BYTES),
        name="factor",
    )(*chunks, s_new, s_old)


def shards(snapshots, old_modes, mode_scales, plane_counts, links):
    new_count, planes, rows_y, rows_z = snapshots.shape
    order = new_count + old_modes.shape[0]
    peers = lax.axis_size("blk")
    up = [(i, (i + 1) % peers) for i in range(peers)]
    down = [(j, i) for i, j in up]
    first = lax.slice_in_dim(snapshots, 0, 1, axis=1)
    last = lax.dynamic_slice_in_dim(snapshots, plane_counts[0] - 1, 1, axis=1)
    after = lax.ppermute(first, "blk", down)
    before = lax.ppermute(last, "blk", up)
    s_old, old_gram = scaled_rows(old_modes, mode_scales, plane_counts)
    s_new, *chunks = filtered_rows(
        snapshots, before, after, plane_counts, links, s_old, old_gram
    )
    sums = sum_chunks(chunks, "blk")
    factor, modes = factor_and_modes(
        sums, s_new, s_old, (order, planes, rows_y, rows_z), peers * planes * rows_y * rows_z
    )
    return (modes, factor)


def solution(mesh):
    return jax.shard_map(
        shards,
        mesh=mesh,
        in_specs=(
            P(None, ("groups", "blk"), None, None),
            P(None, ("groups", "blk"), None, None),
            P("groups"),
            P(("groups", "blk")),
            P(("groups", "blk"), None),
        ),
        out_specs=(P(None, ("groups", "blk"), None, None), P("groups", None)),
        check_vma=False,
    )
```

time: 138 us -> 54.2 us (0.39)
  waiting for transfers between devices: 87.7 us -> 11.3 us
  between operations: 16.2 us -> 1.42 us
  Pallas kernels: 13.7 us -> 24.3 us
  starting transfers between devices: 5.51 us -> 13.8 us
  other arithmetic: 4.86 us -> 0.02 us
  local copies, waits for them, and re-layouts: 6.36 us -> 3.17 us
  matrix products: 2.93 us -> 0 us
    psum x1 -> x0, waiting for transfers between devices: 82.1 us -> none  [shards(): gram_sum = lax.psum(local_gram, 'blk')]
    pallas_call x1 -> x3, Pallas kernels: 13.7 us -> 24.3 us  [the longest x1 17.8 us: factor_and_modes(): pl.pallas_call(functools.partial(factor_kernel, 1.0 / cell_total), out_sh...]
    ppermute x2 -> x11, starting transfers between devices: 5.47 us -> 13.8 us  [the longest x9 8.3 us: swap(): return lax.ppermute(x, axis, [(i, i ^ flip) for i in range(peers)])]
    ppermute x2 -> x11, waiting for transfers between devices: 5.65 us -> 11.3 us  [the longest x9 7.65 us: swap(): return lax.ppermute(x, axis, [(i, i ^ flip) for i in range(peers)])]
    dot_general x3 -> x0, matrix products: 2.93 us -> none  [the longest x1 1.45 us: gram_term(): lax.dot_general(left_rows, right_rows, (((1,), (1,)), ((), ())), preferre...]
    concatenate x1 -> x0, local copies, waits for them, and re-layouts: 2.86 us -> none  [shards(): jnp.concatenate([filtered, scaled], axis=0)]
    concatenate x1 -> x0, other arithmetic: 1.5 us -> none  [shards(): jnp.concatenate([filtered, scaled], axis=0)]
    convert_element_type x3 -> x0, other arithmetic: 1.38 us -> none  [the longest x1 0.76 us: shards(): (mode_scales[:, None, None, None] * old_modes.astype(jnp.float32) * alive...]
  transfers between devices with their start and end apart: 3 -> 11, of which waited for: 3 -> 6; matrix products, arithmetic and copies ran while one was open for 4% -> 0% of each run, Pallas kernels for 0% -> 5%
where the time goes in v3:
time: 54.2 us; the launch traced here: 54 us
  Pallas kernels  24.3 us (45%)
  starting transfers between devices  13.8 us (25%)
  waiting for transfers between devices  11.3 us (21%)
  local copies, waits for them, and re-layouts  3.17 us (6%)
  between operations  1.42 us (3%)
    pallas_call x1, Pallas kernels, factor_and_modes(): pl.pallas_call(functools.partial(factor_kernel, 1.0 / cell_total), out_sh...  17.8 us
    ppermute x9, starting transfers between devices, swap(): return lax.ppermute(x, axis, [(i, i ^ flip) for i in range(peers)])  8.3 us
    ppermute x9, waiting for transfers between devices, swap(): return lax.ppermute(x, axis, [(i, i ^ flip) for i in range(peers)])  7.65 us
    ppermute x1, starting transfers between devices, shards(): after = lax.ppermute(first, 'blk', down)  5.47 us
    pallas_call x1, Pallas kernels, filtered_rows(): pl.pallas_call(filter_kernel, out_shape=[jax.ShapeDtypeStruct((rows, cell...  3.8 us
    ppermute x1, waiting for transfers between devices, shards(): before = lax.ppermute(last, 'blk', up)  3.65 us
    pallas_call x1, Pallas kernels, scaled_rows(): pl.pallas_call(scale_kernel, out_shape=[jax.ShapeDtypeStruct((rows, cells...  2.73 us
    unnamed x8, local copies, waits for them, and re-layouts  2.09 us
  transfers between devices with their start and end apart: 11, of which 6 were waited for; matrix products, arithmetic and copies ran while one was open for 0% of the time, Pallas kernels for 5%

profile of v3, /device:TPU:0, one launch (start us, length us, event | category | flops | bytes accessed | tf_op | source)
XLA Modules:
  0.0 54.0 jit_solution(28682611595782702)
XLA Ops:
  0.6 0.0 copy-start
  0.6 0.0 copy-start.3
  1.4 1.1 %fusion = (bf16[64,1,16,128]{3,2,1,0:T(8,128)(2,1)S(1)}, bf16[64,1,16,128]{3,2,1,0:T(8,128)(2,1)S(1)}) fusion(bf16[64,2,16,128]{3,2,1,0:T(8,128)(2,1)} %snap_ref.1, s32[]{:T(128)S(6)} %select_n.3), kind=kLoop, calls=%fused_computation.3 | loop fusion | bytes 1048580 | tf_op jit(solution)/shard_map/slice | solution.py:359
  2.4 5.5 %collective-permute-start.1 = (bf16[64,1,16,128]{3,2,1,0:T(8,128)(2,1)S(1)}, bf16[64,1,16,128]{3,2,1,0:T(8,128)(2,1)S(1)}, u32[]{:S(2)}, u32[]{:S(2)}) collective-permute-start(bf16[64,1,16,128]{3,2,1,0:T(8,128)(2,1)S(1)} %get-tuple-element.20), channel_id=1, source_target_pairs={{1,0},{2,1},{3,2},{4,3},{5,4},{6,5},{7,6},{8,7},{9,8},{10,9},{11,1... | collective-permute-start | bytes 786440 | tf_op jit(solution)/shard_map/ppermute | solution.py:361
  7.9 0.0 collective-permute-start
  7.9 0.0 copy-start.1
  7.9 1.4 %copy-done.1 = bf16[192,2,16,128]{3,2,1,0:T(8,128)(2,1)S(1)} copy-done((bf16[192,2,16,128]{3,2,1,0:T(8,128)(2,1)S(1)}, bf16[192,2,16,128]{3,2,1,0:T(8,128)(2,1)}, u32[]{:S(2)}) %copy-start.1) | copy-done | bytes 1572888
  9.3 0.0 copy-start.2
  9.3 0.7 %copy-done.2 = f32[192]{0:T(256)S(1)} copy-done((f32[192]{0:T(256)S(1)}, f32[192]{0:T(256)}, u32[]{:S(2)}) %copy-start.2) | copy-done | bytes 792
  10.0 2.7 %scale_gram.1 = (bf16[192,4096]{1,0:T(8,128)(2,1)S(1)}, f32[192,192]{1,0:T(8,128)S(1)}) custom-call(f32[192]{0:T(256)S(1)} %copy-done.2, s32[1]{0:T(128)S(6)} %copy.7.count_ref, bf16[192,2,16,128]{3,2,1,0:T(8,128)(2,1)S(1)} %copy-done.1), custom_call_target="tpu_custom_call" | custom-call | flops 301989888 | bytes 6291456 | tf_op jit(solution)/shard_map/scale_gram/pallas_call | solution.py:56
  12.7 0.0 collective-permute-done.1.after_ref
  12.7 3.7 %collective-permute-done.before_ref = bf16[64,1,16,128]{3,2,1,0:T(8,128)(2,1)S(1)} collective-permute-done((bf16[64,1,16,128]{3,2,1,0:T(8,128)(2,1)S(1)}, bf16[64,1,16,128]{3,2,1,0:T(8,128)(2,1)S(1)}, u32[]{:S(2)}, u32[]{:S(2)}) %collective-permute-start) | collective-permute-done | bytes 262176 | tf_op jit(solution)/shard_map/ppermute | solution.py:362
  16.4 0.0 copy-done
  16.4 0.0 copy-done.3
  16.4 3.8 %filter_gram.1 = (bf16[64,4096]{1,0:T(8,128)(2,1)S(1)}, f32[72,128]{1,0:T(8,128)S(1)}, f32[72,128]{1,0:T(8,128)S(1)}, f32[72,128]{1,0:T(8,128)S(1)}, f32[72,128]{1,0:T(8,128)S(1)}) custom-call(s32[1]{0:T(128)S(6)} %copy.7.count_ref, s32[1,2]{1,0:T(1,128)S(1)} %copy-done.3, bf16[64,2,16,128]{3,2,1,0:T(8,128)(2,1)S(1)} %copy-done, ...), custom_call_target="tpu_custom_call" | custom-call | flops 134217728 | bytes 2097152 | tf_op jit(solution)/shard_map/filter_gram/pallas_call | solution.py:148
  20.2 0.1 collective-permute-start.2
  20.3 0.1 collective-permute-start.3
  20.4 1.8 %collective-permute-start.4 = (f32[72,128]{1,0:T(8,128)S(1)}, f32[72,128]{1,0:T(8,128)S(1)}, u32[]{:S(2)}, u32[]{:S(2)}) collective-permute-start(f32[72,128]{1,0:T(8,128)S(1)} %get-tuple-element.16), channel_id=1, source_target_pairs={{0,3},{1,2},{2,1},{3,0},{4,7},{5,6},{6,5},{7,4},{8,11},{9,10},{10,... | collective-permute-start | bytes 110600 | tf_op jit(solution)/shard_map/ppermute | solution.py:25
  22.1 0.0 collective-permute-done.2
  22.1 2.4 %collective-permute-done.3 = f32[72,128]{1,0:T(8,128)S(1)} collective-permute-done((f32[72,128]{1,0:T(8,128)S(1)}, f32[72,128]{1,0:T(8,128)S(1)}, u32[]{:S(2)}, u32[]{:S(2)}) %collective-permute-start.3) | collective-permute-done | bytes 36896 | tf_op jit(solution)/shard_map/ppermute | solution.py:25
  24.6 0.0 collective-permute-done.4
  24.6 1.3 %collective-permute-start.7 = (f32[72,128]{1,0:T(8,128)S(1)}, f32[72,128]{1,0:T(8,128)S(1)}, u32[]{:S(2)}, u32[]{:S(2)}) collective-permute-start(f32[72,128]{1,0:T(8,128)S(1)} %add_add_fusion.1), channel_id=1, source_target_pairs={{0,12},{1,13},{2,14},{3,15},{4,8},{5,9},{6,10},{7,11},{8,4},{9,5},... | collective-permute-start | bytes 110600 | tf_op jit(solution)/shard_map/ppermute | solution.py:25
  25.9 0.0 collective-permute-start.6
  25.9 3.2 %collective-permute-start.5 = (f32[72,128]{1,0:T(8,128)S(1)}, f32[72,128]{1,0:T(8,128)S(1)}, u32[]{:S(2)}, u32[]{:S(2)}) collective-permute-start(f32[72,128]{1,0:T(8,128)S(1)} %add_add_fusion.1), channel_id=1, source_target_pairs={{0,4},{1,5},{2,6},{3,7},{4,0},{5,1},{6,2},{7,3},{8,12},{9,13},{10,... | collective-permute-start | bytes 110600 | tf_op jit(solution)/shard_map/ppermute | solution.py:25
  29.0 1.6 %collective-permute-done.7 = f32[72,128]{1,0:T(8,128)S(1)} collective-permute-done((f32[72,128]{1,0:T(8,128)S(1)}, f32[72,128]{1,0:T(8,128)S(1)}, u32[]{:S(2)}, u32[]{:S(2)}) %collective-permute-start.7) | collective-permute-done | bytes 36896 | tf_op jit(solution)/shard_map/ppermute | solution.py:25
  30.6 0.9 %collective-permute-done.6 = f32[72,128]{1,0:T(8,128)S(1)} collective-permute-done((f32[72,128]{1,0:T(8,128)S(1)}, f32[72,128]{1,0:T(8,128)S(1)}, u32[]{:S(2)}, u32[]{:S(2)}) %collective-permute-start.6) | collective-permute-done | bytes 36896 | tf_op jit(solution)/shard_map/ppermute | solution.py:25
  31.6 0.0 collective-permute-done.5
  31.6 0.1 collective-permute-start.10
  31.7 1.6 %collective-permute-start.9 = (f32[72,128]{1,0:T(8,128)S(1)}, f32[72,128]{1,0:T(8,128)S(1)}, u32[]{:S(2)}, u32[]{:S(2)}) collective-permute-start(f32[72,128]{1,0:T(8,128)S(1)} %add_add_fusion.refs_0_), channel_id=1, source_target_pairs={{0,2},{1,3},{2,0},{3,1},{4,6},{5,7},{6,4},{7,5},{8,10},{9,11},{10,... | collective-permute-start | bytes 110600 | tf_op jit(solution)/shard_map/ppermute | solution.py:25
  33.2 0.3 collective-permute-start.8
  33.5 1.8 %collective-permute-done.10.refs_3_ = f32[72,128]{1,0:T(8,128)S(1)} collective-permute-done((f32[72,128]{1,0:T(8,128)S(1)}, f32[72,128]{1,0:T(8,128)S(1)}, u32[]{:S(2)}, u32[]{:S(2)}) %collective-permute-start.10) | collective-permute-done | bytes 36896 | tf_op jit(solution)/shard_map/ppermute | solution.py:25
  35.3 0.9 %collective-permute-done.9.refs_2_ = f32[72,128]{1,0:T(8,128)S(1)} collective-permute-done((f32[72,128]{1,0:T(8,128)S(1)}, f32[72,128]{1,0:T(8,128)S(1)}, u32[]{:S(2)}, u32[]{:S(2)}) %collective-permute-start.9) | collective-permute-done | bytes 36896 | tf_op jit(solution)/shard_map/ppermute | solution.py:25
  36.2 0.0 collective-permute-done.8.refs_1_
  36.2 17.8 %factor.1 = (f32[256,256]{1,0:T(8,128)}, bf16[256,2,16,128]{3,2,1,0:T(8,128)(2,1)}) custom-call(f32[72,128]{1,0:T(8,128)S(1)} %add_add_fusion.refs_0_, f32[72,128]{1,0:T(8,128)S(1)} %collective-permute-done.8.refs_1_, f32[72,128]{1,0:T(8,128)S(1)} %collective-permute-done.9.refs_2_, f32[72,128]{1,0:T(8,128)S(1)} %collective-permute-done.10.refs_3_, ...), custom_call_target="tpu_custom_call" | custom-call | tf_op jit(solution)/shard_map/factor/pallas_call | solution.py:327
  (2 shorter events, 0.0 us)
Async XLA Ops:
  0.6 15.8 %copy-start = (bf16[64,2,16,128]{3,2,1,0:T(8,128)(2,1)S(1)}, bf16[64,2,16,128]{3,2,1,0:T(8,128)(2,1)}, u32[]{:S(2)}) copy-start(bf16[64,2,16,128]{3,2,1,0:T(8,128)(2,1)} %snap_ref.1) | copy-start | bytes 1572868
  0.6 15.8 %copy-start.3 = (s32[1,2]{1,0:T(1,128)S(1)}, s32[1,2]{1,0:T(1,128)}, u32[]{:S(2)}) copy-start(s32[1,2]{1,0:T(1,128)} %links_ref.1) | copy-start | bytes 28
  2.4 10.3 %collective-permute-start.1 = (bf16[64,1,16,128]{3,2,1,0:T(8,128)(2,1)S(1)}, bf16[64,1,16,128]{3,2,1,0:T(8,128)(2,1)S(1)}, u32[]{:S(2)}, u32[]{:S(2)}) collective-permute-start(bf16[64,1,16,128]{3,2,1,0:T(8,128)(2,1)S(1)} %get-tuple-element.20), channel_id=1, source_target_pairs={{1,0},{2,1},{3,2},{4,3},{5,4},{6,5},{7,6},{8,7},{9,8},{10,9},{11,1... | collective-permute-start | bytes 786440 | tf_op jit(solution)/shard_map/ppermute | solution.py:361
  7.9 8.5 %collective-permute-start = (bf16[64,1,16,128]{3,2,1,0:T(8,128)(2,1)S(1)}, bf16[64,1,16,128]{3,2,1,0:T(8,128)(2,1)S(1)}, u32[]{:S(2)}, u32[]{:S(2)}) collective-permute-start(bf16[64,1,16,128]{3,2,1,0:T(8,128)(2,1)S(1)} %get-tuple-element.21), channel_id=1, source_target_pairs={{0,1},{1,2},{2,3},{3,4},{4,5},{5,6},{6,7},{7,8},{8,9},{9,10},{10,1... | collective-permute-start | bytes 786440 | tf_op jit(solution)/shard_map/ppermute | solution.py:362
  7.9 1.4 %copy-start.1 = (bf16[192,2,16,128]{3,2,1,0:T(8,128)(2,1)S(1)}, bf16[192,2,16,128]{3,2,1,0:T(8,128)(2,1)}, u32[]{:S(2)}) copy-start(bf16[192,2,16,128]{3,2,1,0:T(8,128)(2,1)} %old_ref.1) | copy-start | bytes 4718596
  9.3 0.7 %copy-start.2 = (f32[192]{0:T(256)S(1)}, f32[192]{0:T(256)}, u32[]{:S(2)}) copy-start(f32[192]{0:T(256)} %scales_ref.1) | copy-start | bytes 2308
  20.2 1.9 %collective-permute-start.2 = (f32[72,128]{1,0:T(8,128)S(1)}, f32[72,128]{1,0:T(8,128)S(1)}, u32[]{:S(2)}, u32[]{:S(2)}) collective-permute-start(f32[72,128]{1,0:T(8,128)S(1)} %get-tuple-element.14), channel_id=1, source_target_pairs={{0,1},{1,0},{2,3},{3,2},{4,5},{5,4},{6,7},{7,6},{8,9},{9,8},{10,11... | collective-permute-start | bytes 110600 | tf_op jit(solution)/shard_map/ppermute | solution.py:25
  20.3 4.3 %collective-permute-start.3 = (f32[72,128]{1,0:T(8,128)S(1)}, f32[72,128]{1,0:T(8,128)S(1)}, u32[]{:S(2)}, u32[]{:S(2)}) collective-permute-start(f32[72,128]{1,0:T(8,128)S(1)} %get-tuple-element.15), channel_id=1, source_target_pairs={{0,2},{1,3},{2,0},{3,1},{4,6},{5,7},{6,4},{7,5},{8,10},{9,11},{10,... | collective-permute-start | bytes 110600 | tf_op jit(solution)/shard_map/ppermute | solution.py:25
  20.4 4.2 %collective-permute-start.4 = (f32[72,128]{1,0:T(8,128)S(1)}, f32[72,128]{1,0:T(8,128)S(1)}, u32[]{:S(2)}, u32[]{:S(2)}) collective-permute-start(f32[72,128]{1,0:T(8,128)S(1)} %get-tuple-element.16), channel_id=1, source_target_pairs={{0,3},{1,2},{2,1},{3,0},{4,7},{5,6},{6,5},{7,4},{8,11},{9,10},{10,... | collective-permute-start | bytes 110600 | tf_op jit(solution)/shard_map/ppermute | solution.py:25
  24.6 6.0 %collective-permute-start.7 = (f32[72,128]{1,0:T(8,128)S(1)}, f32[72,128]{1,0:T(8,128)S(1)}, u32[]{:S(2)}, u32[]{:S(2)}) collective-permute-start(f32[72,128]{1,0:T(8,128)S(1)} %add_add_fusion.1), channel_id=1, source_target_pairs={{0,12},{1,13},{2,14},{3,15},{4,8},{5,9},{6,10},{7,11},{8,4},{9,5},... | collective-permute-start | bytes 110600 | tf_op jit(solution)/shard_map/ppermute | solution.py:25
  25.9 5.7 %collective-permute-start.6 = (f32[72,128]{1,0:T(8,128)S(1)}, f32[72,128]{1,0:T(8,128)S(1)}, u32[]{:S(2)}, u32[]{:S(2)}) collective-permute-start(f32[72,128]{1,0:T(8,128)S(1)} %add_add_fusion.1), channel_id=1, source_target_pairs={{0,8},{1,9},{2,10},{3,11},{4,12},{5,13},{6,14},{7,15},{8,0},{9,1},... | collective-permute-start | bytes 110600 | tf_op jit(solution)/shard_map/ppermute | solution.py:25
  25.9 5.7 %collective-permute-start.5 = (f32[72,128]{1,0:T(8,128)S(1)}, f32[72,128]{1,0:T(8,128)S(1)}, u32[]{:S(2)}, u32[]{:S(2)}) collective-permute-start(f32[72,128]{1,0:T(8,128)S(1)} %add_add_fusion.1), channel_id=1, source_target_pairs={{0,4},{1,5},{2,6},{3,7},{4,0},{5,1},{6,2},{7,3},{8,12},{9,13},{10,... | collective-permute-start | bytes 110600 | tf_op jit(solution)/shard_map/ppermute | solution.py:25
  31.6 3.7 %collective-permute-start.10 = (f32[72,128]{1,0:T(8,128)S(1)}, f32[72,128]{1,0:T(8,128)S(1)}, u32[]{:S(2)}, u32[]{:S(2)}) collective-permute-start(f32[72,128]{1,0:T(8,128)S(1)} %add_add_fusion.refs_0_), channel_id=1, source_target_pairs={{0,3},{1,2},{2,1},{3,0},{4,7},{5,6},{6,5},{7,4},{8,11},{9,10},{10,... | collective-permute-start | bytes 110600 | tf_op jit(solution)/shard_map/ppermute | solution.py:25
  31.7 4.6 %collective-permute-start.9 = (f32[72,128]{1,0:T(8,128)S(1)}, f32[72,128]{1,0:T(8,128)S(1)}, u32[]{:S(2)}, u32[]{:S(2)}) collective-permute-start(f32[72,128]{1,0:T(8,128)S(1)} %add_add_fusion.refs_0_), channel_id=1, source_target_pairs={{0,2},{1,3},{2,0},{3,1},{4,6},{5,7},{6,4},{7,5},{8,10},{9,11},{10,... | collective-permute-start | bytes 110600 | tf_op jit(solution)/shard_map/ppermute | solution.py:25
  33.2 3.0 %collective-permute-start.8 = (f32[72,128]{1,0:T(8,128)S(1)}, f32[72,128]{1,0:T(8,128)S(1)}, u32[]{:S(2)}, u32[]{:S(2)}) collective-permute-start(f32[72,128]{1,0:T(8,128)S(1)} %add_add_fusion.refs_0_), channel_id=1, source_target_pairs={{0,1},{1,0},{2,3},{3,2},{4,5},{5,4},{6,7},{7,6},{8,9},{9,8},{10,11... | collective-permute-start | bytes 110600 | tf_op jit(solution)/shard_map/ppermute | solution.py:25

commit v4 on v3

--- a/solution.py
+++ b/solution.py
@@ -18,11 +18,6 @@
     return lax.dot_general(
         left_rows, right_rows, (((1,), (1,)), ((), ())), preferred_element_type=jnp.float32
     )
-
-
-def swap(x, axis, flip):
-    peers = lax.axis_size(axis)
-    return lax.ppermute(x, axis, [(i, i ^ flip) for i in range(peers)])
 
 
 def relay(tall, s_ref, plane, rows_y):
@@ -84,7 +79,7 @@
 def filter_kernel(
     count_ref, links_ref, snap_ref, before_ref, after_ref, old_ref, oldgram_ref, s_ref, *rest
 ):
-    chunk_refs, (tall, packed) = rest[:SPREAD], rest[SPREAD:]
+    packed, tall = rest
     rows, planes, rows_y, rows_z = snap_ref.shape
     count = count_ref[0]
     join_low = links_ref[0, 0].astype(jnp.float32)
@@ -130,11 +125,6 @@
     packed[2 * LANES:2 * LANES + 1, :] = jnp.sum(
         jnp.where(i == j, lower_right, 0.0), axis=0, keepdims=True
     )
-    share = lax.axis_index("blk") % SPREAD
-    height = packed.shape[0] // SPREAD
-    for flip in range(SPREAD):
-        at = pl.multiple_of((share ^ flip) * height, SUBS)
-        chunk_refs[flip][...] = packed[pl.ds(at, height), :]
 
 
 def filtered_rows(snapshots, before, after, plane_counts, links, s_old, old_gram):
@@ -144,16 +134,15 @@
     height = packed_rows(order)
     smem = pl.BlockSpec(memory_space=pltpu.SMEM)
     vmem = pl.BlockSpec(memory_space=pltpu.VMEM)
-    chunk = jax.ShapeDtypeStruct((height // SPREAD, LANES), jnp.float32)
     return pl.pallas_call(
         filter_kernel,
-        out_shape=[jax.ShapeDtypeStruct((rows, cells), jnp.bfloat16)] + [chunk] * SPREAD,
+        out_shape=[
+            jax.ShapeDtypeStruct((rows, cells), jnp.bfloat16),
+            jax.ShapeDtypeStruct((height, LANES), jnp.float32),
+        ],
         in_specs=[smem, smem] + [vmem] * 5,
-        out_specs=[vmem] * (1 + SPREAD),
-        scratch_shapes=[
-            pltpu.VMEM((rows * rows_y, rows_z), jnp.float32),
-            pltpu.VMEM((height, LANES), jnp.float32),
-        ],
+        out_specs=[vmem, vmem],
+        scratch_shapes=[pltpu.VMEM((rows * rows_y, rows_z), jnp.float32)],
         compiler_params=pltpu.CompilerParams(vmem_limit_bytes=VMEM_BYTES),
         cost_estimate=pl.CostEstimate(
             flops=2 * rows * order * cells, bytes_accessed=2 * order * cells, transcendentals=0
@@ -162,20 +151,26 @@
     )(plane_counts, links, snapshots, before, after, s_old, old_gram)
 
 
-def sum_chunks(chunks, axis):
+def sum_over(packed, axis):
     peers = lax.axis_size(axis)
-    arrived = [chunks[0]] + [swap(chunks[d], axis, d) for d in range(1, SPREAD)]
-    total = (arrived[0] + arrived[1]) + (arrived[2] + arrived[3])
+    near = [list(range(i, i + SPREAD)) for i in range(0, peers, SPREAD)]
+    shares = packed.reshape(SPREAD, packed.shape[0] // SPREAD, LANES)
+    arrived = lax.all_to_all(shares, axis, 0, 0, axis_index_groups=near)
+    total = jnp.sum(arrived, axis=0)
     step = SPREAD
     while step < peers:
-        if step * 4 <= peers:
-            one, two, three = (swap(total, axis, d * step) for d in (1, 2, 3))
-            total = (total + one) + (two + three)
-            step *= 4
-        else:
-            total = total + swap(total, axis, step)
-            step *= 2
-    return [total] + [swap(total, axis, d) for d in range(1, SPREAD)]
+        width = min(SPREAD, peers // step)
+        far = [
+            [base + low + k * step for k in range(width)]
+            for base in range(0, peers, step * width)
+            for low in range(step)
+        ]
+        spread = jnp.broadcast_to(total[None], (width,) + total.shape)
+        total = jnp.sum(lax.all_to_all(spread, axis, 0, 0, axis_index_groups=far), axis=0)
+        step *= width
+    spread = jnp.broadcast_to(total[None], (SPREAD,) + total.shape)
+    sums = lax.all_to_all(spread, axis, 0, 0, axis_index_groups=near)
+    return sums.reshape(packed.shape)
 
 
 def factor_panel(tile, tiles, panel, t_ref, f_ref, x_ref, cols, rows, vpad):
@@ -254,9 +249,8 @@
 
 
 def factor_kernel(scale, *refs):
-    chunk_refs, refs = refs[:SPREAD], refs[SPREAD:]
-    new_ref, old_ref, f_ref, out_ref, refs = *refs[:4], refs[4:]
-    packed, t_ref, x_ref, cols, rows, vpad, stack, tall, staged, in_sem, out_sem = refs
+    packed, new_ref, old_ref, f_ref, out_ref, *refs = refs
+    t_ref, x_ref, cols, rows, vpad, stack, tall, staged, in_sem, out_sem = refs
     order = t_ref.shape[0]
     tiles = order // LANES
     new_count = new_ref.shape[0]
@@ -266,18 +260,13 @@
     )
     load_new.start()
     load_old.start()
-    share = lax.axis_index("blk") % SPREAD
-    height = packed.shape[0] // SPREAD
-    for flip in range(SPREAD):
-        at = pl.multiple_of((share ^ flip) * height, SUBS)
-        packed[pl.ds(at, height), :] = chunk_refs[flip][...] * scale
     i = lax.broadcasted_iota(jnp.int32, (LANES, LANES), 0)
     j = lax.broadcasted_iota(jnp.int32, (LANES, LANES), 1)
-    shared = packed[:LANES, :]
-    right = packed[LANES:2 * LANES, :]
+    shared = packed[:LANES, :] * scale
+    right = packed[LANES:2 * LANES, :] * scale
     upper = jnp.where(j >= i, shared, 0.0)
     lower = jnp.where(j < i, shared, 0.0)
-    diagonal = packed[2 * LANES:2 * LANES + 1, :]
+    diagonal = packed[2 * LANES:2 * LANES + 1, :] * scale
     t_ref[:LANES, :LANES] = jnp.where(j >= i, shared, upper.T)
     t_ref[:LANES, LANES:] = right
     t_ref[LANES:, :LANES] = right.T
@@ -318,9 +307,8 @@
         store.wait()
 
 
-def factor_and_modes(chunks, s_new, s_old, shape, cell_total):
+def factor_and_modes(packed, s_new, s_old, shape, cell_total):
     order, planes, rows_y, rows_z = shape
-    height = chunks[0].shape[0] * SPREAD
     vmem = pl.BlockSpec(memory_space=pltpu.VMEM)
     hbm = pl.BlockSpec(memory_space=pl.ANY)
     square = (order, order)
@@ -330,10 +318,9 @@
             jax.ShapeDtypeStruct(square, jnp.float32),
             jax.ShapeDtypeStruct(shape, jnp.bfloat16),
         ],
-        in_specs=[vmem] * SPREAD + [hbm, hbm],
+        in_specs=[vmem, hbm, hbm],
         out_specs=[vmem, hbm],
         scratch_shapes=[
-            pltpu.VMEM((height, LANES), jnp.float32),
             pltpu.VMEM(square, jnp.float32),
             pltpu.VMEM(square, jnp.float32),
             pltpu.VMEM((PANEL, PANEL, LANES), jnp.float32),
@@ -347,7 +334,7 @@
         ],
         compiler_params=pltpu.CompilerParams(vmem_limit_bytes=VMEM_BYTES),
         name="factor",
-    )(*chunks, s_new, s_old)
+    )(packed, s_new, s_old)
 
 
 def shards(snapshots, old_modes, mode_scales, plane_counts, links):
@@ -361,10 +348,10 @@
     after = lax.ppermute(first, "blk", down)
     before = lax.ppermute(last, "blk", up)
     s_old, old_gram = scaled_rows(old_modes, mode_scales, plane_counts)
-    s_new, *chunks = filtered_rows(
+    s_new, packed = filtered_rows(
         snapshots, before, after, plane_counts, links, s_old, old_gram
     )
-    sums = sum_chunks(chunks, "blk")
+    sums = sum_over(packed, "blk")
     factor, modes = factor_and_modes(
         sums, s_new, s_old, (order, planes, rows_y, rows_z), peers * planes * rows_y * rows_z
     )

time: 54.2 us -> 61.9 us (1.14)
  blocking collectives: 0 us -> 23.6 us
  starting transfers between devices: 13.8 us -> 5.47 us
  waiting for transfers between devices: 11.3 us -> 3.73 us
    all_to_all x0 -> x3, blocking collectives: none -> 23.6 us  [the longest x1 9.3 us: sum_over(): lax.all_to_all(spread, axis, 0, 0, axis_index_groups=far)]
    ppermute x9 -> x0, starting transfers between devices: 8.3 us -> none  [swap(): return lax.ppermute(x, axis, [(i, i ^ flip) for i in range(peers)])]
    ppermute x9 -> x0, waiting for transfers between devices: 7.65 us -> none  [swap(): return lax.ppermute(x, axis, [(i, i ^ flip) for i in range(peers)])]
  transfers between devices with their start and end apart: 11 -> 2, of which waited for: 6 -> 1; matrix products, arithmetic and copies ran while one was open for 0% -> 0% of each run, Pallas kernels for 5% -> 4%
where the time goes in v4:
time: 61.9 us; the launch traced here: 61.6 us
  Pallas kernels  24.2 us (39%)
  blocking collectives  23.6 us (38%)
  starting transfers between devices  5.47 us (9%)
  waiting for transfers between devices  3.73 us (6%)
  local copies, waits for them, and re-layouts  3.19 us (5%)
  between operations  1.41 us (2%)
    pallas_call x1, Pallas kernels, factor_and_modes(): pl.pallas_call(functools.partial(factor_kernel, 1.0 / cell_total), out_sh...  17.7 us
    all_to_all x1, blocking collectives, sum_over(): lax.all_to_all(spread, axis, 0, 0, axis_index_groups=far)  9.3 us
    all_to_all x1, blocking collectives, sum_over(): arrived = lax.all_to_all(shares, axis, 0, 0, axis_index_groups=near)  7.16 us
    all_to_all x1, blocking collectives, sum_over(): sums = lax.all_to_all(spread, axis, 0, 0, axis_index_groups=near)  7.16 us
    ppermute x1, starting transfers between devices, shards(): after = lax.ppermute(first, 'blk', down)  5.47 us
    pallas_call x1, Pallas kernels, filtered_rows(): pl.pallas_call(filter_kernel, out_shape=[jax.ShapeDtypeStruct((rows, cell...  3.75 us
    ppermute x1, waiting for transfers between devices, shards(): before = lax.ppermute(last, 'blk', up)  3.73 us
    pallas_call x1, Pallas kernels, scaled_rows(): pl.pallas_call(scale_kernel, out_shape=[jax.ShapeDtypeStruct((rows, cells...  2.66 us
  transfers between devices with their start and end apart: 2, of which 1 were waited for; matrix products, arithmetic and copies ran while one was open for 0% of the time, Pallas kernels for 4%

profile of v4, /device:TPU:0, one launch (start us, length us, event | category | flops | bytes accessed | tf_op | source)
XLA Modules:
  0.0 61.6 jit_solution(14078044867959481049)
XLA Ops:
  0.6 0.0 copy-start
  0.6 0.0 copy-start.3
  1.4 1.1 %fusion = (bf16[64,1,16,128]{3,2,1,0:T(8,128)(2,1)S(1)}, bf16[64,1,16,128]{3,2,1,0:T(8,128)(2,1)S(1)}) fusion(bf16[64,2,16,128]{3,2,1,0:T(8,128)(2,1)} %snap_ref.1, s32[]{:T(128)S(6)} %select_n.3), kind=kLoop, calls=%fused_computation.1 | loop fusion | bytes 1048580 | tf_op jit(solution)/shard_map/slice | solution.py:346
  2.4 5.5 %collective-permute-start.1 = (bf16[64,1,16,128]{3,2,1,0:T(8,128)(2,1)S(1)}, bf16[64,1,16,128]{3,2,1,0:T(8,128)(2,1)S(1)}, u32[]{:S(2)}, u32[]{:S(2)}) collective-permute-start(bf16[64,1,16,128]{3,2,1,0:T(8,128)(2,1)S(1)} %get-tuple-element.14), channel_id=1, source_target_pairs={{1,0},{2,1},{3,2},{4,3},{5,4},{6,5},{7,6},{8,7},{9,8},{10,9},{11,1... | collective-permute-start | bytes 786440 | tf_op jit(solution)/shard_map/ppermute | solution.py:348
  7.9 0.0 collective-permute-start
  7.9 0.0 copy-start.1
  7.9 1.4 %copy-done.1 = bf16[192,2,16,128]{3,2,1,0:T(8,128)(2,1)S(1)} copy-done((bf16[192,2,16,128]{3,2,1,0:T(8,128)(2,1)S(1)}, bf16[192,2,16,128]{3,2,1,0:T(8,128)(2,1)}, u32[]{:S(2)}) %copy-start.1) | copy-done | bytes 1572888
  9.3 0.0 copy-start.2
  9.3 0.7 %copy-done.2 = f32[192]{0:T(256)S(1)} copy-done((f32[192]{0:T(256)S(1)}, f32[192]{0:T(256)}, u32[]{:S(2)}) %copy-start.2) | copy-done | bytes 792
  10.0 2.7 %scale_gram.1 = (bf16[192,4096]{1,0:T(8,128)(2,1)S(1)}, f32[192,192]{1,0:T(8,128)S(1)}) custom-call(f32[192]{0:T(256)S(1)} %copy-done.2, s32[1]{0:T(128)S(6)} %copy.7.count_ref, bf16[192,2,16,128]{3,2,1,0:T(8,128)(2,1)S(1)} %copy-done.1), custom_call_target="tpu_custom_call" | custom-call | flops 301989888 | bytes 6291456 | tf_op jit(solution)/shard_map/scale_gram/pallas_call | solution.py:51
  12.7 0.0 collective-permute-done.1.after_ref
  12.7 3.7 %collective-permute-done.before_ref = bf16[64,1,16,128]{3,2,1,0:T(8,128)(2,1)S(1)} collective-permute-done((bf16[64,1,16,128]{3,2,1,0:T(8,128)(2,1)S(1)}, bf16[64,1,16,128]{3,2,1,0:T(8,128)(2,1)S(1)}, u32[]{:S(2)}, u32[]{:S(2)}) %collective-permute-start) | collective-permute-done | bytes 262176 | tf_op jit(solution)/shard_map/ppermute | solution.py:349
  16.4 0.0 copy-done
  16.4 0.0 copy-done.3
  16.4 3.7 %filter_gram.1 = (bf16[64,4096]{1,0:T(8,128)(2,1)S(1)}, f32[288,128]{1,0:T(8,128)S(1)}) custom-call(s32[1]{0:T(128)S(6)} %copy.7.count_ref, s32[1,2]{1,0:T(1,128)S(1)} %copy-done.3, bf16[64,2,16,128]{3,2,1,0:T(8,128)(2,1)S(1)} %copy-done, bf16[64,1,16,128]{3,2,1,0:T(8,128)(2,1)S(1)} %collective-permute-done.before_ref, ...), custom_call_target="tpu_custom_call" | custom-call | flops 134217728 | bytes 2097152 | tf_op jit(solution)/shard_map/filter_gram/pallas_call | solution.py:137
  20.2 7.2 %all_to_all.15 = f32[4,72,128]{2,1,0:T(8,128)S(1)} all-to-all(f32[4,72,128]{2,1,0:T(8,128)S(1)} %bitcast.5), channel_id=1, replica_groups={{0,1,2,3},{4,5,6,7},{8,9,10,11},{12,13,14,15},{16,17,18,19},{20,21,22,2..., dimensions={0} | all-to-all | bytes 294912 | tf_op jit(solution)/shard_map/all_to_all | solution.py:158
  27.4 9.3 %all_to_all.16 = f32[4,72,128]{2,1,0:T(8,128)S(1)} all-to-all(f32[4,72,128]{2,1,0:T(8,128)S(1)} %broadcast_in_dim.4), channel_id=1, replica_groups={{0,4,8,12},{1,5,9,13},{2,6,10,14},{3,7,11,15},{16,20,24,28},{17,21,25,2..., dimensions={0} | all-to-all | bytes 294912 | tf_op jit(solution)/shard_map/all_to_all | solution.py:169
  36.7 7.2 %all_to_all.17 = f32[4,72,128]{2,1,0:T(8,128)S(1)} all-to-all(f32[4,72,128]{2,1,0:T(8,128)S(1)} %broadcast_in_dim.5), channel_id=1, replica_groups={{0,1,2,3},{4,5,6,7},{8,9,10,11},{12,13,14,15},{16,17,18,19},{20,21,22,2..., dimensions={0} | all-to-all | bytes 294912 | tf_op jit(solution)/shard_map/all_to_all | solution.py:172
  43.9 17.7 %factor.1 = (f32[256,256]{1,0:T(8,128)}, bf16[256,2,16,128]{3,2,1,0:T(8,128)(2,1)}) custom-call(f32[288,128]{1,0:T(8,128)S(1)} %bitcast.4, bf16[64,4096]{1,0:T(8,128)(2,1)S(1)} %get-tuple-element.11.refs_1_, bf16[192,4096]{1,0:T(8,128)(2,1)S(1)} %get-tuple-element.8.old_ref.refs_2_), custom_call_target="tpu_custom_call" | custom-call | tf_op jit(solution)/shard_map/factor/pallas_call | solution.py:315
  (4 shorter events, 0.0 us)
Async XLA Ops:
  0.6 15.8 %copy-start = (bf16[64,2,16,128]{3,2,1,0:T(8,128)(2,1)S(1)}, bf16[64,2,16,128]{3,2,1,0:T(8,128)(2,1)}, u32[]{:S(2)}) copy-start(bf16[64,2,16,128]{3,2,1,0:T(8,128)(2,1)} %snap_ref.1) | copy-start | bytes 1572868
  0.6 15.8 %copy-start.3 = (s32[1,2]{1,0:T(1,128)S(1)}, s32[1,2]{1,0:T(1,128)}, u32[]{:S(2)}) copy-start(s32[1,2]{1,0:T(1,128)} %links_ref.1) | copy-start | bytes 28
  2.4 10.2 %collective-permute-start.1 = (bf16[64,1,16,128]{3,2,1,0:T(8,128)(2,1)S(1)}, bf16[64,1,16,128]{3,2,1,0:T(8,128)(2,1)S(1)}, u32[]{:S(2)}, u32[]{:S(2)}) collective-permute-start(bf16[64,1,16,128]{3,2,1,0:T(8,128)(2,1)S(1)} %get-tuple-element.14), channel_id=1, source_target_pairs={{1,0},{2,1},{3,2},{4,3},{5,4},{6,5},{7,6},{8,7},{9,8},{10,9},{11,1... | collective-permute-start | bytes 786440 | tf_op jit(solution)/shard_map/ppermute | solution.py:348
  7.9 8.5 %collective-permute-start = (bf16[64,1,16,128]{3,2,1,0:T(8,128)(2,1)S(1)}, bf16[64,1,16,128]{3,2,1,0:T(8,128)(2,1)S(1)}, u32[]{:S(2)}, u32[]{:S(2)}) collective-permute-start(bf16[64,1,16,128]{3,2,1,0:T(8,128)(2,1)S(1)} %get-tuple-element.15), channel_id=1, source_target_pairs={{0,1},{1,2},{2,3},{3,4},{4,5},{5,6},{6,7},{7,8},{8,9},{9,10},{10,1... | collective-permute-start | bytes 786440 | tf_op jit(solution)/shard_map/ppermute | solution.py:349
  7.9 1.4 %copy-start.1 = (bf16[192,2,16,128]{3,2,1,0:T(8,128)(2,1)S(1)}, bf16[192,2,16,128]{3,2,1,0:T(8,128)(2,1)}, u32[]{:S(2)}) copy-start(bf16[192,2,16,128]{3,2,1,0:T(8,128)(2,1)} %old_ref.1) | copy-start | bytes 4718596
  9.3 0.7 %copy-start.2 = (f32[192]{0:T(256)S(1)}, f32[192]{0:T(256)}, u32[]{:S(2)}) copy-start(f32[192]{0:T(256)} %scales_ref.1) | copy-start | bytes 2308

commit v5 on v3

--- a/solution.py
+++ b/solution.py
@@ -26,11 +26,11 @@
 
 
 def relay(tall, s_ref, plane, rows_y):
-    rows = s_ref.shape[0]
+    rows = s_ref.shape[1]
     for y in range(rows_y):
-        column = (plane * rows_y + y) * LANES
-        part = tall[pl.ds(y, rows, stride=rows_y), :]
-        s_ref[:, column:column + LANES] = part.astype(jnp.bfloat16)
+        part = tall[pl.ds(y, rows, stride=rows_y), :].astype(jnp.bfloat16)
+        half = (y % 2) * LANES
+        s_ref[(plane * rows_y + y) // 2, :, half:half + LANES] = part
 
 
 def scale_kernel(scales_ref, count_ref, old_ref, s_ref, gram_ref, tall):
@@ -45,7 +45,7 @@
             tall[pl.ds(at, rows_y), :] = old_ref[row, plane].astype(jnp.float32) * weight * alive
 
         relay(tall, s_ref, plane, rows_y)
-    gram_ref[...] = nt_dot(s_ref[...], s_ref[...])
+    gram_ref[...] = sum(nt_dot(s_ref[k], s_ref[k]) for k in range(s_ref.shape[0]))
 
 
 def scaled_rows(old_modes, mode_scales, plane_counts):
@@ -56,7 +56,7 @@
     return pl.pallas_call(
         scale_kernel,
         out_shape=[
-            jax.ShapeDtypeStruct((rows, cells), jnp.bfloat16),
+            jax.ShapeDtypeStruct((planes * rows_y // 2, rows, 2 * rows_z), jnp.bfloat16),
             jax.ShapeDtypeStruct((rows, rows), jnp.float32),
         ],
         in_specs=[smem, smem, vmem],
@@ -111,9 +111,9 @@
             tall[pl.ds(at, rows_y), :] = field
 
         relay(tall, s_ref, plane, rows_y)
-    fresh = s_ref[...]
-    new_new = nt_dot(fresh, fresh)
-    new_old = nt_dot(fresh, old_ref[...])
+    pairs = range(s_ref.shape[0])
+    new_new = sum(nt_dot(s_ref[k], s_ref[k]) for k in pairs)
+    new_old = sum(nt_dot(s_ref[k], old_ref[k]) for k in pairs)
     split = LANES - rows
     old_old = oldgram_ref[...]
     top = jnp.concatenate([new_new, new_old[:, :split]], axis=1)
@@ -140,14 +140,14 @@
 def filtered_rows(snapshots, before, after, plane_counts, links, s_old, old_gram):
     rows, planes, rows_y, rows_z = snapshots.shape
     cells = planes * rows_y * rows_z
-    order = rows + s_old.shape[0]
+    order = rows + s_old.shape[1]
     height = packed_rows(order)
     smem = pl.BlockSpec(memory_space=pltpu.SMEM)
     vmem = pl.BlockSpec(memory_space=pltpu.VMEM)
     chunk = jax.ShapeDtypeStruct((height // SPREAD, LANES), jnp.float32)
     return pl.pallas_call(
         filter_kernel,
-        out_shape=[jax.ShapeDtypeStruct((rows, cells), jnp.bfloat16)] + [chunk] * SPREAD,
+        out_shape=[jax.ShapeDtypeStruct((planes * rows_y // 2, rows, 2 * rows_z), jnp.bfloat16)] + [chunk] * SPREAD,
         in_specs=[smem, smem] + [vmem] * 5,
         out_specs=[vmem] * (1 + SPREAD),
         scratch_shapes=[
@@ -178,29 +178,70 @@
     return [total] + [swap(total, axis, d) for d in range(1, SPREAD)]
 
 
-def factor_panel(tile, tiles, panel, t_ref, f_ref, x_ref, cols, rows, vpad):
+def split_three(x):
+    one = x.astype(jnp.bfloat16)
+    rest = x - one.astype(jnp.float32)
+    two = rest.astype(jnp.bfloat16)
+    three = (rest - two.astype(jnp.float32)).astype(jnp.bfloat16)
+    return one, two, three
+
+
+LEFT = (0, 0, 0, 1, 1, 2)
+RIGHT = (0, 1, 2, 0, 1, 0)
+
+
+def eliminate_all(panel, t_ref, wide):
+    tiles, order, _ = t_ref.shape
+    first = panel * PANEL
+    tile = jnp.maximum(panel, 0) // (LANES // PANEL)
+    left = split_three(t_ref[tile])
+    left = jnp.concatenate([left[k] for k in LEFT], axis=1)
+    update = jnp.dot(left, wide[lax.rem(panel + 2, 2)], preferred_element_type=jnp.float32)
+    row = lax.broadcasted_iota(jnp.int32, (order, LANES), 0)
+    lane = lax.broadcasted_iota(jnp.int32, (order, LANES), 1)
+    below = row >= first + 2 * PANEL
+    for s in range(tiles):
+        column = lane + s * LANES
+        mine = (column >= first) & (column < first + PANEL)
+        held = t_ref[s]
+        fresh = jnp.where(mine, 0.0, held) - update[:, s * LANES:(s + 1) * LANES]
+        t_ref[s] = jnp.where(below, fresh, held)
+
+
+def factor_panel(panel, t_ref, f_ref, x_ref, cols, rows, wide, narrow):
+    tiles, order, _ = t_ref.shape
     first = pl.multiple_of(panel * PANEL, PANEL)
+    tile = panel // (LANES // PANEL)
     off = pl.multiple_of(first - tile * LANES, PANEL)
     here = pl.ds(first, PANEL)
     lane = lax.broadcasted_iota(jnp.int32, (PANEL, LANES), 1)
     sub = lax.broadcasted_iota(jnp.int32, (PANEL, LANES), 0)
-    inside = (lane >= off) & (lane < off + PANEL)
-    own = t_ref[here, tile * LANES:(tile + 1) * LANES]
-    for s in range(tiles):
-        if s == tile:
-            block = jnp.where(inside, jnp.where(lane - off == sub, 1.0, 0.0), own)
-        else:
-            block = t_ref[here, s * LANES:(s + 1) * LANES]
-        rows[pl.ds(s, PANEL, stride=SUBS), :] = block
-    rows[pl.ds(tiles, PANEL, stride=SUBS), :] = own
-    turned = pltpu.roll(own, lax.rem(LANES - off, LANES), axis=1)
+    own = t_ref[tile, here, :]
+    turn = lax.rem(LANES - off, LANES)
+    turned = pltpu.roll(own, turn, axis=1)
     for j in range(PANEL):
         cols[j] = jnp.broadcast_to(turned[:, j:j + 1], (PANEL, LANES))
+    for s in range(tiles):
+        column = lane + s * LANES
+        inside = (column >= first) & (column < first + PANEL)
+        unit_rows = jnp.where(column - first == sub, 1.0, 0.0)
+        rows[pl.ds(s, PANEL, stride=SUBS), :] = jnp.where(inside, unit_rows, t_ref[s, here, :])
+    rows[pl.ds(tiles, PANEL, stride=SUBS), :] = own
     entry = [
         [jnp.broadcast_to(cols[j, i:i + 1, :], (SUBS, LANES)) for j in range(i + 1)]
         for i in range(PANEL)
     ]
     y = [rows[i * SUBS:(i + 1) * SUBS, :] for i in range(PANEL)]
+    eliminate_all(panel - 1, t_ref, wide)
+    after = jnp.minimum(first + PANEL, order - PANEL)
+    after = pl.ds(pl.multiple_of(after, PANEL), PANEL)
+    ahead = pltpu.roll(t_ref[tile, after, :], turn, axis=1)
+    pieces = [jnp.where(lane < PANEL, piece.astype(jnp.float32), 0.0) for piece in split_three(ahead)]
+    left = pieces[LEFT[0]]
+    for k in range(1, len(LEFT)):
+        left = left + pltpu.roll(pieces[LEFT[k]], k * PANEL, axis=1)
+    left = left.astype(jnp.bfloat16)
+
     unit = [[None] * PANEL for _ in range(PANEL)]
     recip = []
     for k in range(PANEL):
@@ -209,7 +250,11 @@
             unit[i][k] = entry[i][k] * recip[k]
         for j in range(k + 1, PANEL):
             for i in range(j, PANEL):
-                entry[i][j] = entry[i][j] - unit[i][k] * entry[j][k]
+                if i == j:
+                    part = (entry[i][k] * entry[i][k]) * recip[k]
+                else:
+                    part = unit[i][k] * entry[j][k]
+                entry[i][j] = entry[i][j] - part
         for i in range(k + 1, PANEL):
             y[i] = y[i] - unit[i][k] * y[k]
     v = [recip[i] * y[i] for i in range(PANEL)]
@@ -218,51 +263,48 @@
             v[i] = v[i] - unit[j][i] * v[j]
     for i in range(PANEL):
         rows[i * SUBS:(i + 1) * SUBS, :] = v[i]
+    v = jnp.concatenate([rows[pl.ds(s, PANEL, stride=SUBS), :] for s in range(tiles)], axis=1)
+    v = split_three(v)
+    for k in range(len(RIGHT)):
+        narrow[k * PANEL:(k + 1) * PANEL, :] = v[RIGHT[k]]
+    update = jnp.dot(left, narrow[...], preferred_element_type=jnp.float32)
+    more = first + PANEL < order
     for s in range(tiles):
-        vpad[pl.ds(off, PANEL), s * LANES:(s + 1) * LANES] = rows[pl.ds(s, PANEL, stride=SUBS), :]
+        column = lane + s * LANES
+        mine = (column >= first) & (column < first + PANEL)
+        held = t_ref[s, after, :]
+        fresh = jnp.where(mine, 0.0, held) - update[:, s * LANES:(s + 1) * LANES]
+        t_ref[s, after, :] = jnp.where(more, fresh, held)
+    side = lax.rem(panel, 2)
+    old_off = lax.rem(off + LANES - 2 * PANEL, LANES)
+    for k in range(len(RIGHT)):
+        old_at = pl.multiple_of(old_off + k * LANES, PANEL)
+        wide[side, pl.ds(old_at, PANEL), :] = jnp.zeros((PANEL, order), jnp.bfloat16)
+        at = pl.multiple_of(off + k * LANES, PANEL)
+        wide[side, pl.ds(at, PANEL), :] = v[RIGHT[k]]
+
     for i in range(PANEL):
         rows[i * SUBS:(i + 1) * SUBS, :] = jnp.sqrt(recip[i]) * y[i]
-    zero = jnp.zeros((PANEL, LANES), jnp.float32)
+    whole = rows[pl.ds(tiles, PANEL, stride=SUBS), :]
     for s in range(tiles):
         span = slice(s * LANES, (s + 1) * LANES)
+        column = lane + s * LANES
         part = rows[pl.ds(s, PANEL, stride=SUBS), :]
-        if s == tile:
-            whole = rows[pl.ds(tiles, PANEL, stride=SUBS), :]
-            f_ref[here, span] = jnp.where(lane >= off + sub, whole, 0.0)
-            x_ref[here, span] = jnp.where(lane <= off + sub, part, 0.0)
-        else:
-            f_ref[here, span] = part if s > tile else zero
-            x_ref[here, span] = part if s < tile else zero
-    low = tile * LANES
-    order = t_ref.shape[0]
-    update = jnp.dot(
-        t_ref[low:, low:low + LANES],
-        vpad[...],
-        precision=lax.Precision.HIGHEST,
-        preferred_element_type=jnp.float32,
-    )
-    row_id = lax.broadcasted_iota(jnp.int32, (order - low, LANES), 0) + low
-    lane_id = lax.broadcasted_iota(jnp.int32, (order - low, LANES), 1)
-    below = row_id >= first + PANEL
-    mine = (lane_id >= off) & (lane_id < off + PANEL)
-    for s in range(tiles):
-        span = slice(s * LANES, (s + 1) * LANES)
-        held = t_ref[low:, span]
-        base = jnp.where(mine, 0.0, held) if s == tile else held
-        t_ref[low:, span] = jnp.where(below, base - update[:, span], held)
-    vpad[pl.ds(off, PANEL), :] = jnp.zeros((PANEL, order), jnp.float32)
+        inside = (column >= first) & (column < first + PANEL)
+        f_ref[here, span] = jnp.where(column >= first + sub, jnp.where(inside, whole, part), 0.0)
+        x_ref[here, span] = jnp.where(column <= first + sub, part, 0.0)
 
 
 def factor_kernel(scale, *refs):
     chunk_refs, refs = refs[:SPREAD], refs[SPREAD:]
-    new_ref, old_ref, f_ref, out_ref, refs = *refs[:4], refs[4:]
-    packed, t_ref, x_ref, cols, rows, vpad, stack, tall, staged, in_sem, out_sem = refs
-    order = t_ref.shape[0]
-    tiles = order // LANES
-    new_count = new_ref.shape[0]
-    load_new = pltpu.make_async_copy(new_ref, stack.at[pl.ds(0, new_count)], in_sem.at[0])
+    new_ref, old_ref, f_ref, out_ref, *refs = refs
+    packed, t_ref, x_ref, cols, rows, wide, narrow, x_pair, stack, *refs = refs
+    tall, staged, in_sem, out_sem = refs
+    tiles, order, _ = t_ref.shape
+    new_count = new_ref.shape[1]
+    load_new = pltpu.make_async_copy(new_ref, stack.at[:, pl.ds(0, new_count)], in_sem.at[0])
     load_old = pltpu.make_async_copy(
-        old_ref, stack.at[pl.ds(new_count, order - new_count)], in_sem.at[1]
+        old_ref, stack.at[:, pl.ds(new_count, order - new_count)], in_sem.at[1]
     )
     load_new.start()
     load_old.start()
@@ -278,44 +320,55 @@
     upper = jnp.where(j >= i, shared, 0.0)
     lower = jnp.where(j < i, shared, 0.0)
     diagonal = packed[2 * LANES:2 * LANES + 1, :]
-    t_ref[:LANES, :LANES] = jnp.where(j >= i, shared, upper.T)
-    t_ref[:LANES, LANES:] = right
-    t_ref[LANES:, :LANES] = right.T
+    t_ref[0, :LANES, :] = jnp.where(j >= i, shared, upper.T)
+    t_ref[1, :LANES, :] = right
+    t_ref[0, LANES:, :] = right.T
     corner = jnp.where(j < i, shared, lower.T)
-    t_ref[LANES:, LANES:] = jnp.where(i == j, diagonal, corner)
-    vpad[...] = jnp.zeros(vpad.shape, jnp.float32)
+    t_ref[1, LANES:, :] = jnp.where(i == j, diagonal, corner)
+    wide[...] = jnp.zeros(wide.shape, wide.dtype)
+    narrow[...] = jnp.zeros(narrow.shape, narrow.dtype)
     rows[...] = jnp.zeros(rows.shape, jnp.float32)
-    per_tile = LANES // PANEL
-    for tile in range(tiles):
-        @pl.loop(tile * per_tile, (tile + 1) * per_tile)
-        def _(panel):
-            factor_panel(tile, tiles, panel, t_ref, f_ref, x_ref, cols, rows, vpad)
+
+    @pl.loop(0, order // PANEL)
+    def _(panel):
+        factor_panel(panel, t_ref, f_ref, x_ref, cols, rows, wide, narrow)
+
     inverse = x_ref[...]
     high = inverse.astype(jnp.bfloat16)
     low = (inverse - high.astype(jnp.float32)).astype(jnp.bfloat16)
+    x_pair[...] = jnp.concatenate([high, low], axis=1)
     load_new.wait()
     load_old.wait()
     _, planes, rows_y, rows_z = out_ref.shape
-    stores = []
+    steps = rows_y // 2
+    count = order // steps
+
+    def store(plane, step):
+        some = pl.ds(step * count, count)
+        return pltpu.make_async_copy(
+            staged.at[plane, some], out_ref.at[some, plane], out_sem.at[plane, step]
+        )
+
+    for plane in range(planes + 1):
+        @pl.loop(0, steps)
+        def _(step):
+            if plane < planes:
+                block = stack[plane * steps + step]
+                sums = jnp.dot(x_pair[:, :order], block, preferred_element_type=jnp.float32)
+                sums = sums + jnp.dot(x_pair[:, order:], block, preferred_element_type=jnp.float32)
+                for y in (0, 1):
+                    part = sums[:, y * rows_z:(y + 1) * rows_z]
+                    tall[plane % 2, pl.ds(2 * step + y, order, stride=rows_y), :] = part
+            if plane > 0:
+                at = pl.multiple_of(step * count * rows_y, count * rows_y)
+                ready = tall[(plane - 1) % 2, pl.ds(at, count * rows_y), :].astype(jnp.bfloat16)
+                staged[plane - 1, pl.ds(step * count, count)] = ready.reshape(count, rows_y, rows_z)
+                store(plane - 1, step).start()
+
     for plane in range(planes):
-        for pair in range(0, rows_y, 2):
-            column = (plane * rows_y + pair) * LANES
-            block = stack[:, column:column + 2 * LANES]
-            sums = jnp.dot(high, block, preferred_element_type=jnp.float32)
-            sums = sums + jnp.dot(low, block, preferred_element_type=jnp.float32)
-            for y in (0, 1):
-                tall[pl.ds(pair + y, order, stride=rows_y), :] = sums[:, y * LANES:(y + 1) * LANES]
-
-        @pl.loop(0, order, unroll=8)
-        def _(row):
-            at = pl.multiple_of(row * rows_y, rows_y)
-            staged[plane, row] = tall[pl.ds(at, rows_y), :].astype(jnp.bfloat16)
-
-        store = pltpu.make_async_copy(staged.at[plane], out_ref.at[:, plane], out_sem.at[plane])
-        store.start()
-        stores.append(store)
-    for store in stores:
-        store.wait()
+        @pl.loop(0, steps)
+        def _(step):
+            store(plane, step).wait()
 
 
 def factor_and_modes(chunks, s_new, s_old, shape, cell_total):
@@ -334,16 +387,18 @@
         out_specs=[vmem, hbm],
         scratch_shapes=[
             pltpu.VMEM((height, LANES), jnp.float32),
-            pltpu.VMEM(square, jnp.float32),
+            pltpu.VMEM((order // LANES, order, LANES), jnp.float32),
             pltpu.VMEM(square, jnp.float32),
             pltpu.VMEM((PANEL, PANEL, LANES), jnp.float32),
             pltpu.VMEM((PANEL * SUBS, LANES), jnp.float32),
-            pltpu.VMEM((LANES, order), jnp.float32),
-            pltpu.VMEM((order, planes * rows_y * rows_z), jnp.bfloat16),
-            pltpu.VMEM((order * rows_y, rows_z), jnp.float32),
+            pltpu.VMEM((2, len(LEFT) * LANES, order), jnp.bfloat16),
+            pltpu.VMEM((LANES, order), jnp.bfloat16),
+            pltpu.VMEM((order, 2 * order), jnp.bfloat16),
+            pltpu.VMEM((planes * rows_y // 2, order, 2 * rows_z), jnp.bfloat16),
+            pltpu.VMEM((2, order * rows_y, rows_z), jnp.float32),
             pltpu.VMEM((planes, order, rows_y, rows_z), jnp.bfloat16),
             pltpu.SemaphoreType.DMA((2,)),
-            pltpu.SemaphoreType.DMA((planes,)),
+            pltpu.SemaphoreType.DMA((planes, rows_y // 2)),
         ],
         compiler_params=pltpu.CompilerParams(vmem_limit_bytes=VMEM_BYTES),
         name="factor",

time: 54.2 us -> 55.3 us (1.020)
  Pallas kernels: 24.3 us -> 25.4 us
    pallas_call x1, Pallas kernels: 17.8 us -> 18.9 us  [factor_and_modes(): pl.pallas_call(functools.partial(factor_kernel, 1.0 / cell_total), out_sh...]
where the time goes in v5:
time: 55.3 us; the launch traced here: 55.1 us
  Pallas kernels  25.4 us (46%)
  starting transfers between devices  13.8 us (25%)
  waiting for transfers between devices  11.3 us (20%)
  local copies, waits for them, and re-layouts  3.17 us (6%)
  between operations  1.42 us (3%)
    pallas_call x1, Pallas kernels, factor_and_modes(): pl.pallas_call(functools.partial(factor_kernel, 1.0 / cell_total), out_sh...  18.9 us
    ppermute x9, starting transfers between devices, swap(): return lax.ppermute(x, axis, [(i, i ^ flip) for i in range(peers)])  8.3 us
    ppermute x9, waiting for transfers between devices, swap(): return lax.ppermute(x, axis, [(i, i ^ flip) for i in range(peers)])  7.61 us
    ppermute x1, starting transfers between devices, shards(): after = lax.ppermute(first, 'blk', down)  5.47 us
    pallas_call x1, Pallas kernels, filtered_rows(): pl.pallas_call(filter_kernel, out_shape=[jax.ShapeDtypeStruct((planes * r...  3.75 us
    ppermute x1, waiting for transfers between devices, shards(): before = lax.ppermute(last, 'blk', up)  3.7 us
    pallas_call x1, Pallas kernels, scaled_rows(): pl.pallas_call(scale_kernel, out_shape=[jax.ShapeDtypeStruct((planes * ro...  2.68 us
    unnamed x8, local copies, waits for them, and re-layouts  2.09 us
  transfers between devices with their start and end apart: 11, of which 6 were waited for; matrix products, arithmetic and copies ran while one was open for 0% of the time, Pallas kernels for 5%

profile of v5, /device:TPU:0, one launch (start us, length us, event | category | flops | bytes accessed | tf_op | source)
XLA Modules:
  0.0 55.1 jit_solution(12018938816650084547)
XLA Ops:
  0.6 0.0 copy-start
  0.6 0.0 copy-start.3
  1.4 1.1 %fusion = (bf16[64,1,16,128]{3,2,1,0:T(8,128)(2,1)S(1)}, bf16[64,1,16,128]{3,2,1,0:T(8,128)(2,1)S(1)}) fusion(bf16[64,2,16,128]{3,2,1,0:T(8,128)(2,1)} %snap_ref.1, s32[]{:T(128)S(6)} %select_n.3), kind=kLoop, calls=%fused_computation.3 | loop fusion | bytes 1048580 | tf_op jit(solution)/shard_map/slice | solution.py:414
  2.4 5.5 %collective-permute-start.1 = (bf16[64,1,16,128]{3,2,1,0:T(8,128)(2,1)S(1)}, bf16[64,1,16,128]{3,2,1,0:T(8,128)(2,1)S(1)}, u32[]{:S(2)}, u32[]{:S(2)}) collective-permute-start(bf16[64,1,16,128]{3,2,1,0:T(8,128)(2,1)S(1)} %get-tuple-element.20), channel_id=1, source_target_pairs={{1,0},{2,1},{3,2},{4,3},{5,4},{6,5},{7,6},{8,7},{9,8},{10,9},{11,1... | collective-permute-start | bytes 786440 | tf_op jit(solution)/shard_map/ppermute | solution.py:416
  7.9 0.0 collective-permute-start
  7.9 0.0 copy-start.1
  7.9 1.4 %copy-done.1 = bf16[192,2,16,128]{3,2,1,0:T(8,128)(2,1)S(1)} copy-done((bf16[192,2,16,128]{3,2,1,0:T(8,128)(2,1)S(1)}, bf16[192,2,16,128]{3,2,1,0:T(8,128)(2,1)}, u32[]{:S(2)}) %copy-start.1) | copy-done | bytes 1572888
  9.3 0.0 copy-start.2
  9.3 0.7 %copy-done.2 = f32[192]{0:T(256)S(1)} copy-done((f32[192]{0:T(256)S(1)}, f32[192]{0:T(256)}, u32[]{:S(2)}) %copy-start.2) | copy-done | bytes 792
  10.0 2.7 %scale_gram.1 = (bf16[16,192,256]{2,1,0:T(8,128)(2,1)S(1)}, f32[192,192]{1,0:T(8,128)S(1)}) custom-call(f32[192]{0:T(256)S(1)} %copy-done.2, s32[1]{0:T(128)S(6)} %copy.7.count_ref, bf16[192,2,16,128]{3,2,1,0:T(8,128)(2,1)S(1)} %copy-done.1), custom_call_target="tpu_custom_call" | custom-call | flops 301989888 | bytes 6291456 | tf_op jit(solution)/shard_map/scale_gram/pallas_call | solution.py:56
  12.7 0.0 collective-permute-done.1.after_ref
  12.7 3.7 %collective-permute-done.before_ref = bf16[64,1,16,128]{3,2,1,0:T(8,128)(2,1)S(1)} collective-permute-done((bf16[64,1,16,128]{3,2,1,0:T(8,128)(2,1)S(1)}, bf16[64,1,16,128]{3,2,1,0:T(8,128)(2,1)S(1)}, u32[]{:S(2)}, u32[]{:S(2)}) %collective-permute-start) | collective-permute-done | bytes 262176 | tf_op jit(solution)/shard_map/ppermute | solution.py:417
  16.4 0.0 copy-done
  16.4 0.0 copy-done.3
  16.4 3.8 %filter_gram.1 = (bf16[16,64,256]{2,1,0:T(8,128)(2,1)S(1)}, f32[72,128]{1,0:T(8,128)S(1)}, f32[72,128]{1,0:T(8,128)S(1)}, f32[72,128]{1,0:T(8,128)S(1)}, f32[72,128]{1,0:T(8,128)S(1)}) custom-call(s32[1]{0:T(128)S(6)} %copy.7.count_ref, s32[1,2]{1,0:T(1,128)S(1)} %copy-done.3, bf16[64,2,16,128]{3,2,1,0:T(8,128)(2,1)S(1)} %copy-done, ...), custom_call_target="tpu_custom_call" | custom-call | flops 134217728 | bytes 2097152 | tf_op jit(solution)/shard_map/filter_gram/pallas_call | solution.py:148
  20.2 0.1 collective-permute-start.2
  20.2 0.1 collective-permute-start.3
  20.3 1.8 %collective-permute-start.4 = (f32[72,128]{1,0:T(8,128)S(1)}, f32[72,128]{1,0:T(8,128)S(1)}, u32[]{:S(2)}, u32[]{:S(2)}) collective-permute-start(f32[72,128]{1,0:T(8,128)S(1)} %get-tuple-element.16), channel_id=1, source_target_pairs={{0,3},{1,2},{2,1},{3,0},{4,7},{5,6},{6,5},{7,4},{8,11},{9,10},{10,... | collective-permute-start | bytes 110600 | tf_op jit(solution)/shard_map/ppermute | solution.py:25
  22.1 0.0 collective-permute-done.2
  22.1 2.4 %collective-permute-done.3 = f32[72,128]{1,0:T(8,128)S(1)} collective-permute-done((f32[72,128]{1,0:T(8,128)S(1)}, f32[72,128]{1,0:T(8,128)S(1)}, u32[]{:S(2)}, u32[]{:S(2)}) %collective-permute-start.3) | collective-permute-done | bytes 36896 | tf_op jit(solution)/shard_map/ppermute | solution.py:25
  24.5 0.0 collective-permute-done.4
  24.5 1.2 %collective-permute-start.7 = (f32[72,128]{1,0:T(8,128)S(1)}, f32[72,128]{1,0:T(8,128)S(1)}, u32[]{:S(2)}, u32[]{:S(2)}) collective-permute-start(f32[72,128]{1,0:T(8,128)S(1)} %add_add_fusion.1), channel_id=1, source_target_pairs={{0,12},{1,13},{2,14},{3,15},{4,8},{5,9},{6,10},{7,11},{8,4},{9,5},... | collective-permute-start | bytes 110600 | tf_op jit(solution)/shard_map/ppermute | solution.py:25
  25.8 0.0 collective-permute-start.6
  25.8 3.2 %collective-permute-start.5 = (f32[72,128]{1,0:T(8,128)S(1)}, f32[72,128]{1,0:T(8,128)S(1)}, u32[]{:S(2)}, u32[]{:S(2)}) collective-permute-start(f32[72,128]{1,0:T(8,128)S(1)} %add_add_fusion.1), channel_id=1, source_target_pairs={{0,4},{1,5},{2,6},{3,7},{4,0},{5,1},{6,2},{7,3},{8,12},{9,13},{10,... | collective-permute-start | bytes 110600 | tf_op jit(solution)/shard_map/ppermute | solution.py:25
  29.0 1.6 %collective-permute-done.7 = f32[72,128]{1,0:T(8,128)S(1)} collective-permute-done((f32[72,128]{1,0:T(8,128)S(1)}, f32[72,128]{1,0:T(8,128)S(1)}, u32[]{:S(2)}, u32[]{:S(2)}) %collective-permute-start.7) | collective-permute-done | bytes 36896 | tf_op jit(solution)/shard_map/ppermute | solution.py:25
  30.6 0.9 %collective-permute-done.6 = f32[72,128]{1,0:T(8,128)S(1)} collective-permute-done((f32[72,128]{1,0:T(8,128)S(1)}, f32[72,128]{1,0:T(8,128)S(1)}, u32[]{:S(2)}, u32[]{:S(2)}) %collective-permute-start.6) | collective-permute-done | bytes 36896 | tf_op jit(solution)/shard_map/ppermute | solution.py:25
  31.5 0.0 collective-permute-done.5
  31.5 0.1 collective-permute-start.10
  31.6 1.5 %collective-permute-start.9 = (f32[72,128]{1,0:T(8,128)S(1)}, f32[72,128]{1,0:T(8,128)S(1)}, u32[]{:S(2)}, u32[]{:S(2)}) collective-permute-start(f32[72,128]{1,0:T(8,128)S(1)} %add_add_fusion.refs_0_), channel_id=1, source_target_pairs={{0,2},{1,3},{2,0},{3,1},{4,6},{5,7},{6,4},{7,5},{8,10},{9,11},{10,... | collective-permute-start | bytes 110600 | tf_op jit(solution)/shard_map/ppermute | solution.py:25
  33.1 0.3 collective-permute-start.8
  33.4 1.8 %collective-permute-done.10.refs_3_ = f32[72,128]{1,0:T(8,128)S(1)} collective-permute-done((f32[72,128]{1,0:T(8,128)S(1)}, f32[72,128]{1,0:T(8,128)S(1)}, u32[]{:S(2)}, u32[]{:S(2)}) %collective-permute-start.10) | collective-permute-done | bytes 36896 | tf_op jit(solution)/shard_map/ppermute | solution.py:25
  35.3 0.9 %collective-permute-done.9.refs_2_ = f32[72,128]{1,0:T(8,128)S(1)} collective-permute-done((f32[72,128]{1,0:T(8,128)S(1)}, f32[72,128]{1,0:T(8,128)S(1)}, u32[]{:S(2)}, u32[]{:S(2)}) %collective-permute-start.9) | collective-permute-done | bytes 36896 | tf_op jit(solution)/shard_map/ppermute | solution.py:25
  36.1 0.0 collective-permute-done.8.refs_1_
  36.1 18.9 %factor.1 = (f32[256,256]{1,0:T(8,128)}, bf16[256,2,16,128]{3,2,1,0:T(8,128)(2,1)}) custom-call(f32[72,128]{1,0:T(8,128)S(1)} %add_add_fusion.refs_0_, f32[72,128]{1,0:T(8,128)S(1)} %collective-permute-done.8.refs_1_, f32[72,128]{1,0:T(8,128)S(1)} %collective-permute-done.9.refs_2_, f32[72,128]{1,0:T(8,128)S(1)} %collective-permute-done.10.refs_3_, ...), custom_call_target="tpu_custom_call" | custom-call | tf_op jit(solution)/shard_map/factor/pallas_call | solution.py:380
  (2 shorter events, 0.0 us)
Async XLA Ops:
  0.6 15.8 %copy-start = (bf16[64,2,16,128]{3,2,1,0:T(8,128)(2,1)S(1)}, bf16[64,2,16,128]{3,2,1,0:T(8,128)(2,1)}, u32[]{:S(2)}) copy-start(bf16[64,2,16,128]{3,2,1,0:T(8,128)(2,1)} %snap_ref.1) | copy-start | bytes 1572868
  0.6 15.8 %copy-start.3 = (s32[1,2]{1,0:T(1,128)S(1)}, s32[1,2]{1,0:T(1,128)}, u32[]{:S(2)}) copy-start(s32[1,2]{1,0:T(1,128)} %links_ref.1) | copy-start | bytes 28
  2.4 10.3 %collective-permute-start.1 = (bf16[64,1,16,128]{3,2,1,0:T(8,128)(2,1)S(1)}, bf16[64,1,16,128]{3,2,1,0:T(8,128)(2,1)S(1)}, u32[]{:S(2)}, u32[]{:S(2)}) collective-permute-start(bf16[64,1,16,128]{3,2,1,0:T(8,128)(2,1)S(1)} %get-tuple-element.20), channel_id=1, source_target_pairs={{1,0},{2,1},{3,2},{4,3},{5,4},{6,5},{7,6},{8,7},{9,8},{10,9},{11,1... | collective-permute-start | bytes 786440 | tf_op jit(solution)/shard_map/ppermute | solution.py:416
  7.9 8.5 %collective-permute-start = (bf16[64,1,16,128]{3,2,1,0:T(8,128)(2,1)S(1)}, bf16[64,1,16,128]{3,2,1,0:T(8,128)(2,1)S(1)}, u32[]{:S(2)}, u32[]{:S(2)}) collective-permute-start(bf16[64,1,16,128]{3,2,1,0:T(8,128)(2,1)S(1)} %get-tuple-element.21), channel_id=1, source_target_pairs={{0,1},{1,2},{2,3},{3,4},{4,5},{5,6},{6,7},{7,8},{8,9},{9,10},{10,1... | collective-permute-start | bytes 786440 | tf_op jit(solution)/shard_map/ppermute | solution.py:417
  7.9 1.4 %copy-start.1 = (bf16[192,2,16,128]{3,2,1,0:T(8,128)(2,1)S(1)}, bf16[192,2,16,128]{3,2,1,0:T(8,128)(2,1)}, u32[]{:S(2)}) copy-start(bf16[192,2,16,128]{3,2,1,0:T(8,128)(2,1)} %old_ref.1) | copy-start | bytes 4718596
  9.3 0.7 %copy-start.2 = (f32[192]{0:T(256)S(1)}, f32[192]{0:T(256)}, u32[]{:S(2)}) copy-start(f32[192]{0:T(256)} %scales_ref.1) | copy-start | bytes 2308
  20.2 1.9 %collective-permute-start.2 = (f32[72,128]{1,0:T(8,128)S(1)}, f32[72,128]{1,0:T(8,128)S(1)}, u32[]{:S(2)}, u32[]{:S(2)}) collective-permute-start(f32[72,128]{1,0:T(8,128)S(1)} %get-tuple-element.14), channel_id=1, source_target_pairs={{0,1},{1,0},{2,3},{3,2},{4,5},{5,4},{6,7},{7,6},{8,9},{9,8},{10,11... | collective-permute-start | bytes 110600 | tf_op jit(solution)/shard_map/ppermute | solution.py:25
  20.2 4.3 %collective-permute-start.3 = (f32[72,128]{1,0:T(8,128)S(1)}, f32[72,128]{1,0:T(8,128)S(1)}, u32[]{:S(2)}, u32[]{:S(2)}) collective-permute-start(f32[72,128]{1,0:T(8,128)S(1)} %get-tuple-element.15), channel_id=1, source_target_pairs={{0,2},{1,3},{2,0},{3,1},{4,6},{5,7},{6,4},{7,5},{8,10},{9,11},{10,... | collective-permute-start | bytes 110600 | tf_op jit(solution)/shard_map/ppermute | solution.py:25
  20.3 4.2 %collective-permute-start.4 = (f32[72,128]{1,0:T(8,128)S(1)}, f32[72,128]{1,0:T(8,128)S(1)}, u32[]{:S(2)}, u32[]{:S(2)}) collective-permute-start(f32[72,128]{1,0:T(8,128)S(1)} %get-tuple-element.16), channel_id=1, source_target_pairs={{0,3},{1,2},{2,1},{3,0},{4,7},{5,6},{6,5},{7,4},{8,11},{9,10},{10,... | collective-permute-start | bytes 110600 | tf_op jit(solution)/shard_map/ppermute | solution.py:25
  24.5 6.1 %collective-permute-start.7 = (f32[72,128]{1,0:T(8,128)S(1)}, f32[72,128]{1,0:T(8,128)S(1)}, u32[]{:S(2)}, u32[]{:S(2)}) collective-permute-start(f32[72,128]{1,0:T(8,128)S(1)} %add_add_fusion.1), channel_id=1, source_target_pairs={{0,12},{1,13},{2,14},{3,15},{4,8},{5,9},{6,10},{7,11},{8,4},{9,5},... | collective-permute-start | bytes 110600 | tf_op jit(solution)/shard_map/ppermute | solution.py:25
  25.8 5.7 %collective-permute-start.6 = (f32[72,128]{1,0:T(8,128)S(1)}, f32[72,128]{1,0:T(8,128)S(1)}, u32[]{:S(2)}, u32[]{:S(2)}) collective-permute-start(f32[72,128]{1,0:T(8,128)S(1)} %add_add_fusion.1), channel_id=1, source_target_pairs={{0,8},{1,9},{2,10},{3,11},{4,12},{5,13},{6,14},{7,15},{8,0},{9,1},... | collective-permute-start | bytes 110600 | tf_op jit(solution)/shard_map/ppermute | solution.py:25
  25.8 5.7 %collective-permute-start.5 = (f32[72,128]{1,0:T(8,128)S(1)}, f32[72,128]{1,0:T(8,128)S(1)}, u32[]{:S(2)}, u32[]{:S(2)}) collective-permute-start(f32[72,128]{1,0:T(8,128)S(1)} %add_add_fusion.1), channel_id=1, source_target_pairs={{0,4},{1,5},{2,6},{3,7},{4,0},{5,1},{6,2},{7,3},{8,12},{9,13},{10,... | collective-permute-start | bytes 110600 | tf_op jit(solution)/shard_map/ppermute | solution.py:25
  31.5 3.8 %collective-permute-start.10 = (f32[72,128]{1,0:T(8,128)S(1)}, f32[72,128]{1,0:T(8,128)S(1)}, u32[]{:S(2)}, u32[]{:S(2)}) collective-permute-start(f32[72,128]{1,0:T(8,128)S(1)} %add_add_fusion.refs_0_), channel_id=1, source_target_pairs={{0,3},{1,2},{2,1},{3,0},{4,7},{5,6},{6,5},{7,4},{8,11},{9,10},{10,... | collective-permute-start | bytes 110600 | tf_op jit(solution)/shard_map/ppermute | solution.py:25
  31.6 4.6 %collective-permute-start.9 = (f32[72,128]{1,0:T(8,128)S(1)}, f32[72,128]{1,0:T(8,128)S(1)}, u32[]{:S(2)}, u32[]{:S(2)}) collective-permute-start(f32[72,128]{1,0:T(8,128)S(1)} %add_add_fusion.refs_0_), channel_id=1, source_target_pairs={{0,2},{1,3},{2,0},{3,1},{4,6},{5,7},{6,4},{7,5},{8,10},{9,11},{10,... | collective-permute-start | bytes 110600 | tf_op jit(solution)/shard_map/ppermute | solution.py:25
  33.1 3.0 %collective-permute-start.8 = (f32[72,128]{1,0:T(8,128)S(1)}, f32[72,128]{1,0:T(8,128)S(1)}, u32[]{:S(2)}, u32[]{:S(2)}) collective-permute-start(f32[72,128]{1,0:T(8,128)S(1)} %add_add_fusion.refs_0_), channel_id=1, source_target_pairs={{0,1},{1,0},{2,3},{3,2},{4,5},{5,4},{6,7},{7,6},{8,9},{9,8},{10,11... | collective-permute-start | bytes 110600 | tf_op jit(solution)/shard_map/ppermute | solution.py:25

commit v6 on v5

--- a/solution.py
+++ b/solution.py
@@ -8,6 +8,7 @@
 from jax.sharding import PartitionSpec as P
 
 PANEL = 16
+HALF = 8
 LANES = 128
 SUBS = 8
 SPREAD = 4
@@ -190,25 +191,65 @@
 RIGHT = (0, 1, 2, 0, 1, 0)
 
 
-def eliminate_all(panel, t_ref, wide):
+def eliminate_all(panel, low, t_ref, wide):
     tiles, order, _ = t_ref.shape
     first = panel * PANEL
     tile = jnp.maximum(panel, 0) // (LANES // PANEL)
-    left = split_three(t_ref[tile])
+    left = split_three(t_ref[tile, low:, :])
     left = jnp.concatenate([left[k] for k in LEFT], axis=1)
     update = jnp.dot(left, wide[lax.rem(panel + 2, 2)], preferred_element_type=jnp.float32)
-    row = lax.broadcasted_iota(jnp.int32, (order, LANES), 0)
-    lane = lax.broadcasted_iota(jnp.int32, (order, LANES), 1)
+    row = lax.broadcasted_iota(jnp.int32, (order - low, LANES), 0) + low
+    lane = lax.broadcasted_iota(jnp.int32, (order - low, LANES), 1)
     below = row >= first + 2 * PANEL
     for s in range(tiles):
         column = lane + s * LANES
         mine = (column >= first) & (column < first + PANEL)
-        held = t_ref[s]
+        held = t_ref[s, low:, :]
         fresh = jnp.where(mine, 0.0, held) - update[:, s * LANES:(s + 1) * LANES]
-        t_ref[s] = jnp.where(below, fresh, held)
-
-
-def factor_panel(panel, t_ref, f_ref, x_ref, cols, rows, wide, narrow):
+        t_ref[s, low:, :] = jnp.where(below, fresh, held)
+
+
+def small_factor(entry, count):
+    unit = [[None] * count for _ in range(count)]
+    recip = []
+    for k in range(count):
+        recip.append(1.0 / entry[k][k])
+        for i in range(k + 1, count):
+            unit[i][k] = entry[i][k] * recip[k]
+        for j in range(k + 1, count):
+            for i in range(j, count):
+                if i == j:
+                    part = (entry[i][k] * entry[i][k]) * recip[k]
+                else:
+                    part = unit[i][k] * entry[j][k]
+                entry[i][j] = entry[i][j] - part
+    return unit, recip
+
+
+def pivots(cols):
+    def spread(j, i):
+        return jnp.broadcast_to(cols[j, i:i + 1, :], (SUBS, LANES))
+
+    upper, recip = small_factor([[spread(j, i) for j in range(i + 1)] for i in range(HALF)], HALF)
+    below = [cols[j, HALF:, :] for j in range(HALF)]
+    for k in range(HALF):
+        for j in range(k + 1, HALF):
+            below[j] = below[j] - below[k] * upper[j][k]
+    corner = [cols[j, HALF:, :] for j in range(HALF, PANEL)]
+    for k in range(HALF):
+        cols[k, HALF:, :] = below[k] * recip[k]
+    left = [[spread(k, HALF + i) for k in range(HALF)] for i in range(HALF)]
+    for j in range(HALF):
+        for k in range(HALF):
+            corner[j] = corner[j] - below[k] * left[j][k]
+        cols[HALF + j, HALF:, :] = corner[j]
+    entry = [[spread(HALF + j, HALF + i) for j in range(i + 1)] for i in range(HALF)]
+    lower, more = small_factor(entry, HALF)
+    unit = [row + [None] * HALF for row in upper] + [left[i] + lower[i] for i in range(HALF)]
+    return unit, recip + more
+
+
+def factor_panel(panel, low, t_ref, f_ref, x_ref, cols, rows, wide, narrow):
     tiles, order, _ = t_ref.shape
     first = pl.multiple_of(panel * PANEL, PANEL)
     tile = panel // (LANES // PANEL)
@@ -227,12 +268,8 @@
         unit_rows = jnp.where(column - first == sub, 1.0, 0.0)
         rows[pl.ds(s, PANEL, stride=SUBS), :] = jnp.where(inside, unit_rows, t_ref[s, here, :])
     rows[pl.ds(tiles, PANEL, stride=SUBS), :] = own
-    entry = [
-        [jnp.broadcast_to(cols[j, i:i + 1, :], (SUBS, LANES)) for j in range(i + 1)]
-        for i in range(PANEL)
-    ]
     y = [rows[i * SUBS:(i + 1) * SUBS, :] for i in range(PANEL)]
-    eliminate_all(panel - 1, t_ref, wide)
+    eliminate_all(panel - 1, low, t_ref, wide)
     after = jnp.minimum(first + PANEL, order - PANEL)
     after = pl.ds(pl.multiple_of(after, PANEL), PANEL)
     ahead = pltpu.roll(t_ref[tile, after, :], turn, axis=1)
@@ -242,19 +279,8 @@
         left = left + pltpu.roll(pieces[LEFT[k]], k * PANEL, axis=1)
     left = left.astype(jnp.bfloat16)
 
-    unit = [[None] * PANEL for _ in range(PANEL)]
-    recip = []
+    unit, recip = pivots(cols)
     for k in range(PANEL):
-        recip.append(1.0 / entry[k][k])
-        for i in range(k + 1, PANEL):
-            unit[i][k] = entry[i][k] * recip[k]
-        for j in range(k + 1, PANEL):
-            for i in range(j, PANEL):
-                if i == j:
-                    part = (entry[i][k] * entry[i][k]) * recip[k]
-                else:
-                    part = unit[i][k] * entry[j][k]
-                entry[i][j] = entry[i][j] - part
         for i in range(k + 1, PANEL):
             y[i] = y[i] - unit[i][k] * y[k]
     v = [recip[i] * y[i] for i in range(PANEL)]
@@ -297,17 +323,8 @@
 
 def factor_kernel(scale, *refs):
     chunk_refs, refs = refs[:SPREAD], refs[SPREAD:]
-    new_ref, old_ref, f_ref, out_ref, *refs = refs
-    packed, t_ref, x_ref, cols, rows, wide, narrow, x_pair, stack, *refs = refs
-    tall, staged, in_sem, out_sem = refs
+    f_ref, x_pair, packed, t_ref, x_ref, cols, rows, wide, narrow = refs
     tiles, order, _ = t_ref.shape
-    new_count = new_ref.shape[1]
-    load_new = pltpu.make_async_copy(new_ref, stack.at[:, pl.ds(0, new_count)], in_sem.at[0])
-    load_old = pltpu.make_async_copy(
-        old_ref, stack.at[:, pl.ds(new_count, order - new_count)], in_sem.at[1]
-    )
-    load_new.start()
-    load_old.start()
     share = lax.axis_index("blk") % SPREAD
     height = packed.shape[0] // SPREAD
     for flip in range(SPREAD):
@@ -329,14 +346,27 @@
     narrow[...] = jnp.zeros(narrow.shape, narrow.dtype)
     rows[...] = jnp.zeros(rows.shape, jnp.float32)
 
-    @pl.loop(0, order // PANEL)
-    def _(panel):
-        factor_panel(panel, t_ref, f_ref, x_ref, cols, rows, wide, narrow)
+    per_tile = LANES // PANEL
+    for low in range(0, order, LANES):
+        @pl.loop(low // PANEL, low // PANEL + per_tile)
+        def _(panel):
+            factor_panel(panel, low, t_ref, f_ref, x_ref, cols, rows, wide, narrow)
 
     inverse = x_ref[...]
     high = inverse.astype(jnp.bfloat16)
     low = (inverse - high.astype(jnp.float32)).astype(jnp.bfloat16)
     x_pair[...] = jnp.concatenate([high, low], axis=1)
+
+
+def modes_kernel(x_pair, new_ref, old_ref, out_ref, stack, tall, staged, in_sem, out_sem):
+    order = stack.shape[1]
+    new_count = new_ref.shape[1]
+    load_new = pltpu.make_async_copy(new_ref, stack.at[:, pl.ds(0, new_count)], in_sem.at[0])
+    load_old = pltpu.make_async_copy(
+        old_ref, stack.at[:, pl.ds(new_count, order - new_count)], in_sem.at[1]
+    )
+    load_new.start()
+    load_old.start()
     load_new.wait()
     load_old.wait()
     _, planes, rows_y, rows_z = out_ref.shape
@@ -371,20 +401,15 @@
             store(plane, step).wait()
 
 
-def factor_and_modes(chunks, s_new, s_old, shape, cell_total):
-    order, planes, rows_y, rows_z = shape
+def factor_and_inverse(chunks, order, cell_total):
     height = chunks[0].shape[0] * SPREAD
-    vmem = pl.BlockSpec(memory_space=pltpu.VMEM)
-    hbm = pl.BlockSpec(memory_space=pl.ANY)
     square = (order, order)
     return pl.pallas_call(
         functools.partial(factor_kernel, 1.0 / cell_total),
         out_shape=[
             jax.ShapeDtypeStruct(square, jnp.float32),
-            jax.ShapeDtypeStruct(shape, jnp.bfloat16),
+            jax.ShapeDtypeStruct((order, 2 * order), jnp.bfloat16),
         ],
-        in_specs=[vmem] * SPREAD + [hbm, hbm],
-        out_specs=[vmem, hbm],
         scratch_shapes=[
             pltpu.VMEM((height, LANES), jnp.float32),
             pltpu.VMEM((order // LANES, order, LANES), jnp.float32),
@@ -393,7 +418,22 @@
             pltpu.VMEM((PANEL * SUBS, LANES), jnp.float32),
             pltpu.VMEM((2, len(LEFT) * LANES, order), jnp.bfloat16),
             pltpu.VMEM((LANES, order), jnp.bfloat16),
-            pltpu.VMEM((order, 2 * order), jnp.bfloat16),
+        ],
+        compiler_params=pltpu.CompilerParams(vmem_limit_bytes=VMEM_BYTES),
+        name="factor",
+    )(*chunks)
+
+
+def modes_product(x_pair, s_new, s_old, shape):
+    order, planes, rows_y, rows_z = shape
+    vmem = pl.BlockSpec(memory_space=pltpu.VMEM)
+    hbm = pl.BlockSpec(memory_space=pl.ANY)
+    return pl.pallas_call(
+        modes_kernel,
+        out_shape=jax.ShapeDtypeStruct(shape, jnp.bfloat16),
+        in_specs=[vmem, hbm, hbm],
+        out_specs=hbm,
+        scratch_shapes=[
             pltpu.VMEM((planes * rows_y // 2, order, 2 * rows_z), jnp.bfloat16),
             pltpu.VMEM((2, order * rows_y, rows_z), jnp.float32),
             pltpu.VMEM((planes, order, rows_y, rows_z), jnp.bfloat16),
@@ -401,8 +441,8 @@
             pltpu.SemaphoreType.DMA((planes, rows_y // 2)),
         ],
         compiler_params=pltpu.CompilerParams(vmem_limit_bytes=VMEM_BYTES),
-        name="factor",
-    )(*chunks, s_new, s_old)
+        name="modes",
+    )(x_pair, s_new, s_old)
 
 
 def shards(snapshots, old_modes, mode_scales, plane_counts, links):
@@ -420,9 +460,8 @@
         snapshots, before, after, plane_counts, links, s_old, old_gram
     )
     sums = sum_chunks(chunks, "blk")
-    factor, modes = factor_and_modes(
-        sums, s_new, s_old, (order, planes, rows_y, rows_z), peers * planes * rows_y * rows_z
-    )
+    factor, x_pair = factor_and_inverse(sums, order, peers * planes * rows_y * rows_z)
+    modes = modes_product(x_pair, s_new, s_old, (order, planes, rows_y, rows_z))
     return (modes, factor)
 
 

time: 55.3 us -> 52.3 us (0.946)
  Pallas kernels: 25.4 us -> 22.4 us
    pallas_call x1 -> x2, Pallas kernels: 18.9 us -> 16 us  [the longest x1 10.5 us: factor_and_inverse(): pl.pallas_call(functools.partial(factor_kernel, 1.0 / cell_total), out_sh...]
where the time goes in v6:
time: 52.3 us; the launch traced here: 52.1 us
  Pallas kernels  22.4 us (43%)
  starting transfers between devices  13.8 us (26%)
  waiting for transfers between devices  11.3 us (22%)
  local copies, waits for them, and re-layouts  3.17 us (6%)
  between operations  1.42 us (3%)
    pallas_call x1, Pallas kernels, factor_and_inverse(): pl.pallas_call(functools.partial(factor_kernel, 1.0 / cell_total), out_sh...  10.5 us
    ppermute x9, starting transfers between devices, swap(): return lax.ppermute(x, axis, [(i, i ^ flip) for i in range(peers)])  8.3 us
    ppermute x9, waiting for transfers between devices, swap(): return lax.ppermute(x, axis, [(i, i ^ flip) for i in range(peers)])  7.61 us
    pallas_call x1, Pallas kernels, modes_product(): pl.pallas_call(modes_kernel, out_shape=jax.ShapeDtypeStruct(shape, jnp.bf...  5.54 us
    ppermute x1, starting transfers between devices, shards(): after = lax.ppermute(first, 'blk', down)  5.47 us
    pallas_call x1, Pallas kernels, filtered_rows(): pl.pallas_call(filter_kernel, out_shape=[jax.ShapeDtypeStruct((planes * r...  3.75 us
    ppermute x1, waiting for transfers between devices, shards(): before = lax.ppermute(last, 'blk', up)  3.7 us
    pallas_call x1, Pallas kernels, scaled_rows(): pl.pallas_call(scale_kernel, out_shape=[jax.ShapeDtypeStruct((planes * ro...  2.68 us
  transfers between devices with their start and end apart: 11, of which 6 were waited for; matrix products, arithmetic and copies ran while one was open for 0% of the time, Pallas kernels for 5%

profile of v6, /device:TPU:0, one launch (start us, length us, event | category | flops | bytes accessed | tf_op | source)
XLA Modules:
  0.0 52.1 jit_solution(17442953911597442342)
XLA Ops:
  0.6 0.0 copy-start
  0.6 0.0 copy-start.3
  1.4 1.1 %fusion = (bf16[64,1,16,128]{3,2,1,0:T(8,128)(2,1)S(1)}, bf16[64,1,16,128]{3,2,1,0:T(8,128)(2,1)S(1)}) fusion(bf16[64,2,16,128]{3,2,1,0:T(8,128)(2,1)} %snap_ref.1, s32[]{:T(128)S(6)} %select_n.3), kind=kLoop, calls=%fused_computation.3 | loop fusion | bytes 1048580 | tf_op jit(solution)/shard_map/slice | solution.py:454
  2.4 5.5 %collective-permute-start.1 = (bf16[64,1,16,128]{3,2,1,0:T(8,128)(2,1)S(1)}, bf16[64,1,16,128]{3,2,1,0:T(8,128)(2,1)S(1)}, u32[]{:S(2)}, u32[]{:S(2)}) collective-permute-start(bf16[64,1,16,128]{3,2,1,0:T(8,128)(2,1)S(1)} %get-tuple-element.20), channel_id=1, source_target_pairs={{1,0},{2,1},{3,2},{4,3},{5,4},{6,5},{7,6},{8,7},{9,8},{10,9},{11,1... | collective-permute-start | bytes 786440 | tf_op jit(solution)/shard_map/ppermute | solution.py:456
  7.9 0.0 collective-permute-start
  7.9 0.0 copy-start.1
  7.9 1.4 %copy-done.1 = bf16[192,2,16,128]{3,2,1,0:T(8,128)(2,1)S(1)} copy-done((bf16[192,2,16,128]{3,2,1,0:T(8,128)(2,1)S(1)}, bf16[192,2,16,128]{3,2,1,0:T(8,128)(2,1)}, u32[]{:S(2)}) %copy-start.1) | copy-done | bytes 1572888
  9.3 0.0 copy-start.2
  9.3 0.7 %copy-done.2 = f32[192]{0:T(256)S(1)} copy-done((f32[192]{0:T(256)S(1)}, f32[192]{0:T(256)}, u32[]{:S(2)}) %copy-start.2) | copy-done | bytes 792
  10.0 2.7 %scale_gram.1 = (bf16[16,192,256]{2,1,0:T(8,128)(2,1)S(1)}, f32[192,192]{1,0:T(8,128)S(1)}) custom-call(f32[192]{0:T(256)S(1)} %copy-done.2, s32[1]{0:T(128)S(6)} %copy.7.count_ref, bf16[192,2,16,128]{3,2,1,0:T(8,128)(2,1)S(1)} %copy-done.1), custom_call_target="tpu_custom_call" | custom-call | flops 301989888 | bytes 6291456 | tf_op jit(solution)/shard_map/scale_gram/pallas_call | solution.py:57
  12.7 0.0 collective-permute-done.1.after_ref
  12.7 3.7 %collective-permute-done.before_ref = bf16[64,1,16,128]{3,2,1,0:T(8,128)(2,1)S(1)} collective-permute-done((bf16[64,1,16,128]{3,2,1,0:T(8,128)(2,1)S(1)}, bf16[64,1,16,128]{3,2,1,0:T(8,128)(2,1)S(1)}, u32[]{:S(2)}, u32[]{:S(2)}) %collective-permute-start) | collective-permute-done | bytes 262176 | tf_op jit(solution)/shard_map/ppermute | solution.py:457
  16.4 0.0 copy-done
  16.4 0.0 copy-done.3
  16.4 3.8 %filter_gram.1 = (bf16[16,64,256]{2,1,0:T(8,128)(2,1)S(1)}, f32[72,128]{1,0:T(8,128)S(1)}, f32[72,128]{1,0:T(8,128)S(1)}, f32[72,128]{1,0:T(8,128)S(1)}, f32[72,128]{1,0:T(8,128)S(1)}) custom-call(s32[1]{0:T(128)S(6)} %copy.7.count_ref, s32[1,2]{1,0:T(1,128)S(1)} %copy-done.3, bf16[64,2,16,128]{3,2,1,0:T(8,128)(2,1)S(1)} %copy-done, ...), custom_call_target="tpu_custom_call" | custom-call | flops 134217728 | bytes 2097152 | tf_op jit(solution)/shard_map/filter_gram/pallas_call | solution.py:149
  20.2 0.1 collective-permute-start.2
  20.2 0.1 collective-permute-start.3
  20.3 1.8 %collective-permute-start.4 = (f32[72,128]{1,0:T(8,128)S(1)}, f32[72,128]{1,0:T(8,128)S(1)}, u32[]{:S(2)}, u32[]{:S(2)}) collective-permute-start(f32[72,128]{1,0:T(8,128)S(1)} %get-tuple-element.16), channel_id=1, source_target_pairs={{0,3},{1,2},{2,1},{3,0},{4,7},{5,6},{6,5},{7,4},{8,11},{9,10},{10,... | collective-permute-start | bytes 110600 | tf_op jit(solution)/shard_map/ppermute | solution.py:26
  22.1 0.0 collective-permute-done.2
  22.1 2.4 %collective-permute-done.3 = f32[72,128]{1,0:T(8,128)S(1)} collective-permute-done((f32[72,128]{1,0:T(8,128)S(1)}, f32[72,128]{1,0:T(8,128)S(1)}, u32[]{:S(2)}, u32[]{:S(2)}) %collective-permute-start.3) | collective-permute-done | bytes 36896 | tf_op jit(solution)/shard_map/ppermute | solution.py:26
  24.5 0.0 collective-permute-done.4
  24.5 1.2 %collective-permute-start.7 = (f32[72,128]{1,0:T(8,128)S(1)}, f32[72,128]{1,0:T(8,128)S(1)}, u32[]{:S(2)}, u32[]{:S(2)}) collective-permute-start(f32[72,128]{1,0:T(8,128)S(1)} %add_add_fusion.1), channel_id=1, source_target_pairs={{0,12},{1,13},{2,14},{3,15},{4,8},{5,9},{6,10},{7,11},{8,4},{9,5},... | collective-permute-start | bytes 110600 | tf_op jit(solution)/shard_map/ppermute | solution.py:26
  25.8 0.0 collective-permute-start.6
  25.8 3.2 %collective-permute-start.5 = (f32[72,128]{1,0:T(8,128)S(1)}, f32[72,128]{1,0:T(8,128)S(1)}, u32[]{:S(2)}, u32[]{:S(2)}) collective-permute-start(f32[72,128]{1,0:T(8,128)S(1)} %add_add_fusion.1), channel_id=1, source_target_pairs={{0,4},{1,5},{2,6},{3,7},{4,0},{5,1},{6,2},{7,3},{8,12},{9,13},{10,... | collective-permute-start | bytes 110600 | tf_op jit(solution)/shard_map/ppermute | solution.py:26
  29.0 1.6 %collective-permute-done.7 = f32[72,128]{1,0:T(8,128)S(1)} collective-permute-done((f32[72,128]{1,0:T(8,128)S(1)}, f32[72,128]{1,0:T(8,128)S(1)}, u32[]{:S(2)}, u32[]{:S(2)}) %collective-permute-start.7) | collective-permute-done | bytes 36896 | tf_op jit(solution)/shard_map/ppermute | solution.py:26
  30.6 0.9 %collective-permute-done.6 = f32[72,128]{1,0:T(8,128)S(1)} collective-permute-done((f32[72,128]{1,0:T(8,128)S(1)}, f32[72,128]{1,0:T(8,128)S(1)}, u32[]{:S(2)}, u32[]{:S(2)}) %collective-permute-start.6) | collective-permute-done | bytes 36896 | tf_op jit(solution)/shard_map/ppermute | solution.py:26
  31.5 0.0 collective-permute-done.5
  31.5 0.1 collective-permute-start.10
  31.6 1.5 %collective-permute-start.9 = (f32[72,128]{1,0:T(8,128)S(1)}, f32[72,128]{1,0:T(8,128)S(1)}, u32[]{:S(2)}, u32[]{:S(2)}) collective-permute-start(f32[72,128]{1,0:T(8,128)S(1)} %add_add_fusion.refs_0_), channel_id=1, source_target_pairs={{0,2},{1,3},{2,0},{3,1},{4,6},{5,7},{6,4},{7,5},{8,10},{9,11},{10,... | collective-permute-start | bytes 110600 | tf_op jit(solution)/shard_map/ppermute | solution.py:26
  33.1 0.3 collective-permute-start.8
  33.4 1.8 %collective-permute-done.10.refs_3_ = f32[72,128]{1,0:T(8,128)S(1)} collective-permute-done((f32[72,128]{1,0:T(8,128)S(1)}, f32[72,128]{1,0:T(8,128)S(1)}, u32[]{:S(2)}, u32[]{:S(2)}) %collective-permute-start.10) | collective-permute-done | bytes 36896 | tf_op jit(solution)/shard_map/ppermute | solution.py:26
  35.3 0.9 %collective-permute-done.9.refs_2_ = f32[72,128]{1,0:T(8,128)S(1)} collective-permute-done((f32[72,128]{1,0:T(8,128)S(1)}, f32[72,128]{1,0:T(8,128)S(1)}, u32[]{:S(2)}, u32[]{:S(2)}) %collective-permute-start.9) | collective-permute-done | bytes 36896 | tf_op jit(solution)/shard_map/ppermute | solution.py:26
  36.1 0.0 collective-permute-done.8.refs_1_
  36.1 10.5 %factor.1 = (f32[256,256]{1,0:T(8,128)}, bf16[256,512]{1,0:T(8,128)(2,1)S(1)}) custom-call(f32[72,128]{1,0:T(8,128)S(1)} %add_add_fusion.refs_0_, f32[72,128]{1,0:T(8,128)S(1)} %collective-permute-done.8.refs_1_, f32[72,128]{1,0:T(8,128)S(1)} %collective-permute-done.9.refs_2_, f32[72,128]{1,0:T(8,128)S(1)} %collective-permute-done.10.refs_3_), custom_call_target="tpu_custom_call" | custom-call | tf_op jit(solution)/shard_map/factor/pallas_call | solution.py:407
  46.6 5.5 %modes.1 = bf16[256,2,16,128]{3,2,1,0:T(8,128)(2,1)} custom-call(bf16[256,512]{1,0:T(8,128)(2,1)S(1)} %get-tuple-element.17.x_pair, bf16[16,64,256]{2,1,0:T(8,128)(2,1)S(1)} %get-tuple-element.18.new_ref, bf16[16,192,256]{2,1,0:T(8,128)(2,1)S(1)} %get-tuple-element.11.old_ref), custom_call_target="tpu_custom_call" | custom-call | tf_op jit(solution)/shard_map/modes/pallas_call | solution.py:431
  (2 shorter events, 0.0 us)
Async XLA Ops:
  0.6 15.8 %copy-start = (bf16[64,2,16,128]{3,2,1,0:T(8,128)(2,1)S(1)}, bf16[64,2,16,128]{3,2,1,0:T(8,128)(2,1)}, u32[]{:S(2)}) copy-start(bf16[64,2,16,128]{3,2,1,0:T(8,128)(2,1)} %snap_ref.1) | copy-start | bytes 1572868
  0.6 15.8 %copy-start.3 = (s32[1,2]{1,0:T(1,128)S(1)}, s32[1,2]{1,0:T(1,128)}, u32[]{:S(2)}) copy-start(s32[1,2]{1,0:T(1,128)} %links_ref.1) | copy-start | bytes 28
  2.4 10.3 %collective-permute-start.1 = (bf16[64,1,16,128]{3,2,1,0:T(8,128)(2,1)S(1)}, bf16[64,1,16,128]{3,2,1,0:T(8,128)(2,1)S(1)}, u32[]{:S(2)}, u32[]{:S(2)}) collective-permute-start(bf16[64,1,16,128]{3,2,1,0:T(8,128)(2,1)S(1)} %get-tuple-element.20), channel_id=1, source_target_pairs={{1,0},{2,1},{3,2},{4,3},{5,4},{6,5},{7,6},{8,7},{9,8},{10,9},{11,1... | collective-permute-start | bytes 786440 | tf_op jit(solution)/shard_map/ppermute | solution.py:456
  7.9 8.5 %collective-permute-start = (bf16[64,1,16,128]{3,2,1,0:T(8,128)(2,1)S(1)}, bf16[64,1,16,128]{3,2,1,0:T(8,128)(2,1)S(1)}, u32[]{:S(2)}, u32[]{:S(2)}) collective-permute-start(bf16[64,1,16,128]{3,2,1,0:T(8,128)(2,1)S(1)} %get-tuple-element.21), channel_id=1, source_target_pairs={{0,1},{1,2},{2,3},{3,4},{4,5},{5,6},{6,7},{7,8},{8,9},{9,10},{10,1... | collective-permute-start | bytes 786440 | tf_op jit(solution)/shard_map/ppermute | solution.py:457
  7.9 1.4 %copy-start.1 = (bf16[192,2,16,128]{3,2,1,0:T(8,128)(2,1)S(1)}, bf16[192,2,16,128]{3,2,1,0:T(8,128)(2,1)}, u32[]{:S(2)}) copy-start(bf16[192,2,16,128]{3,2,1,0:T(8,128)(2,1)} %old_ref.1) | copy-start | bytes 4718596
  9.3 0.7 %copy-start.2 = (f32[192]{0:T(256)S(1)}, f32[192]{0:T(256)}, u32[]{:S(2)}) copy-start(f32[192]{0:T(256)} %scales_ref.1) | copy-start | bytes 2308
  20.2 1.9 %collective-permute-start.2 = (f32[72,128]{1,0:T(8,128)S(1)}, f32[72,128]{1,0:T(8,128)S(1)}, u32[]{:S(2)}, u32[]{:S(2)}) collective-permute-start(f32[72,128]{1,0:T(8,128)S(1)} %get-tuple-element.14), channel_id=1, source_target_pairs={{0,1},{1,0},{2,3},{3,2},{4,5},{5,4},{6,7},{7,6},{8,9},{9,8},{10,11... | collective-permute-start | bytes 110600 | tf_op jit(solution)/shard_map/ppermute | solution.py:26
  20.2 4.3 %collective-permute-start.3 = (f32[72,128]{1,0:T(8,128)S(1)}, f32[72,128]{1,0:T(8,128)S(1)}, u32[]{:S(2)}, u32[]{:S(2)}) collective-permute-start(f32[72,128]{1,0:T(8,128)S(1)} %get-tuple-element.15), channel_id=1, source_target_pairs={{0,2},{1,3},{2,0},{3,1},{4,6},{5,7},{6,4},{7,5},{8,10},{9,11},{10,... | collective-permute-start | bytes 110600 | tf_op jit(solution)/shard_map/ppermute | solution.py:26
  20.3 4.2 %collective-permute-start.4 = (f32[72,128]{1,0:T(8,128)S(1)}, f32[72,128]{1,0:T(8,128)S(1)}, u32[]{:S(2)}, u32[]{:S(2)}) collective-permute-start(f32[72,128]{1,0:T(8,128)S(1)} %get-tuple-element.16), channel_id=1, source_target_pairs={{0,3},{1,2},{2,1},{3,0},{4,7},{5,6},{6,5},{7,4},{8,11},{9,10},{10,... | collective-permute-start | bytes 110600 | tf_op jit(solution)/shard_map/ppermute | solution.py:26
  24.5 6.1 %collective-permute-start.7 = (f32[72,128]{1,0:T(8,128)S(1)}, f32[72,128]{1,0:T(8,128)S(1)}, u32[]{:S(2)}, u32[]{:S(2)}) collective-permute-start(f32[72,128]{1,0:T(8,128)S(1)} %add_add_fusion.1), channel_id=1, source_target_pairs={{0,12},{1,13},{2,14},{3,15},{4,8},{5,9},{6,10},{7,11},{8,4},{9,5},... | collective-permute-start | bytes 110600 | tf_op jit(solution)/shard_map/ppermute | solution.py:26
  25.8 5.7 %collective-permute-start.6 = (f32[72,128]{1,0:T(8,128)S(1)}, f32[72,128]{1,0:T(8,128)S(1)}, u32[]{:S(2)}, u32[]{:S(2)}) collective-permute-start(f32[72,128]{1,0:T(8,128)S(1)} %add_add_fusion.1), channel_id=1, source_target_pairs={{0,8},{1,9},{2,10},{3,11},{4,12},{5,13},{6,14},{7,15},{8,0},{9,1},... | collective-permute-start | bytes 110600 | tf_op jit(solution)/shard_map/ppermute | solution.py:26
  25.8 5.7 %collective-permute-start.5 = (f32[72,128]{1,0:T(8,128)S(1)}, f32[72,128]{1,0:T(8,128)S(1)}, u32[]{:S(2)}, u32[]{:S(2)}) collective-permute-start(f32[72,128]{1,0:T(8,128)S(1)} %add_add_fusion.1), channel_id=1, source_target_pairs={{0,4},{1,5},{2,6},{3,7},{4,0},{5,1},{6,2},{7,3},{8,12},{9,13},{10,... | collective-permute-start | bytes 110600 | tf_op jit(solution)/shard_map/ppermute | solution.py:26
  31.5 3.8 %collective-permute-start.10 = (f32[72,128]{1,0:T(8,128)S(1)}, f32[72,128]{1,0:T(8,128)S(1)}, u32[]{:S(2)}, u32[]{:S(2)}) collective-permute-start(f32[72,128]{1,0:T(8,128)S(1)} %add_add_fusion.refs_0_), channel_id=1, source_target_pairs={{0,3},{1,2},{2,1},{3,0},{4,7},{5,6},{6,5},{7,4},{8,11},{9,10},{10,... | collective-permute-start | bytes 110600 | tf_op jit(solution)/shard_map/ppermute | solution.py:26
  31.6 4.6 %collective-permute-start.9 = (f32[72,128]{1,0:T(8,128)S(1)}, f32[72,128]{1,0:T(8,128)S(1)}, u32[]{:S(2)}, u32[]{:S(2)}) collective-permute-start(f32[72,128]{1,0:T(8,128)S(1)} %add_add_fusion.refs_0_), channel_id=1, source_target_pairs={{0,2},{1,3},{2,0},{3,1},{4,6},{5,7},{6,4},{7,5},{8,10},{9,11},{10,... | collective-permute-start | bytes 110600 | tf_op jit(solution)/shard_map/ppermute | solution.py:26
  33.1 3.0 %collective-permute-start.8 = (f32[72,128]{1,0:T(8,128)S(1)}, f32[72,128]{1,0:T(8,128)S(1)}, u32[]{:S(2)}, u32[]{:S(2)}) collective-permute-start(f32[72,128]{1,0:T(8,128)S(1)} %add_add_fusion.refs_0_), channel_id=1, source_target_pairs={{0,1},{1,0},{2,3},{3,2},{4,5},{5,4},{6,7},{7,6},{8,9},{9,8},{10,11... | collective-permute-start | bytes 110600 | tf_op jit(solution)/shard_map/ppermute | solution.py:26

commit v7 on v6

--- a/solution.py
+++ b/solution.py
@@ -26,26 +26,45 @@
     return lax.ppermute(x, axis, [(i, i ^ flip) for i in range(peers)])
 
 
-def relay(tall, s_ref, plane, rows_y):
-    rows = s_ref.shape[1]
-    for y in range(rows_y):
-        part = tall[pl.ds(y, rows, stride=rows_y), :].astype(jnp.bfloat16)
-        half = (y % 2) * LANES
-        s_ref[(plane * rows_y + y) // 2, :, half:half + LANES] = part
-
-
-def scale_kernel(scales_ref, count_ref, old_ref, s_ref, gram_ref, tall):
-    rows, planes, rows_y, _ = old_ref.shape
-    for plane in range(planes):
-        alive = jnp.where(plane < count_ref[0], 1.0, 0.0)
-
-        @pl.loop(0, rows, unroll=8)
-        def _(row):
-            weight = scales_ref[row]
-            at = pl.multiple_of(row * rows_y, rows_y)
-            tall[pl.ds(at, rows_y), :] = old_ref[row, plane].astype(jnp.float32) * weight * alive
-
-        relay(tall, s_ref, plane, rows_y)
+def turn_matrix(size, near):
+    order = size * size
+    row = lax.broadcasted_iota(jnp.int32, (order, order), 0)
+    col = lax.broadcasted_iota(jnp.int32, (order, order), 1)
+    same = row % size == col // size
+    step = row // size - col % size
+    weight = jnp.where(step == 0, 0.5 if near else 1.0, 0.0)
+    if near:
+        weight = jnp.where((step == 1) | (step == -1), near, weight)
+    return jnp.where(same, weight, 0.0).astype(jnp.bfloat16)
+
+
+def place(turned, s_ref, rows_y, at):
+    for plane in range(turned.shape[1] // LANES):
+        for y in range(rows_y):
+            part = turned[y * rows_y:(y + 1) * rows_y, plane * LANES:(plane + 1) * LANES]
+            half = (y % 2) * LANES
+            s_ref[(plane * rows_y + y) // 2, at, half:half + LANES] = part
+
+
+def scale_kernel(count_ref, scales_ref, old_ref, s_ref, gram_ref):
+    rows, planes, rows_y, rows_z = old_ref.shape
+    turn = turn_matrix(rows_y, 0.0)
+    plane = lax.broadcasted_iota(jnp.int32, (rows_y, planes * rows_z), 1) // rows_z
+    alive = jnp.where(plane < count_ref[0], 1.0, 0.0)
+
+    @pl.loop(0, rows // rows_y)
+    def _(group):
+        at = pl.ds(pl.multiple_of(group * rows_y, rows_y), rows_y)
+        block = old_ref[at]
+        block = jnp.concatenate(
+            [block[:, p].reshape(rows_y * rows_y, rows_z) for p in range(planes)], axis=1
+        )
+        turned = jnp.dot(turn, block, preferred_element_type=jnp.float32)
+        weight = scales_ref[at, :] * alive
+        turned = turned.reshape(rows_y, rows_y, planes * rows_z) * weight[None]
+        turned = turned.reshape(rows_y * rows_y, planes * rows_z).astype(jnp.bfloat16)
+        place(turned, s_ref, rows_y, at)
+
     gram_ref[...] = sum(nt_dot(s_ref[k], s_ref[k]) for k in range(s_ref.shape[0]))
 
 
@@ -60,21 +79,14 @@
             jax.ShapeDtypeStruct((planes * rows_y // 2, rows, 2 * rows_z), jnp.bfloat16),
             jax.ShapeDtypeStruct((rows, rows), jnp.float32),
         ],
-        in_specs=[smem, smem, vmem],
+        in_specs=[smem, vmem, vmem],
         out_specs=[vmem, vmem],
-        scratch_shapes=[pltpu.VMEM((rows * rows_y, rows_z), jnp.float32)],
         compiler_params=pltpu.CompilerParams(vmem_limit_bytes=VMEM_BYTES),
         cost_estimate=pl.CostEstimate(
             flops=2 * rows * rows * cells, bytes_accessed=8 * rows * cells, transcendentals=0
         ),
         name="scale_gram",
-    )(mode_scales, plane_counts, old_modes)
-
-
-def smooth(field, axis, place, length):
-    lower = jnp.where(place == 0, 0.0, pltpu.roll(field, 1, axis=axis))
-    upper = jnp.where(place == length - 1, 0.0, pltpu.roll(field, length - 1, axis=axis))
-    return 0.25 * lower + 0.5 * field + 0.25 * upper
+    )(plane_counts, mode_scales.reshape(rows, 1), old_modes)
 
 
 def packed_rows(order):
@@ -85,33 +97,47 @@
 def filter_kernel(
     count_ref, links_ref, snap_ref, before_ref, after_ref, old_ref, oldgram_ref, s_ref, *rest
 ):
-    chunk_refs, (tall, packed) = rest[:SPREAD], rest[SPREAD:]
+    chunk_refs, packed = rest[:SPREAD], rest[SPREAD]
     rows, planes, rows_y, rows_z = snap_ref.shape
     count = count_ref[0]
     join_low = links_ref[0, 0].astype(jnp.float32)
     join_high = links_ref[0, 1].astype(jnp.float32)
-    place_y = lax.broadcasted_iota(jnp.int32, (rows_y, rows_z), 0)
-    place_z = lax.broadcasted_iota(jnp.int32, (rows_y, rows_z), 1)
-    for plane in range(planes):
-        alive = jnp.where(plane < count, 1.0, 0.0)
-        is_last = plane == count - 1
-
-        @pl.loop(0, rows, unroll=8)
-        def _(row):
-            own = snap_ref[row, plane].astype(jnp.float32)
-            if plane == 0:
-                behind = before_ref[row, 0].astype(jnp.float32) * join_low
-            else:
-                behind = snap_ref[row, plane - 1].astype(jnp.float32)
-            forward = after_ref[row, 0].astype(jnp.float32) * join_high
-            if plane < planes - 1:
-                forward = jnp.where(is_last, forward, snap_ref[row, plane + 1].astype(jnp.float32))
-            field = 0.25 * behind + 0.5 * own + 0.25 * forward
-            field = smooth(smooth(field, 0, place_y, rows_y), 1, place_z, rows_z) * alive
-            at = pl.multiple_of(row * rows_y, rows_y)
-            tall[pl.ds(at, rows_y), :] = field
-
-        relay(tall, s_ref, plane, rows_y)
+    z_from = lax.broadcasted_iota(jnp.int32, (rows_z, rows_z), 0)
+    z_to = lax.broadcasted_iota(jnp.int32, (rows_z, rows_z), 1)
+    gap = jnp.abs(z_from - z_to)
+    smooth_z = jnp.where(gap == 0, 0.5, jnp.where(gap == 1, 0.25, 0.0))
+    nothing = jnp.zeros((rows_z, rows_z), jnp.bfloat16)
+    blocks = [[nothing] * planes for _ in range(planes + 2)]
+    for p in range(planes):
+        alive = jnp.where(p < count, 1.0, 0.0)
+        is_last = jnp.where(p == count - 1, 1.0, 0.0)
+        behind = alive * join_low if p == 0 else alive
+        blocks[p][p] = (smooth_z * (0.25 * behind)).astype(jnp.bfloat16)
+        blocks[p + 1][p] = (smooth_z * (0.5 * alive)).astype(jnp.bfloat16)
+        if p < planes - 1:
+            inner = 0.25 * alive * (1.0 - is_last)
+            blocks[p + 2][p] = (smooth_z * inner).astype(jnp.bfloat16)
+            blocks[planes + 1][p] = (smooth_z * (0.25 * is_last * join_high)).astype(jnp.bfloat16)
+        else:
+            blocks[planes + 1][p] = (smooth_z * (0.25 * alive * join_high)).astype(jnp.bfloat16)
+    weights = jnp.concatenate([jnp.concatenate(line, axis=1) for line in blocks], axis=0)
+    turn = turn_matrix(rows_y, 0.25)
+
+    @pl.loop(0, rows // rows_y)
+    def _(group):
+        at = pl.ds(pl.multiple_of(group * rows_y, rows_y), rows_y)
+        snap = snap_ref[at]
+        sources = [before_ref[at][:, 0]] + [snap[:, p] for p in range(planes)] + [after_ref[at][:, 0]]
+        sources = [x.reshape(rows_y * rows_y, rows_z) for x in sources]
+        field = jnp.dot(
+            jnp.concatenate(sources, axis=1), weights, preferred_element_type=jnp.float32
+        )
+        high = field.astype(jnp.bfloat16)
+        low = (field - high.astype(jnp.float32)).astype(jnp.bfloat16)
+        turned = jnp.dot(turn, high, preferred_element_type=jnp.float32)
+        turned = turned + jnp.dot(turn, low, preferred_element_type=jnp.float32)
+        place(turned.astype(jnp.bfloat16), s_ref, rows_y, at)
+
     pairs = range(s_ref.shape[0])
     new_new = sum(nt_dot(s_ref[k], s_ref[k]) for k in pairs)
     new_old = sum(nt_dot(s_ref[k], old_ref[k]) for k in pairs)
@@ -151,10 +177,7 @@
         out_shape=[jax.ShapeDtypeStruct((planes * rows_y // 2, rows, 2 * rows_z), jnp.bfloat16)] + [chunk] * SPREAD,
         in_specs=[smem, smem] + [vmem] * 5,
         out_specs=[vmem] * (1 + SPREAD),
-        scratch_shapes=[
-            pltpu.VMEM((rows * rows_y, rows_z), jnp.float32),
-            pltpu.VMEM((height, LANES), jnp.float32),
-        ],
+        scratch_shapes=[pltpu.VMEM((height, LANES), jnp.float32)],
         compiler_params=pltpu.CompilerParams(vmem_limit_bytes=VMEM_BYTES),
         cost_estimate=pl.CostEstimate(
             flops=2 * rows * order * cells, bytes_accessed=2 * order * cells, transcendentals=0
@@ -323,8 +346,16 @@
 
 def factor_kernel(scale, *refs):
     chunk_refs, refs = refs[:SPREAD], refs[SPREAD:]
-    f_ref, x_pair, packed, t_ref, x_ref, cols, rows, wide, narrow = refs
+    new_ref, old_ref, f_ref, out_ref, packed, t_ref, x_ref, cols, rows, *refs = refs
+    wide, narrow, x_pair, stack, mixed, staged, in_sem, out_sem = refs
     tiles, order, _ = t_ref.shape
+    new_count = new_ref.shape[1]
+    load_new = pltpu.make_async_copy(new_ref, stack.at[:, pl.ds(0, new_count)], in_sem.at[0])
+    load_old = pltpu.make_async_copy(
+        old_ref, stack.at[:, pl.ds(new_count, order - new_count)], in_sem.at[1]
+    )
+    load_new.start()
+    load_old.start()
     share = lax.axis_index("blk") % SPREAD
     height = packed.shape[0] // SPREAD
     for flip in range(SPREAD):
@@ -355,61 +386,61 @@
     inverse = x_ref[...]
     high = inverse.astype(jnp.bfloat16)
     low = (inverse - high.astype(jnp.float32)).astype(jnp.bfloat16)
-    x_pair[...] = jnp.concatenate([high, low], axis=1)
-
-
-def modes_kernel(x_pair, new_ref, old_ref, out_ref, stack, tall, staged, in_sem, out_sem):
-    order = stack.shape[1]
-    new_count = new_ref.shape[1]
-    load_new = pltpu.make_async_copy(new_ref, stack.at[:, pl.ds(0, new_count)], in_sem.at[0])
-    load_old = pltpu.make_async_copy(
-        old_ref, stack.at[:, pl.ds(new_count, order - new_count)], in_sem.at[1]
-    )
-    load_new.start()
-    load_old.start()
+    x_pair[0] = high
+    x_pair[1] = low
     load_new.wait()
     load_old.wait()
     _, planes, rows_y, rows_z = out_ref.shape
     steps = rows_y // 2
-    count = order // steps
-
-    def store(plane, step):
-        some = pl.ds(step * count, count)
-        return pltpu.make_async_copy(
-            staged.at[plane, some], out_ref.at[some, plane], out_sem.at[plane, step]
-        )
-
-    for plane in range(planes + 1):
-        @pl.loop(0, steps)
+    for plane in range(planes):
+        @pl.loop(0, steps, unroll=2)
         def _(step):
-            if plane < planes:
-                block = stack[plane * steps + step]
-                sums = jnp.dot(x_pair[:, :order], block, preferred_element_type=jnp.float32)
-                sums = sums + jnp.dot(x_pair[:, order:], block, preferred_element_type=jnp.float32)
-                for y in (0, 1):
-                    part = sums[:, y * rows_z:(y + 1) * rows_z]
-                    tall[plane % 2, pl.ds(2 * step + y, order, stride=rows_y), :] = part
-            if plane > 0:
-                at = pl.multiple_of(step * count * rows_y, count * rows_y)
-                ready = tall[(plane - 1) % 2, pl.ds(at, count * rows_y), :].astype(jnp.bfloat16)
-                staged[plane - 1, pl.ds(step * count, count)] = ready.reshape(count, rows_y, rows_z)
-                store(plane - 1, step).start()
-
-    for plane in range(planes):
-        @pl.loop(0, steps)
-        def _(step):
-            store(plane, step).wait()
-
-
-def factor_and_inverse(chunks, order, cell_total):
+            block = stack[plane * steps + step]
+            sums = jnp.dot(x_pair[0], block, preferred_element_type=jnp.float32)
+            sums = sums + jnp.dot(x_pair[1], block, preferred_element_type=jnp.float32)
+            sums = sums.astype(jnp.bfloat16).reshape(order // rows_y, rows_y, 2 * rows_z)
+            for half in (0, 1):
+                at = pl.multiple_of((2 * step + half) * rows_y, rows_y)
+                mixed[:, pl.ds(at, rows_y), plane * rows_z:(plane + 1) * rows_z] = sums[
+                    :, :, half * rows_z:(half + 1) * rows_z
+                ]
+
+    turn = turn_matrix(rows_y, 0.0)
+
+    def store(group):
+        some = pl.ds(pl.multiple_of(group * rows_y, rows_y), rows_y)
+        return pltpu.make_async_copy(staged.at[some], out_ref.at[some], out_sem.at[group])
+
+    @pl.loop(0, order // rows_y, unroll=2)
+    def _(group):
+        turned = jnp.dot(turn, mixed[group], preferred_element_type=jnp.float32)
+        turned = turned.astype(jnp.bfloat16)
+        some = pl.ds(pl.multiple_of(group * rows_y, rows_y), rows_y)
+        for plane in range(planes):
+            part = turned[:, plane * rows_z:(plane + 1) * rows_z]
+            staged[some, plane] = part.reshape(rows_y, rows_y, rows_z)
+        store(group).start()
+
+    @pl.loop(0, order // rows_y)
+    def _(group):
+        store(group).wait()
+
+
+def factor_and_modes(chunks, s_new, s_old, shape, cell_total):
+    order, planes, rows_y, rows_z = shape
     height = chunks[0].shape[0] * SPREAD
+    vmem = pl.BlockSpec(memory_space=pltpu.VMEM)
+    hbm = pl.BlockSpec(memory_space=pl.ANY)
     square = (order, order)
+    pairs = planes * rows_y // 2
     return pl.pallas_call(
         functools.partial(factor_kernel, 1.0 / cell_total),
         out_shape=[
             jax.ShapeDtypeStruct(square, jnp.float32),
-            jax.ShapeDtypeStruct((order, 2 * order), jnp.bfloat16),
+            jax.ShapeDtypeStruct(shape, jnp.bfloat16),
         ],
+        in_specs=[vmem] * SPREAD + [hbm, hbm],
+        out_specs=[vmem, hbm],
         scratch_shapes=[
             pltpu.VMEM((height, LANES), jnp.float32),
             pltpu.VMEM((order // LANES, order, LANES), jnp.float32),
@@ -418,31 +449,16 @@
             pltpu.VMEM((PANEL * SUBS, LANES), jnp.float32),
             pltpu.VMEM((2, len(LEFT) * LANES, order), jnp.bfloat16),
             pltpu.VMEM((LANES, order), jnp.bfloat16),
+            pltpu.VMEM((2, order, order), jnp.bfloat16),
+            pltpu.VMEM((pairs, order, 2 * rows_z), jnp.bfloat16),
+            pltpu.VMEM((order // rows_y, rows_y * rows_y, planes * rows_z), jnp.bfloat16),
+            pltpu.VMEM(shape, jnp.bfloat16),
+            pltpu.SemaphoreType.DMA((2,)),
+            pltpu.SemaphoreType.DMA((order // rows_y,)),
         ],
         compiler_params=pltpu.CompilerParams(vmem_limit_bytes=VMEM_BYTES),
         name="factor",
-    )(*chunks)
-
-
-def modes_product(x_pair, s_new, s_old, shape):
-    order, planes, rows_y, rows_z = shape
-    vmem = pl.BlockSpec(memory_space=pltpu.VMEM)
-    hbm = pl.BlockSpec(memory_space=pl.ANY)
-    return pl.pallas_call(
-        modes_kernel,
-        out_shape=jax.ShapeDtypeStruct(shape, jnp.bfloat16),
-        in_specs=[vmem, hbm, hbm],
-        out_specs=hbm,
-        scratch_shapes=[
-            pltpu.VMEM((planes * rows_y // 2, order, 2 * rows_z), jnp.bfloat16),
-            pltpu.VMEM((2, order * rows_y, rows_z), jnp.float32),
-            pltpu.VMEM((planes, order, rows_y, rows_z), jnp.bfloat16),
-            pltpu.SemaphoreType.DMA((2,)),
-            pltpu.SemaphoreType.DMA((planes, rows_y // 2)),
-        ],
-        compiler_params=pltpu.CompilerParams(vmem_limit_bytes=VMEM_BYTES),
-        name="modes",
-    )(x_pair, s_new, s_old)
+    )(*chunks, s_new, s_old)
 
 
 def shards(snapshots, old_modes, mode_scales, plane_counts, links):
@@ -460,8 +476,9 @@
         snapshots, before, after, plane_counts, links, s_old, old_gram
     )
     sums = sum_chunks(chunks, "blk")
-    factor, x_pair = factor_and_inverse(sums, order, peers * planes * rows_y * rows_z)
-    modes = modes_product(x_pair, s_new, s_old, (order, planes, rows_y, rows_z))
+    factor, modes = factor_and_modes(
+        sums, s_new, s_old, (order, planes, rows_y, rows_z), peers * planes * rows_y * rows_z
+    )
     return (modes, factor)
 
 

time: 52.3 us -> 52.5 us (level)
    reshape x0 -> x1, local copies, waits for them, and re-layouts: none -> 0.79 us  [scaled_rows(): mode_scales.reshape(rows, 1)]
    unnamed x8 -> x6, local copies, waits for them, and re-layouts: 2.09 us -> 1.41 us
    pallas_call x2 -> x1, Pallas kernels: 16 us -> 16.2 us  [factor_and_modes(): pl.pallas_call(functools.partial(factor_kernel, 1.0 / cell_total), out_sh...]
  transfers between devices with their start and end apart: 11 -> 11, of which waited for: 6 -> 6; matrix products, arithmetic and copies ran while one was open for 0% -> 2% of each run, Pallas kernels for 5% -> 6%
where the time goes in v7:
time: 52.5 us; the launch traced here: 52.4 us
  Pallas kernels  22.8 us (43%)
  starting transfers between devices  13.8 us (26%)
  waiting for transfers between devices  11.1 us (21%)
  local copies, waits for them, and re-layouts  3.28 us (6%)
  between operations  1.44 us (3%)
    pallas_call x1, Pallas kernels, factor_and_modes(): pl.pallas_call(functools.partial(factor_kernel, 1.0 / cell_total), out_sh...  16.2 us
    ppermute x9, starting transfers between devices, swap(): return lax.ppermute(x, axis, [(i, i ^ flip) for i in range(peers)])  8.3 us
    ppermute x9, waiting for transfers between devices, swap(): return lax.ppermute(x, axis, [(i, i ^ flip) for i in range(peers)])  7.76 us
    ppermute x1, starting transfers between devices, shards(): after = lax.ppermute(first, 'blk', down)  5.47 us
    pallas_call x1, Pallas kernels, filtered_rows(): pl.pallas_call(filter_kernel, out_shape=[jax.ShapeDtypeStruct((planes * r...  3.61 us
    ppermute x1, waiting for transfers between devices, shards(): before = lax.ppermute(last, 'blk', up)  3.3 us
    pallas_call x1, Pallas kernels, scaled_rows(): pl.pallas_call(scale_kernel, out_shape=[jax.ShapeDtypeStruct((planes * ro...  2.96 us
    unnamed x6, local copies, waits for them, and re-layouts  1.41 us
  transfers between devices with their start and end apart: 11, of which 6 were waited for; matrix products, arithmetic and copies ran while one was open for 2% of the time, Pallas kernels for 6%

profile of v7, /device:TPU:0, one launch (start us, length us, event | category | flops | bytes accessed | tf_op | source)
XLA Modules:
  0.0 52.4 jit_solution(14739422376673587866)
XLA Ops:
  0.6 0.0 copy-start
  0.6 0.0 copy-start.2
  1.4 1.1 %fusion = (bf16[64,1,16,128]{3,2,1,0:T(8,128)(2,1)S(1)}, bf16[64,1,16,128]{3,2,1,0:T(8,128)(2,1)S(1)}) fusion(bf16[64,2,16,128]{3,2,1,0:T(8,128)(2,1)} %snap_ref.1, s32[]{:T(128)S(6)} %select_n.3), kind=kLoop, calls=%fused_computation.3 | loop fusion | bytes 1048580 | tf_op jit(solution)/shard_map/slice | solution.py:470
  2.4 5.5 %collective-permute-start.1 = (bf16[64,1,16,128]{3,2,1,0:T(8,128)(2,1)S(1)}, bf16[64,1,16,128]{3,2,1,0:T(8,128)(2,1)S(1)}, u32[]{:S(2)}, u32[]{:S(2)}) collective-permute-start(bf16[64,1,16,128]{3,2,1,0:T(8,128)(2,1)S(1)} %get-tuple-element.20), channel_id=1, source_target_pairs={{1,0},{2,1},{3,2},{4,3},{5,4},{6,5},{7,6},{8,7},{9,8},{10,9},{11,1... | collective-permute-start | bytes 786440 | tf_op jit(solution)/shard_map/ppermute | solution.py:472
  7.9 0.0 collective-permute-start
  7.9 0.8 %copy.7.scales_ref = f32[192,1]{1,0:T(8,128)S(1)} copy(f32[192,1]{0,1:T(1,128)} %bitcast.3) | data formatting | bytes 1536 | tf_op jit(solution)/shard_map/reshape | solution.py:89
  8.7 0.0 copy-start.1
  8.7 1.4 %copy-done.1 = bf16[192,2,16,128]{3,2,1,0:T(8,128)(2,1)S(1)} copy-done((bf16[192,2,16,128]{3,2,1,0:T(8,128)(2,1)S(1)}, bf16[192,2,16,128]{3,2,1,0:T(8,128)(2,1)}, u32[]{:S(2)}) %copy-start.1) | copy-done | bytes 1572888
  10.1 3.0 %scale_gram.1 = (bf16[16,192,256]{2,1,0:T(8,128)(2,1)S(1)}, f32[192,192]{1,0:T(8,128)S(1)}) custom-call(s32[1]{0:T(128)S(6)} %copy.8.count_ref, f32[192,1]{1,0:T(8,128)S(1)} %copy.7.scales_ref, bf16[192,2,16,128]{3,2,1,0:T(8,128)(2,1)S(1)} %copy-done.1), custom_call_target="tpu_custom_call" | custom-call | flops 301989888 | bytes 6291456 | tf_op jit(solution)/shard_map/scale_gram/pallas_call | solution.py:76
  13.1 0.0 collective-permute-done.1.after_ref
  13.1 3.3 %collective-permute-done.before_ref = bf16[64,1,16,128]{3,2,1,0:T(8,128)(2,1)S(1)} collective-permute-done((bf16[64,1,16,128]{3,2,1,0:T(8,128)(2,1)S(1)}, bf16[64,1,16,128]{3,2,1,0:T(8,128)(2,1)S(1)}, u32[]{:S(2)}, u32[]{:S(2)}) %collective-permute-start) | collective-permute-done | bytes 262176 | tf_op jit(solution)/shard_map/ppermute | solution.py:473
  16.4 0.0 copy-done
  16.4 0.0 copy-done.2
  16.4 3.6 %filter_gram.1 = (bf16[16,64,256]{2,1,0:T(8,128)(2,1)S(1)}, f32[72,128]{1,0:T(8,128)S(1)}, f32[72,128]{1,0:T(8,128)S(1)}, f32[72,128]{1,0:T(8,128)S(1)}, f32[72,128]{1,0:T(8,128)S(1)}) custom-call(s32[1]{0:T(128)S(6)} %copy.8.count_ref, s32[1,2]{1,0:T(1,128)S(1)} %copy-done.2, bf16[64,2,16,128]{3,2,1,0:T(8,128)(2,1)S(1)} %copy-done, ...), custom_call_target="tpu_custom_call" | custom-call | flops 134217728 | bytes 2097152 | tf_op jit(solution)/shard_map/filter_gram/pallas_call | solution.py:175
  20.0 0.1 collective-permute-start.2
  20.1 0.1 collective-permute-start.3
  20.2 1.8 %collective-permute-start.4 = (f32[72,128]{1,0:T(8,128)S(1)}, f32[72,128]{1,0:T(8,128)S(1)}, u32[]{:S(2)}, u32[]{:S(2)}) collective-permute-start(f32[72,128]{1,0:T(8,128)S(1)} %get-tuple-element.16), channel_id=1, source_target_pairs={{0,3},{1,2},{2,1},{3,0},{4,7},{5,6},{6,5},{7,4},{8,11},{9,10},{10,... | collective-permute-start | bytes 110600 | tf_op jit(solution)/shard_map/ppermute | solution.py:26
  22.0 0.0 collective-permute-done.2
  22.0 2.4 %collective-permute-done.3 = f32[72,128]{1,0:T(8,128)S(1)} collective-permute-done((f32[72,128]{1,0:T(8,128)S(1)}, f32[72,128]{1,0:T(8,128)S(1)}, u32[]{:S(2)}, u32[]{:S(2)}) %collective-permute-start.3) | collective-permute-done | bytes 36896 | tf_op jit(solution)/shard_map/ppermute | solution.py:26
  24.4 0.0 collective-permute-done.4
  24.4 1.6 %collective-permute-start.7 = (f32[72,128]{1,0:T(8,128)S(1)}, f32[72,128]{1,0:T(8,128)S(1)}, u32[]{:S(2)}, u32[]{:S(2)}) collective-permute-start(f32[72,128]{1,0:T(8,128)S(1)} %add_add_fusion.1), channel_id=1, source_target_pairs={{0,12},{1,13},{2,14},{3,15},{4,8},{5,9},{6,10},{7,11},{8,4},{9,5},... | collective-permute-start | bytes 110600 | tf_op jit(solution)/shard_map/ppermute | solution.py:26
  26.0 0.0 collective-permute-start.6
  26.1 2.8 %collective-permute-start.5 = (f32[72,128]{1,0:T(8,128)S(1)}, f32[72,128]{1,0:T(8,128)S(1)}, u32[]{:S(2)}, u32[]{:S(2)}) collective-permute-start(f32[72,128]{1,0:T(8,128)S(1)} %add_add_fusion.1), channel_id=1, source_target_pairs={{0,4},{1,5},{2,6},{3,7},{4,0},{5,1},{6,2},{7,3},{8,12},{9,13},{10,... | collective-permute-start | bytes 110600 | tf_op jit(solution)/shard_map/ppermute | solution.py:26
  28.9 1.5 %collective-permute-done.7 = f32[72,128]{1,0:T(8,128)S(1)} collective-permute-done((f32[72,128]{1,0:T(8,128)S(1)}, f32[72,128]{1,0:T(8,128)S(1)}, u32[]{:S(2)}, u32[]{:S(2)}) %collective-permute-start.7) | collective-permute-done | bytes 36896 | tf_op jit(solution)/shard_map/ppermute | solution.py:26
  30.4 1.1 %collective-permute-done.6 = f32[72,128]{1,0:T(8,128)S(1)} collective-permute-done((f32[72,128]{1,0:T(8,128)S(1)}, f32[72,128]{1,0:T(8,128)S(1)}, u32[]{:S(2)}, u32[]{:S(2)}) %collective-permute-start.6) | collective-permute-done | bytes 36896 | tf_op jit(solution)/shard_map/ppermute | solution.py:26
  31.5 0.0 collective-permute-done.5
  31.5 0.1 collective-permute-start.10
  31.6 1.6 %collective-permute-start.9 = (f32[72,128]{1,0:T(8,128)S(1)}, f32[72,128]{1,0:T(8,128)S(1)}, u32[]{:S(2)}, u32[]{:S(2)}) collective-permute-start(f32[72,128]{1,0:T(8,128)S(1)} %add_add_fusion.refs_0_), channel_id=1, source_target_pairs={{0,2},{1,3},{2,0},{3,1},{4,6},{5,7},{6,4},{7,5},{8,10},{9,11},{10,... | collective-permute-start | bytes 110600 | tf_op jit(solution)/shard_map/ppermute | solution.py:26
  33.2 0.3 collective-permute-start.8
  33.4 1.8 %collective-permute-done.10.refs_3_ = f32[72,128]{1,0:T(8,128)S(1)} collective-permute-done((f32[72,128]{1,0:T(8,128)S(1)}, f32[72,128]{1,0:T(8,128)S(1)}, u32[]{:S(2)}, u32[]{:S(2)}) %collective-permute-start.10) | collective-permute-done | bytes 36896 | tf_op jit(solution)/shard_map/ppermute | solution.py:26
  35.2 0.9 %collective-permute-done.9.refs_2_ = f32[72,128]{1,0:T(8,128)S(1)} collective-permute-done((f32[72,128]{1,0:T(8,128)S(1)}, f32[72,128]{1,0:T(8,128)S(1)}, u32[]{:S(2)}, u32[]{:S(2)}) %collective-permute-start.9) | collective-permute-done | bytes 36896 | tf_op jit(solution)/shard_map/ppermute | solution.py:26
  36.1 0.0 collective-permute-done.8.refs_1_
  36.1 16.2 %factor.1 = (f32[256,256]{1,0:T(8,128)}, bf16[256,2,16,128]{3,2,1,0:T(8,128)(2,1)}) custom-call(f32[72,128]{1,0:T(8,128)S(1)} %add_add_fusion.refs_0_, f32[72,128]{1,0:T(8,128)S(1)} %collective-permute-done.8.refs_1_, f32[72,128]{1,0:T(8,128)S(1)} %collective-permute-done.9.refs_2_, f32[72,128]{1,0:T(8,128)S(1)} %collective-permute-done.10.refs_3_, ...), custom_call_target="tpu_custom_call" | custom-call | tf_op jit(solution)/shard_map/factor/pallas_call | solution.py:436
  (2 shorter events, 0.0 us)
Async XLA Ops:
  0.6 15.8 %copy-start = (bf16[64,2,16,128]{3,2,1,0:T(8,128)(2,1)S(1)}, bf16[64,2,16,128]{3,2,1,0:T(8,128)(2,1)}, u32[]{:S(2)}) copy-start(bf16[64,2,16,128]{3,2,1,0:T(8,128)(2,1)} %snap_ref.1) | copy-start | bytes 1572868
  0.6 15.8 %copy-start.2 = (s32[1,2]{1,0:T(1,128)S(1)}, s32[1,2]{1,0:T(1,128)}, u32[]{:S(2)}) copy-start(s32[1,2]{1,0:T(1,128)} %links_ref.1) | copy-start | bytes 28
  2.4 10.7 %collective-permute-start.1 = (bf16[64,1,16,128]{3,2,1,0:T(8,128)(2,1)S(1)}, bf16[64,1,16,128]{3,2,1,0:T(8,128)(2,1)S(1)}, u32[]{:S(2)}, u32[]{:S(2)}) collective-permute-start(bf16[64,1,16,128]{3,2,1,0:T(8,128)(2,1)S(1)} %get-tuple-element.20), channel_id=1, source_target_pairs={{1,0},{2,1},{3,2},{4,3},{5,4},{6,5},{7,6},{8,7},{9,8},{10,9},{11,1... | collective-permute-start | bytes 786440 | tf_op jit(solution)/shard_map/ppermute | solution.py:472
  7.9 8.5 %collective-permute-start = (bf16[64,1,16,128]{3,2,1,0:T(8,128)(2,1)S(1)}, bf16[64,1,16,128]{3,2,1,0:T(8,128)(2,1)S(1)}, u32[]{:S(2)}, u32[]{:S(2)}) collective-permute-start(bf16[64,1,16,128]{3,2,1,0:T(8,128)(2,1)S(1)} %get-tuple-element.21), channel_id=1, source_target_pairs={{0,1},{1,2},{2,3},{3,4},{4,5},{5,6},{6,7},{7,8},{8,9},{9,10},{10,1... | collective-permute-start | bytes 786440 | tf_op jit(solution)/shard_map/ppermute | solution.py:473
  8.7 1.4 %copy-start.1 = (bf16[192,2,16,128]{3,2,1,0:T(8,128)(2,1)S(1)}, bf16[192,2,16,128]{3,2,1,0:T(8,128)(2,1)}, u32[]{:S(2)}) copy-start(bf16[192,2,16,128]{3,2,1,0:T(8,128)(2,1)} %old_ref.1) | copy-start | bytes 4718596
  20.0 1.9 %collective-permute-start.2 = (f32[72,128]{1,0:T(8,128)S(1)}, f32[72,128]{1,0:T(8,128)S(1)}, u32[]{:S(2)}, u32[]{:S(2)}) collective-permute-start(f32[72,128]{1,0:T(8,128)S(1)} %get-tuple-element.14), channel_id=1, source_target_pairs={{0,1},{1,0},{2,3},{3,2},{4,5},{5,4},{6,7},{7,6},{8,9},{9,8},{10,11... | collective-permute-start | bytes 110600 | tf_op jit(solution)/shard_map/ppermute | solution.py:26
  20.1 4.3 %collective-permute-start.3 = (f32[72,128]{1,0:T(8,128)S(1)}, f32[72,128]{1,0:T(8,128)S(1)}, u32[]{:S(2)}, u32[]{:S(2)}) collective-permute-start(f32[72,128]{1,0:T(8,128)S(1)} %get-tuple-element.15), channel_id=1, source_target_pairs={{0,2},{1,3},{2,0},{3,1},{4,6},{5,7},{6,4},{7,5},{8,10},{9,11},{10,... | collective-permute-start | bytes 110600 | tf_op jit(solution)/shard_map/ppermute | solution.py:26
  20.2 4.2 %collective-permute-start.4 = (f32[72,128]{1,0:T(8,128)S(1)}, f32[72,128]{1,0:T(8,128)S(1)}, u32[]{:S(2)}, u32[]{:S(2)}) collective-permute-start(f32[72,128]{1,0:T(8,128)S(1)} %get-tuple-element.16), channel_id=1, source_target_pairs={{0,3},{1,2},{2,1},{3,0},{4,7},{5,6},{6,5},{7,4},{8,11},{9,10},{10,... | collective-permute-start | bytes 110600 | tf_op jit(solution)/shard_map/ppermute | solution.py:26
  24.4 6.0 %collective-permute-start.7 = (f32[72,128]{1,0:T(8,128)S(1)}, f32[72,128]{1,0:T(8,128)S(1)}, u32[]{:S(2)}, u32[]{:S(2)}) collective-permute-start(f32[72,128]{1,0:T(8,128)S(1)} %add_add_fusion.1), channel_id=1, source_target_pairs={{0,12},{1,13},{2,14},{3,15},{4,8},{5,9},{6,10},{7,11},{8,4},{9,5},... | collective-permute-start | bytes 110600 | tf_op jit(solution)/shard_map/ppermute | solution.py:26
  26.0 5.4 %collective-permute-start.6 = (f32[72,128]{1,0:T(8,128)S(1)}, f32[72,128]{1,0:T(8,128)S(1)}, u32[]{:S(2)}, u32[]{:S(2)}) collective-permute-start(f32[72,128]{1,0:T(8,128)S(1)} %add_add_fusion.1), channel_id=1, source_target_pairs={{0,8},{1,9},{2,10},{3,11},{4,12},{5,13},{6,14},{7,15},{8,0},{9,1},... | collective-permute-start | bytes 110600 | tf_op jit(solution)/shard_map/ppermute | solution.py:26
  26.1 5.4 %collective-permute-start.5 = (f32[72,128]{1,0:T(8,128)S(1)}, f32[72,128]{1,0:T(8,128)S(1)}, u32[]{:S(2)}, u32[]{:S(2)}) collective-permute-start(f32[72,128]{1,0:T(8,128)S(1)} %add_add_fusion.1), channel_id=1, source_target_pairs={{0,4},{1,5},{2,6},{3,7},{4,0},{5,1},{6,2},{7,3},{8,12},{9,13},{10,... | collective-permute-start | bytes 110600 | tf_op jit(solution)/shard_map/ppermute | solution.py:26
  31.5 3.7 %collective-permute-start.10 = (f32[72,128]{1,0:T(8,128)S(1)}, f32[72,128]{1,0:T(8,128)S(1)}, u32[]{:S(2)}, u32[]{:S(2)}) collective-permute-start(f32[72,128]{1,0:T(8,128)S(1)} %add_add_fusion.refs_0_), channel_id=1, source_target_pairs={{0,3},{1,2},{2,1},{3,0},{4,7},{5,6},{6,5},{7,4},{8,11},{9,10},{10,... | collective-permute-start | bytes 110600 | tf_op jit(solution)/shard_map/ppermute | solution.py:26
  31.6 4.6 %collective-permute-start.9 = (f32[72,128]{1,0:T(8,128)S(1)}, f32[72,128]{1,0:T(8,128)S(1)}, u32[]{:S(2)}, u32[]{:S(2)}) collective-permute-start(f32[72,128]{1,0:T(8,128)S(1)} %add_add_fusion.refs_0_), channel_id=1, source_target_pairs={{0,2},{1,3},{2,0},{3,1},{4,6},{5,7},{6,4},{7,5},{8,10},{9,11},{10,... | collective-permute-start | bytes 110600 | tf_op jit(solution)/shard_map/ppermute | solution.py:26
  33.2 3.0 %collective-permute-start.8 = (f32[72,128]{1,0:T(8,128)S(1)}, f32[72,128]{1,0:T(8,128)S(1)}, u32[]{:S(2)}, u32[]{:S(2)}) collective-permute-start(f32[72,128]{1,0:T(8,128)S(1)} %add_add_fusion.refs_0_), channel_id=1, source_target_pairs={{0,1},{1,0},{2,3},{3,2},{4,5},{5,4},{6,7},{7,6},{8,9},{9,8},{10,11... | collective-permute-start | bytes 110600 | tf_op jit(solution)/shard_map/ppermute | solution.py:26

commit v8 on v7

--- a/solution.py
+++ b/solution.py
@@ -9,6 +9,7 @@
 
 PANEL = 16
 HALF = 8
+GROUP = 64
 LANES = 128
 SUBS = 8
 SPREAD = 4
@@ -52,9 +53,8 @@
     plane = lax.broadcasted_iota(jnp.int32, (rows_y, planes * rows_z), 1) // rows_z
     alive = jnp.where(plane < count_ref[0], 1.0, 0.0)
 
-    @pl.loop(0, rows // rows_y)
-    def _(group):
-        at = pl.ds(pl.multiple_of(group * rows_y, rows_y), rows_y)
+    for group in range(rows // rows_y):
+        at = slice(group * rows_y, (group + 1) * rows_y)
         block = old_ref[at]
         block = jnp.concatenate(
             [block[:, p].reshape(rows_y * rows_y, rows_z) for p in range(planes)], axis=1
@@ -95,9 +95,9 @@
 
 
 def filter_kernel(
-    count_ref, links_ref, snap_ref, before_ref, after_ref, old_ref, oldgram_ref, s_ref, *rest
+    count_ref, links_ref, snap_ref, after_ref, before_ref, old_ref, oldgram_ref, s_ref, *rest
 ):
-    chunk_refs, packed = rest[:SPREAD], rest[SPREAD]
+    keep_ref, give_ref, packed = rest
     rows, planes, rows_y, rows_z = snap_ref.shape
     count = count_ref[0]
     join_low = links_ref[0, 0].astype(jnp.float32)
@@ -123,9 +123,8 @@
     weights = jnp.concatenate([jnp.concatenate(line, axis=1) for line in blocks], axis=0)
     turn = turn_matrix(rows_y, 0.25)
 
-    @pl.loop(0, rows // rows_y)
-    def _(group):
-        at = pl.ds(pl.multiple_of(group * rows_y, rows_y), rows_y)
+    for group in range(rows // rows_y):
+        at = slice(group * rows_y, (group + 1) * rows_y)
         snap = snap_ref[at]
         sources = [before_ref[at][:, 0]] + [snap[:, p] for p in range(planes)] + [after_ref[at][:, 0]]
         sources = [x.reshape(rows_y * rows_y, rows_z) for x in sources]
@@ -161,7 +160,9 @@
     height = packed.shape[0] // SPREAD
     for flip in range(SPREAD):
         at = pl.multiple_of((share ^ flip) * height, SUBS)
-        chunk_refs[flip][...] = packed[pl.ds(at, height), :]
+        side = give_ref if flip % 2 else keep_ref
+        part = flip // 2 * height
+        side[part:part + height, :] = packed[pl.ds(at, height), :]
 
 
 def filtered_rows(snapshots, before, after, plane_counts, links, s_old, old_gram):
@@ -171,35 +172,32 @@
     height = packed_rows(order)
     smem = pl.BlockSpec(memory_space=pltpu.SMEM)
     vmem = pl.BlockSpec(memory_space=pltpu.VMEM)
-    chunk = jax.ShapeDtypeStruct((height // SPREAD, LANES), jnp.float32)
+    half = jax.ShapeDtypeStruct((height // 2, LANES), jnp.float32)
     return pl.pallas_call(
         filter_kernel,
-        out_shape=[jax.ShapeDtypeStruct((planes * rows_y // 2, rows, 2 * rows_z), jnp.bfloat16)] + [chunk] * SPREAD,
+        out_shape=[jax.ShapeDtypeStruct((planes * rows_y // 2, rows, 2 * rows_z), jnp.bfloat16)] + [half] * 2,
         in_specs=[smem, smem] + [vmem] * 5,
-        out_specs=[vmem] * (1 + SPREAD),
+        out_specs=[vmem] * 3,
         scratch_shapes=[pltpu.VMEM((height, LANES), jnp.float32)],
         compiler_params=pltpu.CompilerParams(vmem_limit_bytes=VMEM_BYTES),
         cost_estimate=pl.CostEstimate(
             flops=2 * rows * order * cells, bytes_accessed=2 * order * cells, transcendentals=0
         ),
         name="filter_gram",
-    )(plane_counts, links, snapshots, before, after, s_old, old_gram)
-
-
-def sum_chunks(chunks, axis):
+    )(plane_counts, links, snapshots, after, before, s_old, old_gram)
+
+
+def sum_shares(keep, give, axis):
     peers = lax.axis_size(axis)
-    arrived = [chunks[0]] + [swap(chunks[d], axis, d) for d in range(1, SPREAD)]
-    total = (arrived[0] + arrived[1]) + (arrived[2] + arrived[3])
+    height = keep.shape[0] // 2
+    both = keep + swap(give, axis, 1)
+    total = both[:height] + swap(both[height:], axis, 2)
     step = SPREAD
     while step < peers:
-        if step * 4 <= peers:
-            one, two, three = (swap(total, axis, d * step) for d in (1, 2, 3))
-            total = (total + one) + (two + three)
-            step *= 4
-        else:
-            total = total + swap(total, axis, step)
-            step *= 2
-    return [total] + [swap(total, axis, d) for d in range(1, SPREAD)]
+        total = total + swap(total, axis, step)
+        step *= 2
+    both = jnp.concatenate([total, swap(total, axis, 2)], axis=0)
+    return both, swap(both, axis, 1)
 
 
 def split_three(x):
@@ -345,10 +343,11 @@
 
 
 def factor_kernel(scale, *refs):
-    chunk_refs, refs = refs[:SPREAD], refs[SPREAD:]
+    sum_refs, refs = refs[:2], refs[2:]
     new_ref, old_ref, f_ref, out_ref, packed, t_ref, x_ref, cols, rows, *refs = refs
     wide, narrow, x_pair, stack, mixed, staged, in_sem, out_sem = refs
     tiles, order, _ = t_ref.shape
+    _, planes, rows_y, rows_z = out_ref.shape
     new_count = new_ref.shape[1]
     load_new = pltpu.make_async_copy(new_ref, stack.at[:, pl.ds(0, new_count)], in_sem.at[0])
     load_old = pltpu.make_async_copy(
@@ -360,7 +359,8 @@
     height = packed.shape[0] // SPREAD
     for flip in range(SPREAD):
         at = pl.multiple_of((share ^ flip) * height, SUBS)
-        packed[pl.ds(at, height), :] = chunk_refs[flip][...] * scale
+        part = flip // 2 * height
+        packed[pl.ds(at, height), :] = sum_refs[flip % 2][part:part + height, :] * scale
     i = lax.broadcasted_iota(jnp.int32, (LANES, LANES), 0)
     j = lax.broadcasted_iota(jnp.int32, (LANES, LANES), 1)
     shared = packed[:LANES, :]
@@ -377,58 +377,79 @@
     narrow[...] = jnp.zeros(narrow.shape, narrow.dtype)
     rows[...] = jnp.zeros(rows.shape, jnp.float32)
 
-    per_tile = LANES // PANEL
-    for low in range(0, order, LANES):
-        @pl.loop(low // PANEL, low // PANEL + per_tile)
-        def _(panel):
-            factor_panel(panel, low, t_ref, f_ref, x_ref, cols, rows, wide, narrow)
-
-    inverse = x_ref[...]
-    high = inverse.astype(jnp.bfloat16)
-    low = (inverse - high.astype(jnp.float32)).astype(jnp.bfloat16)
-    x_pair[0] = high
-    x_pair[1] = low
-    load_new.wait()
-    load_old.wait()
-    _, planes, rows_y, rows_z = out_ref.shape
+    turn = turn_matrix(rows_y, 0.0)
     steps = rows_y // 2
-    for plane in range(planes):
-        @pl.loop(0, steps, unroll=2)
-        def _(step):
-            block = stack[plane * steps + step]
-            sums = jnp.dot(x_pair[0], block, preferred_element_type=jnp.float32)
-            sums = sums + jnp.dot(x_pair[1], block, preferred_element_type=jnp.float32)
-            sums = sums.astype(jnp.bfloat16).reshape(order // rows_y, rows_y, 2 * rows_z)
-            for half in (0, 1):
-                at = pl.multiple_of((2 * step + half) * rows_y, rows_y)
-                mixed[:, pl.ds(at, rows_y), plane * rows_z:(plane + 1) * rows_z] = sums[
-                    :, :, half * rows_z:(half + 1) * rows_z
-                ]
-
-    turn = turn_matrix(rows_y, 0.0)
-
-    def store(group):
-        some = pl.ds(pl.multiple_of(group * rows_y, rows_y), rows_y)
-        return pltpu.make_async_copy(staged.at[some], out_ref.at[some], out_sem.at[group])
-
-    @pl.loop(0, order // rows_y, unroll=2)
-    def _(group):
-        turned = jnp.dot(turn, mixed[group], preferred_element_type=jnp.float32)
-        turned = turned.astype(jnp.bfloat16)
-        some = pl.ds(pl.multiple_of(group * rows_y, rows_y), rows_y)
+    per_group = GROUP // PANEL
+    pairs = planes * steps
+    per_panel = pairs // per_group
+
+    def split_rows(group):
+        rows_here = x_ref[group * GROUP:(group + 1) * GROUP, :]
+        high = rows_here.astype(jnp.bfloat16)
+        x_pair[:GROUP, :] = high
+        x_pair[GROUP:, :] = (rows_here - high.astype(jnp.float32)).astype(jnp.bfloat16)
+
+    def multiply(group, pair):
+        depth = (group + 1) * GROUP
+        sums = jnp.dot(
+            x_pair[:, :depth], stack[pair, :depth, :], preferred_element_type=jnp.float32
+        )
+        sums = (sums[:GROUP] + sums[GROUP:]).astype(jnp.bfloat16)
+        sums = sums.reshape(GROUP // rows_y, rows_y, 2 * rows_z)
+        some = slice(group * GROUP // rows_y, (group + 1) * GROUP // rows_y)
+        for half in (0, 1):
+            y = 2 * (pair % steps) + half
+            at = pl.ds(pl.multiple_of(y * rows_y, rows_y), rows_y)
+            mixed[pair // steps, some, at, :] = sums[:, :, half * rows_z:(half + 1) * rows_z]
+
+    def store(some):
+        at = pl.ds(pl.multiple_of(some * rows_y, rows_y), rows_y)
+        return pltpu.make_async_copy(staged.at[at], out_ref.at[at], out_sem.at[some])
+
+    def finish(some):
+        block = jnp.concatenate([mixed[plane, some] for plane in range(planes)], axis=1)
+        turned = jnp.dot(turn, block, preferred_element_type=jnp.float32).astype(jnp.bfloat16)
+        at = pl.ds(pl.multiple_of(some * rows_y, rows_y), rows_y)
         for plane in range(planes):
             part = turned[:, plane * rows_z:(plane + 1) * rows_z]
-            staged[some, plane] = part.reshape(rows_y, rows_y, rows_z)
-        store(group).start()
+            staged[at, plane] = part.reshape(rows_y, rows_y, rows_z)
+        store(some).start()
+
+    groups = order // GROUP
+    blocks = GROUP // rows_y
+    for group in range(groups):
+        if group == 1:
+            load_new.wait()
+            load_old.wait()
+        if group > 0:
+            split_rows(group - 1)
+
+        @pl.loop(0, per_group)
+        def _(step):
+            panel = group * per_group + step
+            factor_panel(panel, group * GROUP, t_ref, f_ref, x_ref, cols, rows, wide, narrow)
+            if group > 0:
+                for k in range(per_panel):
+                    multiply(group - 1, step * per_panel + k)
+            if group > 1:
+                finish((group - 2) * blocks + step)
+
+    split_rows(groups - 1)
+    for k in range(blocks):
+        finish((groups - 2) * blocks + k)
+    for pair in range(pairs):
+        multiply(groups - 1, pair)
+    for k in range(blocks):
+        finish((groups - 1) * blocks + k)
 
     @pl.loop(0, order // rows_y)
-    def _(group):
-        store(group).wait()
-
-
-def factor_and_modes(chunks, s_new, s_old, shape, cell_total):
+    def _(some):
+        store(some).wait()
+
+
+def factor_and_modes(sums, s_new, s_old, shape, cell_total):
     order, planes, rows_y, rows_z = shape
-    height = chunks[0].shape[0] * SPREAD
+    height = sums[0].shape[0] * 2
     vmem = pl.BlockSpec(memory_space=pltpu.VMEM)
     hbm = pl.BlockSpec(memory_space=pl.ANY)
     square = (order, order)
@@ -439,7 +460,7 @@
             jax.ShapeDtypeStruct(square, jnp.float32),
             jax.ShapeDtypeStruct(shape, jnp.bfloat16),
         ],
-        in_specs=[vmem] * SPREAD + [hbm, hbm],
+        in_specs=[vmem] * 2 + [hbm, hbm],
         out_specs=[vmem, hbm],
         scratch_shapes=[
             pltpu.VMEM((height, LANES), jnp.float32),
@@ -449,16 +470,16 @@
             pltpu.VMEM((PANEL * SUBS, LANES), jnp.float32),
             pltpu.VMEM((2, len(LEFT) * LANES, order), jnp.bfloat16),
             pltpu.VMEM((LANES, order), jnp.bfloat16),
-            pltpu.VMEM((2, order, order), jnp.bfloat16),
+            pltpu.VMEM((2 * GROUP, order), jnp.bfloat16),
             pltpu.VMEM((pairs, order, 2 * rows_z), jnp.bfloat16),
-            pltpu.VMEM((order // rows_y, rows_y * rows_y, planes * rows_z), jnp.bfloat16),
+            pltpu.VMEM((planes, order // rows_y, rows_y * rows_y, rows_z), jnp.bfloat16),
             pltpu.VMEM(shape, jnp.bfloat16),
             pltpu.SemaphoreType.DMA((2,)),
             pltpu.SemaphoreType.DMA((order // rows_y,)),
         ],
         compiler_params=pltpu.CompilerParams(vmem_limit_bytes=VMEM_BYTES),
         name="factor",
-    )(*chunks, s_new, s_old)
+    )(*sums, s_new, s_old)
 
 
 def shards(snapshots, old_modes, mode_scales, plane_counts, links):
@@ -469,13 +490,13 @@
     down = [(j, i) for i, j in up]
     first = lax.slice_in_dim(snapshots, 0, 1, axis=1)
     last = lax.dynamic_slice_in_dim(snapshots, plane_counts[0] - 1, 1, axis=1)
+    before = lax.ppermute(last, "blk", up)
     after = lax.ppermute(first, "blk", down)
-    before = lax.ppermute(last, "blk", up)
     s_old, old_gram = scaled_rows(old_modes, mode_scales, plane_counts)
-    s_new, *chunks = filtered_rows(
+    s_new, keep, give = filtered_rows(
         snapshots, before, after, plane_counts, links, s_old, old_gram
     )
-    sums = sum_chunks(chunks, "blk")
+    sums = sum_shares(keep, give, "blk")
     factor, modes = factor_and_modes(
         sums, s_new, s_old, (order, planes, rows_y, rows_z), peers * planes * rows_y * rows_z
     )

time: 52.5 us -> 52.4 us (level)
  waiting for transfers between devices: 11.1 us -> 16.9 us
  starting transfers between devices: 13.8 us -> 10.2 us
  Pallas kernels: 22.8 us -> 20.4 us
    ppermute x9 -> x6, waiting for transfers between devices: 7.76 us -> 16.8 us  [swap(): return lax.ppermute(x, axis, [(i, i ^ flip) for i in range(peers)])]
    ppermute x9 -> x6, starting transfers between devices: 8.3 us -> 4.68 us  [swap(): return lax.ppermute(x, axis, [(i, i ^ flip) for i in range(peers)])]
    ppermute x1, waiting for transfers between devices: 3.3 us -> 0.05 us  [shards(): before = lax.ppermute(last, 'blk', up)]
    pallas_call x1, Pallas kernels: 2.96 us -> 1.83 us  [scaled_rows(): pl.pallas_call(scale_kernel, out_shape=[jax.ShapeDtypeStruct((planes * ro...]
    dynamic_slice x0 -> x1, local copies, waits for them, and re-layouts: none -> 1.07 us  [shards(): last = lax.dynamic_slice_in_dim(snapshots, plane_counts[0] - 1, 1, axis=1)]
    slice x1, local copies, waits for them, and re-layouts: 1.07 us -> 0.01 us  [sum_shares(): total = both[:height] + swap(both[height:], axis, 2)]
    pallas_call x1, Pallas kernels: 3.61 us -> 2.82 us  [filtered_rows(): pl.pallas_call(filter_kernel, out_shape=[jax.ShapeDtypeStruct((planes * r...]
  transfers between devices with their start and end apart: 11 -> 8, of which waited for: 6 -> 6; matrix products, arithmetic and copies ran while one was open for 2% -> 2% of each run, Pallas kernels for 6% -> 4%
where the time goes in v8:
time: 52.4 us; the launch traced here: 52.2 us
  Pallas kernels  20.4 us (39%)
  waiting for transfers between devices  16.9 us (32%)
  starting transfers between devices  10.2 us (19%)
  local copies, waits for them, and re-layouts  3.28 us (6%)
  between operations  1.42 us (3%)
    ppermute x6, waiting for transfers between devices, swap(): return lax.ppermute(x, axis, [(i, i ^ flip) for i in range(peers)])  16.8 us
    pallas_call x1, Pallas kernels, factor_and_modes(): pl.pallas_call(functools.partial(factor_kernel, 1.0 / cell_total), out_sh...  15.7 us
    ppermute x1, starting transfers between devices, shards(): after = lax.ppermute(first, 'blk', down)  5.03 us
    ppermute x6, starting transfers between devices, swap(): return lax.ppermute(x, axis, [(i, i ^ flip) for i in range(peers)])  4.68 us
    pallas_call x1, Pallas kernels, filtered_rows(): pl.pallas_call(filter_kernel, out_shape=[jax.ShapeDtypeStruct((planes * r...  2.82 us
    pallas_call x1, Pallas kernels, scaled_rows(): pl.pallas_call(scale_kernel, out_shape=[jax.ShapeDtypeStruct((planes * ro...  1.83 us
    unnamed x6, local copies, waits for them, and re-layouts  1.41 us
    dynamic_slice x1, local copies, waits for them, and re-layouts, shards(): last = lax.dynamic_slice_in_dim(snapshots, plane_counts[0] - 1, 1, axis=1)  1.07 us
  transfers between devices with their start and end apart: 8, of which 6 were waited for; matrix products, arithmetic and copies ran while one was open for 2% of the time, Pallas kernels for 4%

profile of v8, /device:TPU:0, one launch (start us, length us, event | category | flops | bytes accessed | tf_op | source)
XLA Modules:
  0.0 52.2 jit_solution(17306005559222066852)
XLA Ops:
  0.6 0.0 copy-start
  0.6 0.0 copy-start.2
  1.4 1.1 %constant_dynamic-slice_fusion = (bf16[64,1,16,128]{3,2,1,0:T(8,128)(2,1)S(1)}, bf16[64,1,16,128]{3,2,1,0:T(8,128)(2,1)S(1)}) fusion(bf16[64,2,16,128]{3,2,1,0:T(8,128)(2,1)} %snap_ref.1, s32[]{:T(128)S(6)} %select_n.3), kind=kLoop, calls=%fused_computation.2 | loop fusion | bytes 1048580 | tf_op jit(solution)/shard_map/dynamic_slice | solution.py:492
  2.4 0.5 collective-permute-start.1
  2.9 5.0 %collective-permute-start = (bf16[64,1,16,128]{3,2,1,0:T(8,128)(2,1)S(1)}, bf16[64,1,16,128]{3,2,1,0:T(8,128)(2,1)S(1)}, u32[]{:S(2)}, u32[]{:S(2)}) collective-permute-start(bf16[64,1,16,128]{3,2,1,0:T(8,128)(2,1)S(1)} %get-tuple-element.17), channel_id=1, source_target_pairs={{1,0},{2,1},{3,2},{4,3},{5,4},{6,5},{7,6},{8,7},{9,8},{10,9},{11,1... | collective-permute-start | bytes 786440 | tf_op jit(solution)/shard_map/ppermute | solution.py:494
  8.0 0.8 %copy.7.scales_ref = f32[192,1]{1,0:T(8,128)S(1)} copy(f32[192,1]{0,1:T(1,128)} %bitcast.3) | data formatting | bytes 1536 | tf_op jit(solution)/shard_map/reshape | solution.py:89
  8.8 0.0 copy-start.1
  8.8 1.4 %copy-done.1 = bf16[192,2,16,128]{3,2,1,0:T(8,128)(2,1)S(1)} copy-done((bf16[192,2,16,128]{3,2,1,0:T(8,128)(2,1)S(1)}, bf16[192,2,16,128]{3,2,1,0:T(8,128)(2,1)}, u32[]{:S(2)}) %copy-start.1) | copy-done | bytes 1572888
  10.2 1.8 %scale_gram.1 = (bf16[16,192,256]{2,1,0:T(8,128)(2,1)S(1)}, f32[192,192]{1,0:T(8,128)S(1)}) custom-call(s32[1]{0:T(128)S(6)} %copy.8.count_ref, f32[192,1]{1,0:T(8,128)S(1)} %copy.7.scales_ref, bf16[192,2,16,128]{3,2,1,0:T(8,128)(2,1)S(1)} %copy-done.1), custom_call_target="tpu_custom_call" | custom-call | flops 301989888 | bytes 6291456 | tf_op jit(solution)/shard_map/scale_gram/pallas_call | solution.py:76
  12.0 0.1 collective-permute-done.1.before_ref
  12.1 0.0 collective-permute-done.after_ref
  12.1 0.0 copy-done
  12.1 0.0 copy-done.2
  12.1 2.8 %filter_gram.1 = (bf16[16,64,256]{2,1,0:T(8,128)(2,1)S(1)}, f32[144,128]{1,0:T(8,128)S(1)}, f32[144,128]{1,0:T(8,128)S(1)}) custom-call(s32[1]{0:T(128)S(6)} %copy.8.count_ref, s32[1,2]{1,0:T(1,128)S(1)} %copy-done.2, bf16[64,2,16,128]{3,2,1,0:T(8,128)(2,1)S(1)} %copy-done, bf16[64,1,16,128]{3,2,1,0:T(8,128)(2,1)S(1)} %collective-permute-done.after_ref, ...), custom_call_target="tpu_custom_call" | custom-call | flops 134217728 | bytes 2097152 | tf_op jit(solution)/shard_map/filter_gram/pallas_call | solution.py:176
  14.9 2.1 %collective-permute-start.2 = (f32[144,128]{1,0:T(8,128)S(1)}, f32[144,128]{1,0:T(8,128)S(1)}, u32[]{:S(2)}, u32[]{:S(2)}) collective-permute-start(f32[144,128]{1,0:T(8,128)S(1)} %get-tuple-element.12), channel_id=1, source_target_pairs={{0,1},{1,0},{2,3},{3,2},{4,5},{5,4},{6,7},{7,6},{8,9},{9,8},{10,11... | collective-permute-start | bytes 221192 | tf_op jit(solution)/shard_map/ppermute | solution.py:27
  17.0 0.9 %collective-permute-done.2 = f32[144,128]{1,0:T(8,128)S(1)} collective-permute-done((f32[144,128]{1,0:T(8,128)S(1)}, f32[144,128]{1,0:T(8,128)S(1)}, u32[]{:S(2)}, u32[]{:S(2)}) %collective-permute-start.2) | collective-permute-done | bytes 73760 | tf_op jit(solution)/shard_map/ppermute | solution.py:27
  18.0 0.1 collective-permute-start.3
  18.1 3.9 %collective-permute-done.3 = f32[72,128]{1,0:T(8,128)S(1)} collective-permute-done((f32[72,128]{1,0:T(8,128)S(1)}, f32[72,128]{1,0:T(8,128)S(1)}, u32[]{:S(2)}, u32[]{:S(2)}) %collective-permute-start.3) | collective-permute-done | bytes 36896 | tf_op jit(solution)/shard_map/ppermute | solution.py:27
  22.0 0.7 %collective-permute-start.4 = (f32[72,128]{1,0:T(8,128)S(1)}, f32[72,128]{1,0:T(8,128)S(1)}, u32[]{:S(2)}, u32[]{:S(2)}) collective-permute-start(f32[72,128]{1,0:T(8,128)S(1)} %slice_add_fusion), channel_id=1, source_target_pairs={{0,4},{1,5},{2,6},{3,7},{4,0},{5,1},{6,2},{7,3},{8,12},{9,13},{10,... | collective-permute-start | bytes 110600 | tf_op jit(solution)/shard_map/ppermute | solution.py:27
  22.7 3.3 %collective-permute-done.4 = f32[72,128]{1,0:T(8,128)S(1)} collective-permute-done((f32[72,128]{1,0:T(8,128)S(1)}, f32[72,128]{1,0:T(8,128)S(1)}, u32[]{:S(2)}, u32[]{:S(2)}) %collective-permute-start.4) | collective-permute-done | bytes 36896 | tf_op jit(solution)/shard_map/ppermute | solution.py:27
  26.0 1.7 %collective-permute-start.5 = (f32[72,128]{1,0:T(8,128)S(1)}, f32[72,128]{1,0:T(8,128)S(1)}, u32[]{:S(2)}, u32[]{:S(2)}) collective-permute-start(f32[72,128]{1,0:T(8,128)S(1)} %add.26), channel_id=1, source_target_pairs={{0,8},{1,9},{2,10},{3,11},{4,12},{5,13},{6,14},{7,15},{8,0},{9,1},... | collective-permute-start | bytes 110600 | tf_op jit(solution)/shard_map/ppermute | solution.py:27
  27.7 3.5 %collective-permute-done.5 = f32[72,128]{1,0:T(8,128)S(1)} collective-permute-done((f32[72,128]{1,0:T(8,128)S(1)}, f32[72,128]{1,0:T(8,128)S(1)}, u32[]{:S(2)}, u32[]{:S(2)}) %collective-permute-start.5) | collective-permute-done | bytes 36896 | tf_op jit(solution)/shard_map/ppermute | solution.py:27
  31.2 0.0 collective-permute-start.6
  31.2 3.9 %collective-permute-done.6 = f32[72,128]{1,0:T(8,128)S(1)} collective-permute-done((f32[72,128]{1,0:T(8,128)S(1)}, f32[72,128]{1,0:T(8,128)S(1)}, u32[]{:S(2)}, u32[]{:S(2)}) %collective-permute-start.6) | collective-permute-done | bytes 36896 | tf_op jit(solution)/shard_map/ppermute | solution.py:27
  35.2 0.0 collective-permute-start.7
  35.2 1.3 %collective-permute-done.7.refs_1_ = f32[144,128]{1,0:T(8,128)S(1)} collective-permute-done((f32[144,128]{1,0:T(8,128)S(1)}, f32[144,128]{1,0:T(8,128)S(1)}, u32[]{:S(2)}, u32[]{:S(2)}) %collective-permute-start.7) | collective-permute-done | bytes 73760 | tf_op jit(solution)/shard_map/ppermute | solution.py:27
  36.5 15.7 %factor.1 = (f32[256,256]{1,0:T(8,128)}, bf16[256,2,16,128]{3,2,1,0:T(8,128)(2,1)}) custom-call(f32[144,128]{1,0:T(8,128)S(1)} %pad_maximum_fusion.refs_0_, f32[144,128]{1,0:T(8,128)S(1)} %collective-permute-done.7.refs_1_, bf16[16,64,256]{2,1,0:T(8,128)(2,1)S(1)} %get-tuple-element.13.refs_2_, bf16[16,192,256]{2,1,0:T(8,128)(2,1)S(1)} %get-tuple-element.9.old_ref.refs_3_), custom_call_target="tpu_custom_call" | custom-call | tf_op jit(solution)/shard_map/factor/pallas_call | solution.py:457
  (6 shorter events, 0.0 us)
Async XLA Ops:
  0.6 11.4 %copy-start = (bf16[64,2,16,128]{3,2,1,0:T(8,128)(2,1)S(1)}, bf16[64,2,16,128]{3,2,1,0:T(8,128)(2,1)}, u32[]{:S(2)}) copy-start(bf16[64,2,16,128]{3,2,1,0:T(8,128)(2,1)} %snap_ref.1) | copy-start | bytes 1572868
  0.6 11.4 %copy-start.2 = (s32[1,2]{1,0:T(1,128)S(1)}, s32[1,2]{1,0:T(1,128)}, u32[]{:S(2)}) copy-start(s32[1,2]{1,0:T(1,128)} %links_ref.1) | copy-start | bytes 28
  2.4 9.6 %collective-permute-start.1 = (bf16[64,1,16,128]{3,2,1,0:T(8,128)(2,1)S(1)}, bf16[64,1,16,128]{3,2,1,0:T(8,128)(2,1)S(1)}, u32[]{:S(2)}, u32[]{:S(2)}) collective-permute-start(bf16[64,1,16,128]{3,2,1,0:T(8,128)(2,1)S(1)} %get-tuple-element.16), channel_id=1, source_target_pairs={{0,1},{1,2},{2,3},{3,4},{4,5},{5,6},{6,7},{7,8},{8,9},{9,10},{10,1... | collective-permute-start | bytes 786440 | tf_op jit(solution)/shard_map/ppermute | solution.py:493
  2.9 9.1 %collective-permute-start = (bf16[64,1,16,128]{3,2,1,0:T(8,128)(2,1)S(1)}, bf16[64,1,16,128]{3,2,1,0:T(8,128)(2,1)S(1)}, u32[]{:S(2)}, u32[]{:S(2)}) collective-permute-start(bf16[64,1,16,128]{3,2,1,0:T(8,128)(2,1)S(1)} %get-tuple-element.17), channel_id=1, source_target_pairs={{1,0},{2,1},{3,2},{4,3},{5,4},{6,5},{7,6},{8,7},{9,8},{10,9},{11,1... | collective-permute-start | bytes 786440 | tf_op jit(solution)/shard_map/ppermute | solution.py:494
  8.8 1.4 %copy-start.1 = (bf16[192,2,16,128]{3,2,1,0:T(8,128)(2,1)S(1)}, bf16[192,2,16,128]{3,2,1,0:T(8,128)(2,1)}, u32[]{:S(2)}) copy-start(bf16[192,2,16,128]{3,2,1,0:T(8,128)(2,1)} %old_ref.1) | copy-start | bytes 4718596
  14.9 3.0 %collective-permute-start.2 = (f32[144,128]{1,0:T(8,128)S(1)}, f32[144,128]{1,0:T(8,128)S(1)}, u32[]{:S(2)}, u32[]{:S(2)}) collective-permute-start(f32[144,128]{1,0:T(8,128)S(1)} %get-tuple-element.12), channel_id=1, source_target_pairs={{0,1},{1,0},{2,3},{3,2},{4,5},{5,4},{6,7},{7,6},{8,9},{9,8},{10,11... | collective-permute-start | bytes 221192 | tf_op jit(solution)/shard_map/ppermute | solution.py:27
  18.0 4.0 %collective-permute-start.3 = (f32[72,128]{1,0:T(8,128)S(1)}, f32[72,128]{1,0:T(8,128)S(1)}, u32[]{:S(2)}, u32[]{:S(2)}) collective-permute-start(f32[72,128]{1,0:T(8,128)S(1)} %slice.13), channel_id=1, source_target_pairs={{0,2},{1,3},{2,0},{3,1},{4,6},{5,7},{6,4},{7,5},{8,10},{9,11},{10,... | collective-permute-start | bytes 110600 | tf_op jit(solution)/shard_map/ppermute | solution.py:27
  22.0 4.0 %collective-permute-start.4 = (f32[72,128]{1,0:T(8,128)S(1)}, f32[72,128]{1,0:T(8,128)S(1)}, u32[]{:S(2)}, u32[]{:S(2)}) collective-permute-start(f32[72,128]{1,0:T(8,128)S(1)} %slice_add_fusion), channel_id=1, source_target_pairs={{0,4},{1,5},{2,6},{3,7},{4,0},{5,1},{6,2},{7,3},{8,12},{9,13},{10,... | collective-permute-start | bytes 110600 | tf_op jit(solution)/shard_map/ppermute | solution.py:27
  26.0 5.3 %collective-permute-start.5 = (f32[72,128]{1,0:T(8,128)S(1)}, f32[72,128]{1,0:T(8,128)S(1)}, u32[]{:S(2)}, u32[]{:S(2)}) collective-permute-start(f32[72,128]{1,0:T(8,128)S(1)} %add.26), channel_id=1, source_target_pairs={{0,8},{1,9},{2,10},{3,11},{4,12},{5,13},{6,14},{7,15},{8,0},{9,1},... | collective-permute-start | bytes 110600 | tf_op jit(solution)/shard_map/ppermute | solution.py:27
  31.2 4.0 %collective-permute-start.6 = (f32[72,128]{1,0:T(8,128)S(1)}, f32[72,128]{1,0:T(8,128)S(1)}, u32[]{:S(2)}, u32[]{:S(2)}) collective-permute-start(f32[72,128]{1,0:T(8,128)S(1)} %add.27), channel_id=1, source_target_pairs={{0,2},{1,3},{2,0},{3,1},{4,6},{5,7},{6,4},{7,5},{8,10},{9,11},{10,... | collective-permute-start | bytes 110600 | tf_op jit(solution)/shard_map/ppermute | solution.py:27
  35.2 1.3 %collective-permute-start.7 = (f32[144,128]{1,0:T(8,128)S(1)}, f32[144,128]{1,0:T(8,128)S(1)}, u32[]{:S(2)}, u32[]{:S(2)}) collective-permute-start(f32[144,128]{1,0:T(8,128)S(1)} %pad_maximum_fusion.refs_0_), channel_id=1, source_target_pairs={{0,1},{1,0},{2,3},{3,2},{4,5},{5,4},{6,7},{7,6},{8,9},{9,8},{10,11... | collective-permute-start | bytes 221192 | tf_op jit(solution)/shard_map/ppermute | solution.py:27

commit v9 on v8

--- a/solution.py
+++ b/solution.py
@@ -97,7 +97,7 @@
 def filter_kernel(
     count_ref, links_ref, snap_ref, after_ref, before_ref, old_ref, oldgram_ref, s_ref, *rest
 ):
-    keep_ref, give_ref, packed = rest
+    chunk_refs, packed = rest[:SPREAD], rest[SPREAD]
     rows, planes, rows_y, rows_z = snap_ref.shape
     count = count_ref[0]
     join_low = links_ref[0, 0].astype(jnp.float32)
@@ -160,9 +160,7 @@
     height = packed.shape[0] // SPREAD
     for flip in range(SPREAD):
         at = pl.multiple_of((share ^ flip) * height, SUBS)
-        side = give_ref if flip % 2 else keep_ref
-        part = flip // 2 * height
-        side[part:part + height, :] = packed[pl.ds(at, height), :]
+        chunk_refs[flip][...] = packed[pl.ds(at, height), :]
 
 
 def filtered_rows(snapshots, before, after, plane_counts, links, s_old, old_gram):
@@ -172,12 +170,12 @@
     height = packed_rows(order)
     smem = pl.BlockSpec(memory_space=pltpu.SMEM)
     vmem = pl.BlockSpec(memory_space=pltpu.VMEM)
-    half = jax.ShapeDtypeStruct((height // 2, LANES), jnp.float32)
+    chunk = jax.ShapeDtypeStruct((height // SPREAD, LANES), jnp.float32)
     return pl.pallas_call(
         filter_kernel,
-        out_shape=[jax.ShapeDtypeStruct((planes * rows_y // 2, rows, 2 * rows_z), jnp.bfloat16)] + [half] * 2,
+        out_shape=[jax.ShapeDtypeStruct((planes * rows_y // 2, rows, 2 * rows_z), jnp.bfloat16)] + [chunk] * SPREAD,
         in_specs=[smem, smem] + [vmem] * 5,
-        out_specs=[vmem] * 3,
+        out_specs=[vmem] * (1 + SPREAD),
         scratch_shapes=[pltpu.VMEM((height, LANES), jnp.float32)],
         compiler_params=pltpu.CompilerParams(vmem_limit_bytes=VMEM_BYTES),
         cost_estimate=pl.CostEstimate(
@@ -187,17 +185,20 @@
     )(plane_counts, links, snapshots, after, before, s_old, old_gram)
 
 
-def sum_shares(keep, give, axis):
+def sum_chunks(chunks, axis):
     peers = lax.axis_size(axis)
-    height = keep.shape[0] // 2
-    both = keep + swap(give, axis, 1)
-    total = both[:height] + swap(both[height:], axis, 2)
+    arrived = [chunks[0]] + [swap(chunks[d], axis, d) for d in range(1, SPREAD)]
+    total = (arrived[0] + arrived[1]) + (arrived[2] + arrived[3])
     step = SPREAD
     while step < peers:
-        total = total + swap(total, axis, step)
-        step *= 2
-    both = jnp.concatenate([total, swap(total, axis, 2)], axis=0)
-    return both, swap(both, axis, 1)
+        if step * 4 <= peers:
+            one, two, three = (swap(total, axis, d * step) for d in (1, 2, 3))
+            total = (total + one) + (two + three)
+            step *= 4
+        else:
+            total = total + swap(total, axis, step)
+            step *= 2
+    return [total] + [swap(total, axis, d) for d in range(1, SPREAD)]
 
 
 def split_three(x):
@@ -210,24 +211,6 @@
 
 LEFT = (0, 0, 0, 1, 1, 2)
 RIGHT = (0, 1, 2, 0, 1, 0)
-
-
-def eliminate_all(panel, low, t_ref, wide):
-    tiles, order, _ = t_ref.shape
-    first = panel * PANEL
-    tile = jnp.maximum(panel, 0) // (LANES // PANEL)
-    left = split_three(t_ref[tile, low:, :])
-    left = jnp.concatenate([left[k] for k in LEFT], axis=1)
-    update = jnp.dot(left, wide[lax.rem(panel + 2, 2)], preferred_element_type=jnp.float32)
-    row = lax.broadcasted_iota(jnp.int32, (order - low, LANES), 0) + low
-    lane = lax.broadcasted_iota(jnp.int32, (order - low, LANES), 1)
-    below = row >= first + 2 * PANEL
-    for s in range(tiles):
-        column = lane + s * LANES
-        mine = (column >= first) & (column < first + PANEL)
-        held = t_ref[s, low:, :]
-        fresh = jnp.where(mine, 0.0, held) - update[:, s * LANES:(s + 1) * LANES]
-        t_ref[s, low:, :] = jnp.where(below, fresh, held)
 
 
 def small_factor(entry, count):
@@ -270,35 +253,64 @@
     return unit, recip + more
 
 
-def factor_panel(panel, low, t_ref, f_ref, x_ref, cols, rows, wide, narrow):
-    tiles, order, _ = t_ref.shape
-    first = pl.multiple_of(panel * PANEL, PANEL)
-    tile = panel // (LANES // PANEL)
-    off = pl.multiple_of(first - tile * LANES, PANEL)
-    here = pl.ds(first, PANEL)
-    lane = lax.broadcasted_iota(jnp.int32, (PANEL, LANES), 1)
-    sub = lax.broadcasted_iota(jnp.int32, (PANEL, LANES), 0)
-    own = t_ref[tile, here, :]
-    turn = lax.rem(LANES - off, LANES)
-    turned = pltpu.roll(own, turn, axis=1)
-    for j in range(PANEL):
-        cols[j] = jnp.broadcast_to(turned[:, j:j + 1], (PANEL, LANES))
-    for s in range(tiles):
-        column = lane + s * LANES
-        inside = (column >= first) & (column < first + PANEL)
-        unit_rows = jnp.where(column - first == sub, 1.0, 0.0)
-        rows[pl.ds(s, PANEL, stride=SUBS), :] = jnp.where(inside, unit_rows, t_ref[s, here, :])
-    rows[pl.ds(tiles, PANEL, stride=SUBS), :] = own
-    y = [rows[i * SUBS:(i + 1) * SUBS, :] for i in range(PANEL)]
-    eliminate_all(panel - 1, low, t_ref, wide)
-    after = jnp.minimum(first + PANEL, order - PANEL)
-    after = pl.ds(pl.multiple_of(after, PANEL), PANEL)
-    ahead = pltpu.roll(t_ref[tile, after, :], turn, axis=1)
-    pieces = [jnp.where(lane < PANEL, piece.astype(jnp.float32), 0.0) for piece in split_three(ahead)]
+def left_pieces(panel, t_ref, low, high):
+    off = panel * PANEL % LANES
+    block = t_ref[panel * PANEL // LANES, low:high, :]
+    lane = lax.broadcasted_iota(jnp.int32, block.shape, 1)
+    block = jnp.where((lane >= off) & (lane < off + PANEL), block, 0.0)
+    pieces = [piece.astype(jnp.float32) for piece in split_three(block)]
     left = pieces[LEFT[0]]
     for k in range(1, len(LEFT)):
         left = left + pltpu.roll(pieces[LEFT[k]], k * PANEL, axis=1)
-    left = left.astype(jnp.bfloat16)
+    return left.astype(jnp.bfloat16)
+
+
+def right_pieces(panel, v):
+    pieces = split_three(v)
+    empty = jnp.zeros(v.shape, jnp.bfloat16)
+    slots = [empty] * (LANES // PANEL)
+    for k in range(len(RIGHT)):
+        slots[(panel + k) % len(slots)] = pieces[RIGHT[k]]
+    return jnp.concatenate(slots, axis=0)
+
+
+def subtract(panel, t_ref, low, high, left, right):
+    update = jnp.dot(left, right, preferred_element_type=jnp.float32)
+    off = panel * PANEL % LANES
+    for s in range(t_ref.shape[0]):
+        held = t_ref[s, low:high, :]
+        if s == panel * PANEL // LANES:
+            lane = lax.broadcasted_iota(jnp.int32, held.shape, 1)
+            held = jnp.where((lane >= off) & (lane < off + PANEL), 0.0, held)
+        t_ref[s, low:high, :] = held - update[:, s * LANES:(s + 1) * LANES]
+
+
+def factor_panel(panel, t_ref, f_ref, x_ref, cols, rows, late):
+    tiles, order, _ = t_ref.shape
+    first = panel * PANEL
+    end = first + PANEL
+    tile, off = first // LANES, first % LANES
+    rows_in, rows_v, rows_w = (rows.at[panel % 2, k] for k in range(3))
+    cols = cols.at[panel % 2]
+    lane = lax.broadcasted_iota(jnp.int32, (PANEL, LANES), 1)
+    sub = lax.broadcasted_iota(jnp.int32, (PANEL, LANES), 0)
+    inside = (lane >= off) & (lane < off + PANEL)
+    own = t_ref[tile, first:end, :]
+    for j in range(PANEL):
+        cols[j] = jnp.broadcast_to(own[:, off + j:off + j + 1], (PANEL, LANES))
+    for s in range(tiles):
+        block = t_ref[s, first:end, :]
+        if s == tile:
+            block = jnp.where(inside, jnp.where(lane - off == sub, 1.0, 0.0), block)
+        rows_in[pl.ds(s, PANEL, stride=SUBS), :] = block
+    rows_in[pl.ds(tiles, PANEL, stride=SUBS), :] = own
+    y = [rows_in[i * SUBS:(i + 1) * SUBS, :] for i in range(PANEL)]
+    late()
+    near = min(end + PANEL, order)
+    if end < order:
+        left_near = left_pieces(panel, t_ref, end, near)
+    if near < order:
+        left_far = left_pieces(panel, t_ref, near, order)
 
     unit, recip = pivots(cols)
     for k in range(PANEL):
@@ -308,44 +320,42 @@
     for j in reversed(range(PANEL)):
         for i in range(j):
             v[i] = v[i] - unit[j][i] * v[j]
-    for i in range(PANEL):
-        rows[i * SUBS:(i + 1) * SUBS, :] = v[i]
-    v = jnp.concatenate([rows[pl.ds(s, PANEL, stride=SUBS), :] for s in range(tiles)], axis=1)
-    v = split_three(v)
-    for k in range(len(RIGHT)):
-        narrow[k * PANEL:(k + 1) * PANEL, :] = v[RIGHT[k]]
-    update = jnp.dot(left, narrow[...], preferred_element_type=jnp.float32)
-    more = first + PANEL < order
-    for s in range(tiles):
-        column = lane + s * LANES
-        mine = (column >= first) & (column < first + PANEL)
-        held = t_ref[s, after, :]
-        fresh = jnp.where(mine, 0.0, held) - update[:, s * LANES:(s + 1) * LANES]
-        t_ref[s, after, :] = jnp.where(more, fresh, held)
-    side = lax.rem(panel, 2)
-    old_off = lax.rem(off + LANES - 2 * PANEL, LANES)
-    for k in range(len(RIGHT)):
-        old_at = pl.multiple_of(old_off + k * LANES, PANEL)
-        wide[side, pl.ds(old_at, PANEL), :] = jnp.zeros((PANEL, order), jnp.bfloat16)
-        at = pl.multiple_of(off + k * LANES, PANEL)
-        wide[side, pl.ds(at, PANEL), :] = v[RIGHT[k]]
-
-    for i in range(PANEL):
-        rows[i * SUBS:(i + 1) * SUBS, :] = jnp.sqrt(recip[i]) * y[i]
-    whole = rows[pl.ds(tiles, PANEL, stride=SUBS), :]
-    for s in range(tiles):
-        span = slice(s * LANES, (s + 1) * LANES)
-        column = lane + s * LANES
-        part = rows[pl.ds(s, PANEL, stride=SUBS), :]
-        inside = (column >= first) & (column < first + PANEL)
-        f_ref[here, span] = jnp.where(column >= first + sub, jnp.where(inside, whole, part), 0.0)
-        x_ref[here, span] = jnp.where(column <= first + sub, part, 0.0)
+    if end < order:
+        for i in range(PANEL):
+            rows_v[i * SUBS:(i + 1) * SUBS, :] = v[i]
+        right = jnp.concatenate(
+            [rows_v[pl.ds(s, PANEL, stride=SUBS), :] for s in range(tiles)], axis=1
+        )
+        right = right_pieces(panel, right)
+        subtract(panel, t_ref, end, near, left_near, right)
+
+    def rest():
+        if near < order:
+            subtract(panel, t_ref, near, order, left_far, right)
+
+    def outputs():
+        for i in range(PANEL):
+            rows_w[i * SUBS:(i + 1) * SUBS, :] = jnp.sqrt(recip[i]) * y[i]
+        zero = jnp.zeros((PANEL, LANES), jnp.float32)
+        for s in range(tiles):
+            span = slice(s * LANES, (s + 1) * LANES)
+            part = rows_w[pl.ds(s, PANEL, stride=SUBS), :]
+            if s == tile:
+                whole = rows_w[pl.ds(tiles, PANEL, stride=SUBS), :]
+                upper = jnp.where(inside, whole, part)
+                f_ref[first:end, span] = jnp.where(lane >= off + sub, upper, 0.0)
+                x_ref[first:end, span] = jnp.where(lane <= off + sub, part, 0.0)
+            else:
+                f_ref[first:end, span] = part if s > tile else zero
+                x_ref[first:end, span] = part if s < tile else zero
+
+    return rest, outputs
 
 
 def factor_kernel(scale, *refs):
-    sum_refs, refs = refs[:2], refs[2:]
+    sum_refs, refs = refs[:SPREAD], refs[SPREAD:]
     new_ref, old_ref, f_ref, out_ref, packed, t_ref, x_ref, cols, rows, *refs = refs
-    wide, narrow, x_pair, stack, mixed, staged, in_sem, out_sem = refs
+    x_pair, stack, mixed, staged, in_sem, out_sem = refs
     tiles, order, _ = t_ref.shape
     _, planes, rows_y, rows_z = out_ref.shape
     new_count = new_ref.shape[1]
@@ -359,8 +369,7 @@
     height = packed.shape[0] // SPREAD
     for flip in range(SPREAD):
         at = pl.multiple_of((share ^ flip) * height, SUBS)
-        part = flip // 2 * height
-        packed[pl.ds(at, height), :] = sum_refs[flip % 2][part:part + height, :] * scale
+        packed[pl.ds(at, height), :] = sum_refs[flip][...] * scale
     i = lax.broadcasted_iota(jnp.int32, (LANES, LANES), 0)
     j = lax.broadcasted_iota(jnp.int32, (LANES, LANES), 1)
     shared = packed[:LANES, :]
@@ -373,8 +382,6 @@
     t_ref[0, LANES:, :] = right.T
     corner = jnp.where(j < i, shared, lower.T)
     t_ref[1, LANES:, :] = jnp.where(i == j, diagonal, corner)
-    wide[...] = jnp.zeros(wide.shape, wide.dtype)
-    narrow[...] = jnp.zeros(narrow.shape, narrow.dtype)
     rows[...] = jnp.zeros(rows.shape, jnp.float32)
 
     turn = turn_matrix(rows_y, 0.0)
@@ -386,54 +393,58 @@
     def split_rows(group):
         rows_here = x_ref[group * GROUP:(group + 1) * GROUP, :]
         high = rows_here.astype(jnp.bfloat16)
-        x_pair[:GROUP, :] = high
-        x_pair[GROUP:, :] = (rows_here - high.astype(jnp.float32)).astype(jnp.bfloat16)
+        x_pair[group % 2, :GROUP, :] = high
+        x_pair[group % 2, GROUP:, :] = (rows_here - high.astype(jnp.float32)).astype(jnp.bfloat16)
 
     def multiply(group, pair):
         depth = (group + 1) * GROUP
         sums = jnp.dot(
-            x_pair[:, :depth], stack[pair, :depth, :], preferred_element_type=jnp.float32
+            x_pair[group % 2, :, :depth], stack[pair, :depth, :], preferred_element_type=jnp.float32
         )
         sums = (sums[:GROUP] + sums[GROUP:]).astype(jnp.bfloat16)
         sums = sums.reshape(GROUP // rows_y, rows_y, 2 * rows_z)
         some = slice(group * GROUP // rows_y, (group + 1) * GROUP // rows_y)
         for half in (0, 1):
             y = 2 * (pair % steps) + half
-            at = pl.ds(pl.multiple_of(y * rows_y, rows_y), rows_y)
+            at = slice(y * rows_y, (y + 1) * rows_y)
             mixed[pair // steps, some, at, :] = sums[:, :, half * rows_z:(half + 1) * rows_z]
 
     def store(some):
-        at = pl.ds(pl.multiple_of(some * rows_y, rows_y), rows_y)
+        at = pl.ds(some * rows_y, rows_y)
         return pltpu.make_async_copy(staged.at[at], out_ref.at[at], out_sem.at[some])
 
     def finish(some):
         block = jnp.concatenate([mixed[plane, some] for plane in range(planes)], axis=1)
         turned = jnp.dot(turn, block, preferred_element_type=jnp.float32).astype(jnp.bfloat16)
-        at = pl.ds(pl.multiple_of(some * rows_y, rows_y), rows_y)
         for plane in range(planes):
             part = turned[:, plane * rows_z:(plane + 1) * rows_z]
-            staged[at, plane] = part.reshape(rows_y, rows_y, rows_z)
+            staged[some * rows_y:(some + 1) * rows_y, plane] = part.reshape(rows_y, rows_y, rows_z)
         store(some).start()
 
     groups = order // GROUP
     blocks = GROUP // rows_y
+
+    def nothing():
+        pass
+
+    late, outputs = nothing, nothing
     for group in range(groups):
         if group == 1:
             load_new.wait()
             load_old.wait()
-        if group > 0:
-            split_rows(group - 1)
-
-        @pl.loop(0, per_group)
-        def _(step):
+        for step in range(per_group):
             panel = group * per_group + step
-            factor_panel(panel, group * GROUP, t_ref, f_ref, x_ref, cols, rows, wide, narrow)
+            before = outputs
+            late, outputs = factor_panel(panel, t_ref, f_ref, x_ref, cols, rows, late)
+            before()
             if group > 0:
+                if step == 0:
+                    split_rows(group - 1)
                 for k in range(per_panel):
                     multiply(group - 1, step * per_panel + k)
             if group > 1:
                 finish((group - 2) * blocks + step)
-
+    outputs()
     split_rows(groups - 1)
     for k in range(blocks):
         finish((groups - 2) * blocks + k)
@@ -442,14 +453,13 @@
     for k in range(blocks):
         finish((groups - 1) * blocks + k)
 
-    @pl.loop(0, order // rows_y)
-    def _(some):
+    for some in range(order // rows_y):
         store(some).wait()
 
 
 def factor_and_modes(sums, s_new, s_old, shape, cell_total):
     order, planes, rows_y, rows_z = shape
-    height = sums[0].shape[0] * 2
+    height = sums[0].shape[0] * SPREAD
     vmem = pl.BlockSpec(memory_space=pltpu.VMEM)
     hbm = pl.BlockSpec(memory_space=pl.ANY)
     square = (order, order)
@@ -460,17 +470,15 @@
             jax.ShapeDtypeStruct(square, jnp.float32),
             jax.ShapeDtypeStruct(shape, jnp.bfloat16),
         ],
-        in_specs=[vmem] * 2 + [hbm, hbm],
+        in_specs=[vmem] * SPREAD + [hbm, hbm],
         out_specs=[vmem, hbm],
         scratch_shapes=[
             pltpu.VMEM((height, LANES), jnp.float32),
             pltpu.VMEM((order // LANES, order, LANES), jnp.float32),
             pltpu.VMEM(square, jnp.float32),
-            pltpu.VMEM((PANEL, PANEL, LANES), jnp.float32),
-            pltpu.VMEM((PANEL * SUBS, LANES), jnp.float32),
-            pltpu.VMEM((2, len(LEFT) * LANES, order), jnp.bfloat16),
-            pltpu.VMEM((LANES, order), jnp.bfloat16),
-            pltpu.VMEM((2 * GROUP, order), jnp.bfloat16),
+            pltpu.VMEM((2, PANEL, PANEL, LANES), jnp.float32),
+            pltpu.VMEM((2, 3, PANEL * SUBS, LANES), jnp.float32),
+            pltpu.VMEM((2, 2 * GROUP, order), jnp.bfloat16),
             pltpu.VMEM((pairs, order, 2 * rows_z), jnp.bfloat16),
             pltpu.VMEM((planes, order // rows_y, rows_y * rows_y, rows_z), jnp.bfloat16),
             pltpu.VMEM(shape, jnp.bfloat16),
@@ -493,10 +501,10 @@
     before = lax.ppermute(last, "blk", up)
     after = lax.ppermute(first, "blk", down)
     s_old, old_gram = scaled_rows(old_modes, mode_scales, plane_counts)
-    s_new, keep, give = filtered_rows(
+    s_new, *chunks = filtered_rows(
         snapshots, before, after, plane_counts, links, s_old, old_gram
     )
-    sums = sum_shares(keep, give, "blk")
+    sums = sum_chunks(chunks, "blk")
     factor, modes = factor_and_modes(
         sums, s_new, s_old, (order, planes, rows_y, rows_z), peers * planes * rows_y * rows_z
     )

time: 52.4 us -> 43.5 us (0.83)
  waiting for transfers between devices: 16.9 us -> 8.46 us
  Pallas kernels: 20.4 us -> 14.6 us
  starting transfers between devices: 10.2 us -> 15.5 us
    ppermute x6 -> x9, waiting for transfers between devices: 16.8 us -> 8.41 us  [swap(): return lax.ppermute(x, axis, [(i, i ^ flip) for i in range(peers)])]
    pallas_call x1, Pallas kernels: 15.7 us -> 10 us  [factor_and_modes(): pl.pallas_call(functools.partial(factor_kernel, 1.0 / cell_total), out_sh...]
    ppermute x6 -> x9, starting transfers between devices: 4.68 us -> 9.94 us  [swap(): return lax.ppermute(x, axis, [(i, i ^ flip) for i in range(peers)])]
  transfers between devices with their start and end apart: 8 -> 11, of which waited for: 6 -> 5; matrix products, arithmetic and copies ran while one was open for 2% -> 2% of each run, Pallas kernels for 4% -> 4%
where the time goes in v9:
time: 43.5 us; the launch traced here: 43.3 us
  starting transfers between devices  15.5 us (36%)
  Pallas kernels  14.6 us (34%)
  waiting for transfers between devices  8.46 us (19%)
  local copies, waits for them, and re-layouts  3.28 us (8%)
  between operations  1.41 us (3%)
    pallas_call x1, Pallas kernels, factor_and_modes(): pl.pallas_call(functools.partial(factor_kernel, 1.0 / cell_total), out_sh...  10 us
    ppermute x9, starting transfers between devices, swap(): return lax.ppermute(x, axis, [(i, i ^ flip) for i in range(peers)])  9.94 us
    ppermute x9, waiting for transfers between devices, swap(): return lax.ppermute(x, axis, [(i, i ^ flip) for i in range(peers)])  8.41 us
    ppermute x1, starting transfers between devices, shards(): after = lax.ppermute(first, 'blk', down)  5.03 us
    pallas_call x1, Pallas kernels, filtered_rows(): pl.pallas_call(filter_kernel, out_shape=[jax.ShapeDtypeStruct((planes * r...  2.82 us
    pallas_call x1, Pallas kernels, scaled_rows(): pl.pallas_call(scale_kernel, out_shape=[jax.ShapeDtypeStruct((planes * ro...  1.83 us
    unnamed x6, local copies, waits for them, and re-layouts  1.41 us
    dynamic_slice x1, local copies, waits for them, and re-layouts, shards(): last = lax.dynamic_slice_in_dim(snapshots, plane_counts[0] - 1, 1, axis=1)  1.07 us
  transfers between devices with their start and end apart: 11, of which 5 were waited for; matrix products, arithmetic and copies ran while one was open for 2% of the time, Pallas kernels for 4%

profile of v9, /device:TPU:0, one launch (start us, length us, event | category | flops | bytes accessed | tf_op | source)
XLA Modules:
  0.0 43.3 jit_solution(12928889128612227515)
XLA Ops:
  0.6 0.0 copy-start
  0.6 0.0 copy-start.2
  1.4 1.1 %constant_dynamic-slice_fusion = (bf16[64,1,16,128]{3,2,1,0:T(8,128)(2,1)S(1)}, bf16[64,1,16,128]{3,2,1,0:T(8,128)(2,1)S(1)}) fusion(bf16[64,2,16,128]{3,2,1,0:T(8,128)(2,1)} %snap_ref.1, s32[]{:T(128)S(6)} %select_n.3), kind=kLoop, calls=%fused_computation.2 | loop fusion | bytes 1048580 | tf_op jit(solution)/shard_map/dynamic_slice | solution.py:500
  2.4 0.5 %collective-permute-start.1 = (bf16[64,1,16,128]{3,2,1,0:T(8,128)(2,1)S(1)}, bf16[64,1,16,128]{3,2,1,0:T(8,128)(2,1)S(1)}, u32[]{:S(2)}, u32[]{:S(2)}) collective-permute-start(bf16[64,1,16,128]{3,2,1,0:T(8,128)(2,1)S(1)} %get-tuple-element.20), channel_id=1, source_target_pairs={{0,1},{1,2},{2,3},{3,4},{4,5},{5,6},{6,7},{7,8},{8,9},{9,10},{10,1... | collective-permute-start | bytes 786440 | tf_op jit(solution)/shard_map/ppermute | solution.py:501
  2.9 5.0 %collective-permute-start = (bf16[64,1,16,128]{3,2,1,0:T(8,128)(2,1)S(1)}, bf16[64,1,16,128]{3,2,1,0:T(8,128)(2,1)S(1)}, u32[]{:S(2)}, u32[]{:S(2)}) collective-permute-start(bf16[64,1,16,128]{3,2,1,0:T(8,128)(2,1)S(1)} %get-tuple-element.21), channel_id=1, source_target_pairs={{1,0},{2,1},{3,2},{4,3},{5,4},{6,5},{7,6},{8,7},{9,8},{10,9},{11,1... | collective-permute-start | bytes 786440 | tf_op jit(solution)/shard_map/ppermute | solution.py:502
  8.0 0.8 %copy.7.scales_ref = f32[192,1]{1,0:T(8,128)S(1)} copy(f32[192,1]{0,1:T(1,128)} %bitcast.3) | data formatting | bytes 1536 | tf_op jit(solution)/shard_map/reshape | solution.py:89
  8.8 0.0 copy-start.1
  8.8 1.4 %copy-done.1 = bf16[192,2,16,128]{3,2,1,0:T(8,128)(2,1)S(1)} copy-done((bf16[192,2,16,128]{3,2,1,0:T(8,128)(2,1)S(1)}, bf16[192,2,16,128]{3,2,1,0:T(8,128)(2,1)}, u32[]{:S(2)}) %copy-start.1) | copy-done | bytes 1572888
  10.2 1.8 %scale_gram.1 = (bf16[16,192,256]{2,1,0:T(8,128)(2,1)S(1)}, f32[192,192]{1,0:T(8,128)S(1)}) custom-call(s32[1]{0:T(128)S(6)} %copy.8.count_ref, f32[192,1]{1,0:T(8,128)S(1)} %copy.7.scales_ref, bf16[192,2,16,128]{3,2,1,0:T(8,128)(2,1)S(1)} %copy-done.1), custom_call_target="tpu_custom_call" | custom-call | flops 301989888 | bytes 6291456 | tf_op jit(solution)/shard_map/scale_gram/pallas_call | solution.py:76
  12.0 0.1 collective-permute-done.1.before_ref
  12.1 0.0 collective-permute-done.after_ref
  12.1 0.0 copy-done
  12.1 0.0 copy-done.2
  12.1 2.8 %filter_gram.1 = (bf16[16,64,256]{2,1,0:T(8,128)(2,1)S(1)}, f32[72,128]{1,0:T(8,128)S(1)}, f32[72,128]{1,0:T(8,128)S(1)}, f32[72,128]{1,0:T(8,128)S(1)}, f32[72,128]{1,0:T(8,128)S(1)}) custom-call(s32[1]{0:T(128)S(6)} %copy.8.count_ref, s32[1,2]{1,0:T(1,128)S(1)} %copy-done.2, bf16[64,2,16,128]{3,2,1,0:T(8,128)(2,1)S(1)} %copy-done, ...), custom_call_target="tpu_custom_call" | custom-call | flops 134217728 | bytes 2097152 | tf_op jit(solution)/shard_map/filter_gram/pallas_call | solution.py:174
  14.9 2.1 %collective-permute-start.2 = (f32[72,128]{1,0:T(8,128)S(1)}, f32[72,128]{1,0:T(8,128)S(1)}, u32[]{:S(2)}, u32[]{:S(2)}) collective-permute-start(f32[72,128]{1,0:T(8,128)S(1)} %get-tuple-element.14), channel_id=1, source_target_pairs={{0,1},{1,0},{2,3},{3,2},{4,5},{5,4},{6,7},{7,6},{8,9},{9,8},{10,11... | collective-permute-start | bytes 110600 | tf_op jit(solution)/shard_map/ppermute | solution.py:27
  17.0 0.0 collective-permute-start.3
  17.0 1.4 %collective-permute-start.4 = (f32[72,128]{1,0:T(8,128)S(1)}, f32[72,128]{1,0:T(8,128)S(1)}, u32[]{:S(2)}, u32[]{:S(2)}) collective-permute-start(f32[72,128]{1,0:T(8,128)S(1)} %get-tuple-element.16), channel_id=1, source_target_pairs={{0,3},{1,2},{2,1},{3,0},{4,7},{5,6},{6,5},{7,4},{8,11},{9,10},{10,... | collective-permute-start | bytes 110600 | tf_op jit(solution)/shard_map/ppermute | solution.py:27
  18.5 0.0 collective-permute-done.2
  18.5 2.5 %collective-permute-done.3 = f32[72,128]{1,0:T(8,128)S(1)} collective-permute-done((f32[72,128]{1,0:T(8,128)S(1)}, f32[72,128]{1,0:T(8,128)S(1)}, u32[]{:S(2)}, u32[]{:S(2)}) %collective-permute-start.3) | collective-permute-done | bytes 36896 | tf_op jit(solution)/shard_map/ppermute | solution.py:27
  21.0 0.0 collective-permute-done.4
  21.0 3.2 %collective-permute-start.7 = (f32[72,128]{1,0:T(8,128)S(1)}, f32[72,128]{1,0:T(8,128)S(1)}, u32[]{:S(2)}, u32[]{:S(2)}) collective-permute-start(f32[72,128]{1,0:T(8,128)S(1)} %add_add_fusion.1), channel_id=1, source_target_pairs={{0,12},{1,13},{2,14},{3,15},{4,8},{5,9},{6,10},{7,11},{8,4},{9,5},... | collective-permute-start | bytes 110600 | tf_op jit(solution)/shard_map/ppermute | solution.py:27
  24.2 0.0 collective-permute-start.6
  24.2 1.3 %collective-permute-start.5 = (f32[72,128]{1,0:T(8,128)S(1)}, f32[72,128]{1,0:T(8,128)S(1)}, u32[]{:S(2)}, u32[]{:S(2)}) collective-permute-start(f32[72,128]{1,0:T(8,128)S(1)} %add_add_fusion.1), channel_id=1, source_target_pairs={{0,4},{1,5},{2,6},{3,7},{4,0},{5,1},{6,2},{7,3},{8,12},{9,13},{10,... | collective-permute-start | bytes 110600 | tf_op jit(solution)/shard_map/ppermute | solution.py:27
  25.5 1.6 %collective-permute-done.7 = f32[72,128]{1,0:T(8,128)S(1)} collective-permute-done((f32[72,128]{1,0:T(8,128)S(1)}, f32[72,128]{1,0:T(8,128)S(1)}, u32[]{:S(2)}, u32[]{:S(2)}) %collective-permute-start.7) | collective-permute-done | bytes 36896 | tf_op jit(solution)/shard_map/ppermute | solution.py:27
  27.0 2.0 %collective-permute-done.6 = f32[72,128]{1,0:T(8,128)S(1)} collective-permute-done((f32[72,128]{1,0:T(8,128)S(1)}, f32[72,128]{1,0:T(8,128)S(1)}, u32[]{:S(2)}, u32[]{:S(2)}) %collective-permute-start.6) | collective-permute-done | bytes 36896 | tf_op jit(solution)/shard_map/ppermute | solution.py:27
  29.1 0.0 collective-permute-done.5
  29.1 0.1 collective-permute-start.10
  29.2 1.4 %collective-permute-start.9 = (f32[72,128]{1,0:T(8,128)S(1)}, f32[72,128]{1,0:T(8,128)S(1)}, u32[]{:S(2)}, u32[]{:S(2)}) collective-permute-start(f32[72,128]{1,0:T(8,128)S(1)} %add_add_fusion.refs_0_), channel_id=1, source_target_pairs={{0,2},{1,3},{2,0},{3,1},{4,6},{5,7},{6,4},{7,5},{8,10},{9,11},{10,... | collective-permute-start | bytes 110600 | tf_op jit(solution)/shard_map/ppermute | solution.py:27
  30.6 0.4 collective-permute-start.8
  31.0 1.9 %collective-permute-done.10.refs_3_ = f32[72,128]{1,0:T(8,128)S(1)} collective-permute-done((f32[72,128]{1,0:T(8,128)S(1)}, f32[72,128]{1,0:T(8,128)S(1)}, u32[]{:S(2)}, u32[]{:S(2)}) %collective-permute-start.10) | collective-permute-done | bytes 36896 | tf_op jit(solution)/shard_map/ppermute | solution.py:27
  32.9 0.4 collective-permute-done.9.refs_2_
  33.3 0.0 collective-permute-done.8.refs_1_
  33.3 10.0 %factor.1 = (f32[256,256]{1,0:T(8,128)}, bf16[256,2,16,128]{3,2,1,0:T(8,128)(2,1)}) custom-call(f32[72,128]{1,0:T(8,128)S(1)} %add_add_fusion.refs_0_, f32[72,128]{1,0:T(8,128)S(1)} %collective-permute-done.8.refs_1_, f32[72,128]{1,0:T(8,128)S(1)} %collective-permute-done.9.refs_2_, f32[72,128]{1,0:T(8,128)S(1)} %collective-permute-done.10.refs_3_, ...), custom_call_target="tpu_custom_call" | custom-call | tf_op jit(solution)/shard_map/factor/pallas_call | solution.py:467
  (2 shorter events, 0.0 us)
Async XLA Ops:
  0.6 11.4 %copy-start = (bf16[64,2,16,128]{3,2,1,0:T(8,128)(2,1)S(1)}, bf16[64,2,16,128]{3,2,1,0:T(8,128)(2,1)}, u32[]{:S(2)}) copy-start(bf16[64,2,16,128]{3,2,1,0:T(8,128)(2,1)} %snap_ref.1) | copy-start | bytes 1572868
  0.6 11.4 %copy-start.2 = (s32[1,2]{1,0:T(1,128)S(1)}, s32[1,2]{1,0:T(1,128)}, u32[]{:S(2)}) copy-start(s32[1,2]{1,0:T(1,128)} %links_ref.1) | copy-start | bytes 28
  2.4 9.6 %collective-permute-start.1 = (bf16[64,1,16,128]{3,2,1,0:T(8,128)(2,1)S(1)}, bf16[64,1,16,128]{3,2,1,0:T(8,128)(2,1)S(1)}, u32[]{:S(2)}, u32[]{:S(2)}) collective-permute-start(bf16[64,1,16,128]{3,2,1,0:T(8,128)(2,1)S(1)} %get-tuple-element.20), channel_id=1, source_target_pairs={{0,1},{1,2},{2,3},{3,4},{4,5},{5,6},{6,7},{7,8},{8,9},{9,10},{10,1... | collective-permute-start | bytes 786440 | tf_op jit(solution)/shard_map/ppermute | solution.py:501
  2.9 9.1 %collective-permute-start = (bf16[64,1,16,128]{3,2,1,0:T(8,128)(2,1)S(1)}, bf16[64,1,16,128]{3,2,1,0:T(8,128)(2,1)S(1)}, u32[]{:S(2)}, u32[]{:S(2)}) collective-permute-start(bf16[64,1,16,128]{3,2,1,0:T(8,128)(2,1)S(1)} %get-tuple-element.21), channel_id=1, source_target_pairs={{1,0},{2,1},{3,2},{4,3},{5,4},{6,5},{7,6},{8,7},{9,8},{10,9},{11,1... | collective-permute-start | bytes 786440 | tf_op jit(solution)/shard_map/ppermute | solution.py:502
  8.8 1.4 %copy-start.1 = (bf16[192,2,16,128]{3,2,1,0:T(8,128)(2,1)S(1)}, bf16[192,2,16,128]{3,2,1,0:T(8,128)(2,1)}, u32[]{:S(2)}) copy-start(bf16[192,2,16,128]{3,2,1,0:T(8,128)(2,1)} %old_ref.1) | copy-start | bytes 4718596
  14.9 3.6 %collective-permute-start.2 = (f32[72,128]{1,0:T(8,128)S(1)}, f32[72,128]{1,0:T(8,128)S(1)}, u32[]{:S(2)}, u32[]{:S(2)}) collective-permute-start(f32[72,128]{1,0:T(8,128)S(1)} %get-tuple-element.14), channel_id=1, source_target_pairs={{0,1},{1,0},{2,3},{3,2},{4,5},{5,4},{6,7},{7,6},{8,9},{9,8},{10,11... | collective-permute-start | bytes 110600 | tf_op jit(solution)/shard_map/ppermute | solution.py:27
  17.0 4.0 %collective-permute-start.3 = (f32[72,128]{1,0:T(8,128)S(1)}, f32[72,128]{1,0:T(8,128)S(1)}, u32[]{:S(2)}, u32[]{:S(2)}) collective-permute-start(f32[72,128]{1,0:T(8,128)S(1)} %get-tuple-element.15), channel_id=1, source_target_pairs={{0,2},{1,3},{2,0},{3,1},{4,6},{5,7},{6,4},{7,5},{8,10},{9,11},{10,... | collective-permute-start | bytes 110600 | tf_op jit(solution)/shard_map/ppermute | solution.py:27
  17.0 4.0 %collective-permute-start.4 = (f32[72,128]{1,0:T(8,128)S(1)}, f32[72,128]{1,0:T(8,128)S(1)}, u32[]{:S(2)}, u32[]{:S(2)}) collective-permute-start(f32[72,128]{1,0:T(8,128)S(1)} %get-tuple-element.16), channel_id=1, source_target_pairs={{0,3},{1,2},{2,1},{3,0},{4,7},{5,6},{6,5},{7,4},{8,11},{9,10},{10,... | collective-permute-start | bytes 110600 | tf_op jit(solution)/shard_map/ppermute | solution.py:27
  21.0 6.0 %collective-permute-start.7 = (f32[72,128]{1,0:T(8,128)S(1)}, f32[72,128]{1,0:T(8,128)S(1)}, u32[]{:S(2)}, u32[]{:S(2)}) collective-permute-start(f32[72,128]{1,0:T(8,128)S(1)} %add_add_fusion.1), channel_id=1, source_target_pairs={{0,12},{1,13},{2,14},{3,15},{4,8},{5,9},{6,10},{7,11},{8,4},{9,5},... | collective-permute-start | bytes 110600 | tf_op jit(solution)/shard_map/ppermute | solution.py:27
  24.2 4.9 %collective-permute-start.6 = (f32[72,128]{1,0:T(8,128)S(1)}, f32[72,128]{1,0:T(8,128)S(1)}, u32[]{:S(2)}, u32[]{:S(2)}) collective-permute-start(f32[72,128]{1,0:T(8,128)S(1)} %add_add_fusion.1), channel_id=1, source_target_pairs={{0,8},{1,9},{2,10},{3,11},{4,12},{5,13},{6,14},{7,15},{8,0},{9,1},... | collective-permute-start | bytes 110600 | tf_op jit(solution)/shard_map/ppermute | solution.py:27
  24.2 4.9 %collective-permute-start.5 = (f32[72,128]{1,0:T(8,128)S(1)}, f32[72,128]{1,0:T(8,128)S(1)}, u32[]{:S(2)}, u32[]{:S(2)}) collective-permute-start(f32[72,128]{1,0:T(8,128)S(1)} %add_add_fusion.1), channel_id=1, source_target_pairs={{0,4},{1,5},{2,6},{3,7},{4,0},{5,1},{6,2},{7,3},{8,12},{9,13},{10,... | collective-permute-start | bytes 110600 | tf_op jit(solution)/shard_map/ppermute | solution.py:27
  29.1 3.8 %collective-permute-start.10 = (f32[72,128]{1,0:T(8,128)S(1)}, f32[72,128]{1,0:T(8,128)S(1)}, u32[]{:S(2)}, u32[]{:S(2)}) collective-permute-start(f32[72,128]{1,0:T(8,128)S(1)} %add_add_fusion.refs_0_), channel_id=1, source_target_pairs={{0,3},{1,2},{2,1},{3,0},{4,7},{5,6},{6,5},{7,4},{8,11},{9,10},{10,... | collective-permute-start | bytes 110600 | tf_op jit(solution)/shard_map/ppermute | solution.py:27
  29.2 4.1 %collective-permute-start.9 = (f32[72,128]{1,0:T(8,128)S(1)}, f32[72,128]{1,0:T(8,128)S(1)}, u32[]{:S(2)}, u32[]{:S(2)}) collective-permute-start(f32[72,128]{1,0:T(8,128)S(1)} %add_add_fusion.refs_0_), channel_id=1, source_target_pairs={{0,2},{1,3},{2,0},{3,1},{4,6},{5,7},{6,4},{7,5},{8,10},{9,11},{10,... | collective-permute-start | bytes 110600 | tf_op jit(solution)/shard_map/ppermute | solution.py:27
  30.6 2.7 %collective-permute-start.8 = (f32[72,128]{1,0:T(8,128)S(1)}, f32[72,128]{1,0:T(8,128)S(1)}, u32[]{:S(2)}, u32[]{:S(2)}) collective-permute-start(f32[72,128]{1,0:T(8,128)S(1)} %add_add_fusion.refs_0_), channel_id=1, source_target_pairs={{0,1},{1,0},{2,3},{3,2},{4,5},{5,4},{6,7},{7,6},{8,9},{9,8},{10,11... | collective-permute-start | bytes 110600 | tf_op jit(solution)/shard_map/ppermute | solution.py:27

commit v10 on v9

--- a/solution.py
+++ b/solution.py
@@ -47,11 +47,83 @@
             s_ref[(plane * rows_y + y) // 2, at, half:half + LANES] = part
 
 
-def scale_kernel(count_ref, scales_ref, old_ref, s_ref, gram_ref):
+def edge_kernel(count_ref, snap_ref, first_ref, last_ref):
+    rows, planes, rows_y, rows_z = snap_ref.shape
+    count = count_ref[0]
+    for row in range(rows):
+        first_ref[row, 0] = snap_ref[row, 0]
+        last = snap_ref[row, 0]
+        for p in range(1, planes):
+            last = jnp.where(count > p, snap_ref[row, p], last)
+        last_ref[row, 0] = last
+
+
+def edge_planes(snapshots, plane_counts):
+    rows, _, rows_y, rows_z = snapshots.shape
+    smem = pl.BlockSpec(memory_space=pltpu.SMEM)
+    vmem = pl.BlockSpec(memory_space=pltpu.VMEM)
+    plane = jax.ShapeDtypeStruct((rows, 1, rows_y, rows_z), jnp.bfloat16)
+    return pl.pallas_call(
+        edge_kernel,
+        out_shape=[plane, plane],
+        in_specs=[smem, vmem],
+        out_specs=[vmem, vmem],
+        compiler_params=pltpu.CompilerParams(vmem_limit_bytes=VMEM_BYTES),
+        name="edges",
+    )(plane_counts, snapshots)
+
+
+def plane_weights(table_ref, planes, rows_z):
+    count = table_ref[0]
+    join_low = table_ref[1].astype(jnp.float32)
+    join_high = table_ref[2].astype(jnp.float32)
+    z_from = lax.broadcasted_iota(jnp.int32, (rows_z, rows_z), 0)
+    z_to = lax.broadcasted_iota(jnp.int32, (rows_z, rows_z), 1)
+    gap = jnp.abs(z_from - z_to)
+    smooth_z = jnp.where(gap == 0, 0.5, jnp.where(gap == 1, 0.25, 0.0))
+    inner = [[0.0] * planes for _ in range(planes)]
+    outer = [[0.0] * planes for _ in range(2)]
+    for p in range(planes):
+        alive = jnp.where(p < count, 1.0, 0.0)
+        is_last = jnp.where(p == count - 1, 1.0, 0.0)
+        inner[p][p] = 0.5 * alive
+        if p > 0:
+            inner[p - 1][p] = 0.25 * alive
+        else:
+            outer[0][p] = 0.25 * alive * join_low
+        if p < planes - 1:
+            inner[p + 1][p] = 0.25 * alive * (1.0 - is_last)
+        outer[1][p] = 0.25 * is_last * join_high
+
+    def matrix(weights):
+        lines = [[(smooth_z * w).astype(jnp.bfloat16) for w in line] for line in weights]
+        return jnp.concatenate([jnp.concatenate(line, axis=1) for line in lines], axis=0)
+
+    return matrix(inner), matrix(outer)
+
+
+def smoothed(planes_by_lane, weights, turn):
+    field = jnp.dot(planes_by_lane, weights, preferred_element_type=jnp.float32)
+    high = field.astype(jnp.bfloat16)
+    low = (field - high.astype(jnp.float32)).astype(jnp.bfloat16)
+    turned = jnp.dot(turn, high, preferred_element_type=jnp.float32)
+    return turned + jnp.dot(turn, low, preferred_element_type=jnp.float32)
+
+
+def scale_kernel(
+    table_ref, scales_ref, old_ref, snap_ref,
+    s_ref, gram_ref, inner_ref, outer_ref, turn_ref,
+):
     rows, planes, rows_y, rows_z = old_ref.shape
     turn = turn_matrix(rows_y, 0.0)
     plane = lax.broadcasted_iota(jnp.int32, (rows_y, planes * rows_z), 1) // rows_z
-    alive = jnp.where(plane < count_ref[0], 1.0, 0.0)
+    alive = jnp.where(plane < table_ref[0], 1.0, 0.0)
+    scales = []
+    for low in range(0, rows, LANES):
+        some = scales_ref[:, low:min(low + LANES, rows)]
+        scales.append(jnp.broadcast_to(some, (LANES, some.shape[1])).T)
+    scales = jnp.concatenate(scales, axis=0)
+    scales = jnp.concatenate([scales] * planes, axis=1)
 
     for group in range(rows // rows_y):
         at = slice(group * rows_y, (group + 1) * rows_y)
@@ -60,17 +132,29 @@
             [block[:, p].reshape(rows_y * rows_y, rows_z) for p in range(planes)], axis=1
         )
         turned = jnp.dot(turn, block, preferred_element_type=jnp.float32)
-        weight = scales_ref[at, :] * alive
+        weight = scales[at] * alive
         turned = turned.reshape(rows_y, rows_y, planes * rows_z) * weight[None]
         turned = turned.reshape(rows_y * rows_y, planes * rows_z).astype(jnp.bfloat16)
         place(turned, s_ref, rows_y, at)
 
     gram_ref[...] = sum(nt_dot(s_ref[k], s_ref[k]) for k in range(s_ref.shape[0]))
 
-
-def scaled_rows(old_modes, mode_scales, plane_counts):
+    inner, outer = plane_weights(table_ref, planes, rows_z)
+    turn = turn_matrix(rows_y, 0.25)
+    outer_ref[...] = outer
+    turn_ref[...] = turn
+    for group in range(snap_ref.shape[0] // rows_y):
+        snap = snap_ref[group * rows_y:(group + 1) * rows_y]
+        sources = [snap[:, p].reshape(rows_y * rows_y, rows_z) for p in range(planes)]
+        inner_ref[group] = smoothed(jnp.concatenate(sources, axis=1), inner, turn)
+
+
+def prepared_rows(old_modes, snapshots, mode_scales, plane_counts, links):
     rows, planes, rows_y, rows_z = old_modes.shape
+    table = jnp.concatenate([plane_counts, links.reshape(-1)])
     cells = planes * rows_y * rows_z
+    groups = snapshots.shape[0] // rows_y
+    square = rows_y * rows_y
     smem = pl.BlockSpec(memory_space=pltpu.SMEM)
     vmem = pl.BlockSpec(memory_space=pltpu.VMEM)
     return pl.pallas_call(
@@ -78,15 +162,18 @@
         out_shape=[
             jax.ShapeDtypeStruct((planes * rows_y // 2, rows, 2 * rows_z), jnp.bfloat16),
             jax.ShapeDtypeStruct((rows, rows), jnp.float32),
+            jax.ShapeDtypeStruct((groups, square, planes * rows_z), jnp.float32),
+            jax.ShapeDtypeStruct((2 * rows_z, planes * rows_z), jnp.bfloat16),
+            jax.ShapeDtypeStruct((square, square), jnp.bfloat16),
         ],
-        in_specs=[smem, vmem, vmem],
-        out_specs=[vmem, vmem],
+        in_specs=[smem, vmem, vmem, vmem],
+        out_specs=[vmem] * 5,
         compiler_params=pltpu.CompilerParams(vmem_limit_bytes=VMEM_BYTES),
         cost_estimate=pl.CostEstimate(
             flops=2 * rows * rows * cells, bytes_accessed=8 * rows * cells, transcendentals=0
         ),
-        name="scale_gram",
-    )(plane_counts, mode_scales.reshape(rows, 1), old_modes)
+        name="prepare",
+    )(table, mode_scales.reshape(1, rows), old_modes, snapshots)
 
 
 def packed_rows(order):
@@ -95,47 +182,15 @@
 
 
 def filter_kernel(
-    count_ref, links_ref, snap_ref, after_ref, before_ref, old_ref, oldgram_ref, s_ref, *rest
+    before_ref, after_ref, inner_ref, outer_ref, turn_ref, old_ref, oldgram_ref, s_ref, *rest
 ):
     chunk_refs, packed = rest[:SPREAD], rest[SPREAD]
-    rows, planes, rows_y, rows_z = snap_ref.shape
-    count = count_ref[0]
-    join_low = links_ref[0, 0].astype(jnp.float32)
-    join_high = links_ref[0, 1].astype(jnp.float32)
-    z_from = lax.broadcasted_iota(jnp.int32, (rows_z, rows_z), 0)
-    z_to = lax.broadcasted_iota(jnp.int32, (rows_z, rows_z), 1)
-    gap = jnp.abs(z_from - z_to)
-    smooth_z = jnp.where(gap == 0, 0.5, jnp.where(gap == 1, 0.25, 0.0))
-    nothing = jnp.zeros((rows_z, rows_z), jnp.bfloat16)
-    blocks = [[nothing] * planes for _ in range(planes + 2)]
-    for p in range(planes):
-        alive = jnp.where(p < count, 1.0, 0.0)
-        is_last = jnp.where(p == count - 1, 1.0, 0.0)
-        behind = alive * join_low if p == 0 else alive
-        blocks[p][p] = (smooth_z * (0.25 * behind)).astype(jnp.bfloat16)
-        blocks[p + 1][p] = (smooth_z * (0.5 * alive)).astype(jnp.bfloat16)
-        if p < planes - 1:
-            inner = 0.25 * alive * (1.0 - is_last)
-            blocks[p + 2][p] = (smooth_z * inner).astype(jnp.bfloat16)
-            blocks[planes + 1][p] = (smooth_z * (0.25 * is_last * join_high)).astype(jnp.bfloat16)
-        else:
-            blocks[planes + 1][p] = (smooth_z * (0.25 * alive * join_high)).astype(jnp.bfloat16)
-    weights = jnp.concatenate([jnp.concatenate(line, axis=1) for line in blocks], axis=0)
-    turn = turn_matrix(rows_y, 0.25)
-
+    rows, _, rows_y, rows_z = before_ref.shape
     for group in range(rows // rows_y):
         at = slice(group * rows_y, (group + 1) * rows_y)
-        snap = snap_ref[at]
-        sources = [before_ref[at][:, 0]] + [snap[:, p] for p in range(planes)] + [after_ref[at][:, 0]]
-        sources = [x.reshape(rows_y * rows_y, rows_z) for x in sources]
-        field = jnp.dot(
-            jnp.concatenate(sources, axis=1), weights, preferred_element_type=jnp.float32
-        )
-        high = field.astype(jnp.bfloat16)
-        low = (field - high.astype(jnp.float32)).astype(jnp.bfloat16)
-        turned = jnp.dot(turn, high, preferred_element_type=jnp.float32)
-        turned = turned + jnp.dot(turn, low, preferred_element_type=jnp.float32)
-        place(turned.astype(jnp.bfloat16), s_ref, rows_y, at)
+        sources = [x[at][:, 0].reshape(rows_y * rows_y, rows_z) for x in (before_ref, after_ref)]
+        halo = smoothed(jnp.concatenate(sources, axis=1), outer_ref[...], turn_ref[...])
+        place((inner_ref[group] + halo).astype(jnp.bfloat16), s_ref, rows_y, at)
 
     pairs = range(s_ref.shape[0])
     new_new = sum(nt_dot(s_ref[k], s_ref[k]) for k in pairs)
@@ -163,26 +218,27 @@
         chunk_refs[flip][...] = packed[pl.ds(at, height), :]
 
 
-def filtered_rows(snapshots, before, after, plane_counts, links, s_old, old_gram):
-    rows, planes, rows_y, rows_z = snapshots.shape
-    cells = planes * rows_y * rows_z
-    order = rows + s_old.shape[1]
+def filtered_rows(before, after, inner, outer, turn, s_old, old_gram):
+    rows = before.shape[0]
+    pairs, old_rows, lanes = s_old.shape
+    order = rows + old_rows
     height = packed_rows(order)
-    smem = pl.BlockSpec(memory_space=pltpu.SMEM)
     vmem = pl.BlockSpec(memory_space=pltpu.VMEM)
     chunk = jax.ShapeDtypeStruct((height // SPREAD, LANES), jnp.float32)
     return pl.pallas_call(
         filter_kernel,
-        out_shape=[jax.ShapeDtypeStruct((planes * rows_y // 2, rows, 2 * rows_z), jnp.bfloat16)] + [chunk] * SPREAD,
-        in_specs=[smem, smem] + [vmem] * 5,
+        out_shape=[jax.ShapeDtypeStruct((pairs, rows, lanes), jnp.bfloat16)] + [chunk] * SPREAD,
+        in_specs=[vmem] * 7,
         out_specs=[vmem] * (1 + SPREAD),
         scratch_shapes=[pltpu.VMEM((height, LANES), jnp.float32)],
         compiler_params=pltpu.CompilerParams(vmem_limit_bytes=VMEM_BYTES),
         cost_estimate=pl.CostEstimate(
-            flops=2 * rows * order * cells, bytes_accessed=2 * order * cells, transcendentals=0
+            flops=2 * rows * order * pairs * lanes,
+            bytes_accessed=2 * order * pairs * lanes,
+            transcendentals=0,
         ),
         name="filter_gram",
-    )(plane_counts, links, snapshots, after, before, s_old, old_gram)
+    )(before, after, inner, outer, turn, s_old, old_gram)
 
 
 def sum_chunks(chunks, axis):
@@ -496,14 +552,13 @@
     peers = lax.axis_size("blk")
     up = [(i, (i + 1) % peers) for i in range(peers)]
     down = [(j, i) for i, j in up]
-    first = lax.slice_in_dim(snapshots, 0, 1, axis=1)
-    last = lax.dynamic_slice_in_dim(snapshots, plane_counts[0] - 1, 1, axis=1)
+    first, last = edge_planes(snapshots, plane_counts)
     before = lax.ppermute(last, "blk", up)
     after = lax.ppermute(first, "blk", down)
-    s_old, old_gram = scaled_rows(old_modes, mode_scales, plane_counts)
-    s_new, *chunks = filtered_rows(
-        snapshots, before, after, plane_counts, links, s_old, old_gram
+    s_old, old_gram, inner, outer, turn = prepared_rows(
+        old_modes, snapshots, mode_scales, plane_counts, links
     )
+    s_new, *chunks = filtered_rows(before, after, inner, outer, turn, s_old, old_gram)
     sums = sum_chunks(chunks, "blk")
     factor, modes = factor_and_modes(
         sums, s_new, s_old, (order, planes, rows_y, rows_z), peers * planes * rows_y * rows_z

time: 43.5 us -> 42.7 us (0.982)
  starting transfers between devices: 15.5 us -> 14.3 us
  other arithmetic: 0.02 us -> 0.75 us
    unnamed x6, local copies, waits for them, and re-layouts: 1.41 us -> 3.12 us
    ppermute x9, starting transfers between devices: 9.94 us -> 8.75 us  [swap(): return lax.ppermute(x, axis, [(i, i ^ flip) for i in range(peers)])]
    dynamic_slice x1 -> x0, local copies, waits for them, and re-layouts: 1.07 us -> none  [shards(): last = lax.dynamic_slice_in_dim(snapshots, plane_counts[0] - 1, 1, axis=1)]
    reshape x1 -> x0, local copies, waits for them, and re-layouts: 0.79 us -> none  [scaled_rows(): mode_scales.reshape(rows, 1)]
    concatenate x0 -> x1, other arithmetic: none -> 0.73 us  [prepared_rows(): table = jnp.concatenate([plane_counts, links.reshape(-1)])]
    pallas_call x2 -> x3, Pallas kernels: 4.65 us -> 4.56 us  [the longest x1 2.44 us: prepared_rows(): pl.pallas_call(scale_kernel, out_shape=[jax.ShapeDtypeStruct((planes * ro...]
  transfers between devices with their start and end apart: 11 -> 11, of which waited for: 5 -> 5; matrix products, arithmetic and copies ran while one was open for 2% -> 2% of each run, Pallas kernels for 4% -> 6%
where the time goes in v10:
time: 42.7 us; the launch traced here: 42.5 us
  Pallas kernels  14.6 us (34%)
  starting transfers between devices  14.3 us (33%)
  waiting for transfers between devices  8.42 us (20%)
  local copies, waits for them, and re-layouts  3.12 us (7%)
  between operations  1.34 us (3%)
  other arithmetic  0.75 us (2%)
    pallas_call x1, Pallas kernels, factor_and_modes(): pl.pallas_call(functools.partial(factor_kernel, 1.0 / cell_total), out_sh...  10 us
    ppermute x9, starting transfers between devices, swap(): return lax.ppermute(x, axis, [(i, i ^ flip) for i in range(peers)])  8.75 us
    ppermute x9, waiting for transfers between devices, swap(): return lax.ppermute(x, axis, [(i, i ^ flip) for i in range(peers)])  8.42 us
    ppermute x1, starting transfers between devices, shards(): after = lax.ppermute(first, 'blk', down)  5.03 us
    unnamed x6, local copies, waits for them, and re-layouts  3.12 us
    pallas_call x1, Pallas kernels, prepared_rows(): pl.pallas_call(scale_kernel, out_shape=[jax.ShapeDtypeStruct((planes * ro...  2.44 us
    pallas_call x1, Pallas kernels, filtered_rows(): pl.pallas_call(filter_kernel, out_shape=[jax.ShapeDtypeStruct((pairs, row...  2.03 us
  transfers between devices with their start and end apart: 11, of which 5 were waited for; matrix products, arithmetic and copies ran while one was open for 2% of the time, Pallas kernels for 6%

profile of v10, /device:TPU:0, one launch (start us, length us, event | category | flops | bytes accessed | tf_op | source)
XLA Modules:
  0.0 42.5 jit_solution(3980233994259963946)
XLA Ops:
  1.3 0.0 copy-start
  1.3 1.0 %copy-done = bf16[64,2,16,128]{3,2,1,0:T(8,128)(2,1)S(1)} copy-done((bf16[64,2,16,128]{3,2,1,0:T(8,128)(2,1)S(1)}, bf16[64,2,16,128]{3,2,1,0:T(8,128)(2,1)}, u32[]{:S(2)}) %copy-start) | copy-done | bytes 524312
  2.3 0.1 edges.1
  2.4 0.5 %collective-permute-start = (bf16[64,1,16,128]{3,2,1,0:T(8,128)(2,1)S(1)}, bf16[64,1,16,128]{3,2,1,0:T(8,128)(2,1)S(1)}, u32[]{:S(2)}, u32[]{:S(2)}) collective-permute-start(bf16[64,1,16,128]{3,2,1,0:T(8,128)(2,1)S(1)} %get-tuple-element.16), channel_id=1, source_target_pairs={{0,1},{1,2},{2,3},{3,4},{4,5},{5,6},{6,7},{7,8},{8,9},{9,10},{10,1... | collective-permute-start | bytes 786440 | tf_op jit(solution)/shard_map/ppermute | solution.py:556
  2.9 5.0 %collective-permute-start.1 = (bf16[64,1,16,128]{3,2,1,0:T(8,128)(2,1)S(1)}, bf16[64,1,16,128]{3,2,1,0:T(8,128)(2,1)S(1)}, u32[]{:S(2)}, u32[]{:S(2)}) collective-permute-start(bf16[64,1,16,128]{3,2,1,0:T(8,128)(2,1)S(1)} %get-tuple-element.17), channel_id=1, source_target_pairs={{1,0},{2,1},{3,2},{4,3},{5,4},{6,5},{7,6},{8,7},{9,8},{10,9},{11,1... | collective-permute-start | bytes 786440 | tf_op jit(solution)/shard_map/ppermute | solution.py:557
  7.9 0.7 %pad_add_fusion.table_ref = s32[3]{0:T(128)S(1)} fusion(s32[2]{0:T(128)} %bitcast.3, s32[1]{0:T(128)S(6)} %copy.7.count_ref), kind=kLoop, calls=%fused_computation.2 | loop fusion | flops 3 | bytes 24 | tf_op jit(solution)/shard_map/concatenate | solution.py:154
  8.7 0.0 copy-start.1
  8.7 1.4 %copy-done.1 = bf16[192,2,16,128]{3,2,1,0:T(8,128)(2,1)S(1)} copy-done((bf16[192,2,16,128]{3,2,1,0:T(8,128)(2,1)S(1)}, bf16[192,2,16,128]{3,2,1,0:T(8,128)(2,1)}, u32[]{:S(2)}) %copy-start.1) | copy-done | bytes 1572888
  10.1 0.0 copy-start.2
  10.1 0.7 %copy-done.2 = f32[192]{0:T(256)S(1)} copy-done((f32[192]{0:T(256)S(1)}, f32[192]{0:T(256)}, u32[]{:S(2)}) %copy-start.2) | copy-done | bytes 792
  10.8 2.4 %prepare.1 = (bf16[16,192,256]{2,1,0:T(8,128)(2,1)S(1)}, f32[192,192]{1,0:T(8,128)S(1)}, f32[4,256,256]{2,1,0:T(8,128)S(1)}, bf16[256,256]{1,0:T(8,128)(2,1)S(1)}, bf16[256,256]{1,0:T(8,128)(2,1)S(1)}) custom-call(s32[3]{0:T(128)S(1)} %pad_add_fusion.table_ref, f32[1,192]{1,0:T(1,128)S(1)} %bitcast.2, bf16[192,2,16,128]{3,2,1,0:T(8,128)(2,1)S(1)} %copy-done.1, ...), custom_call_target="tpu_custom_call" | custom-call | flops 301989888 | bytes 6291456 | tf_op jit(solution)/shard_map/prepare/pallas_call | solution.py:160
  13.2 0.0 collective-permute-done.before_ref
  13.2 0.0 collective-permute-done.1.after_ref
  13.2 2.0 %filter_gram.1 = (bf16[16,64,256]{2,1,0:T(8,128)(2,1)S(1)}, f32[72,128]{1,0:T(8,128)S(1)}, f32[72,128]{1,0:T(8,128)S(1)}, f32[72,128]{1,0:T(8,128)S(1)}, f32[72,128]{1,0:T(8,128)S(1)}) custom-call(bf16[64,1,16,128]{3,2,1,0:T(8,128)(2,1)S(1)} %collective-permute-done.before_ref, bf16[64,1,16,128]{3,2,1,0:T(8,128)(2,1)S(1)} %collective-permute-done.1.after_ref, ...), custom_call_target="tpu_custom_call" | custom-call | flops 134217728 | bytes 2097152 | tf_op jit(solution)/shard_map/filter_gram/pallas_call | solution.py:228
  15.3 0.9 %collective-permute-start.2 = (f32[72,128]{1,0:T(8,128)S(1)}, f32[72,128]{1,0:T(8,128)S(1)}, u32[]{:S(2)}, u32[]{:S(2)}) collective-permute-start(f32[72,128]{1,0:T(8,128)S(1)} %get-tuple-element.24), channel_id=1, source_target_pairs={{0,1},{1,0},{2,3},{3,2},{4,5},{5,4},{6,7},{7,6},{8,9},{9,8},{10,11... | collective-permute-start | bytes 110600 | tf_op jit(solution)/shard_map/ppermute | solution.py:27
  16.2 0.0 collective-permute-start.3
  16.2 1.4 %collective-permute-start.4 = (f32[72,128]{1,0:T(8,128)S(1)}, f32[72,128]{1,0:T(8,128)S(1)}, u32[]{:S(2)}, u32[]{:S(2)}) collective-permute-start(f32[72,128]{1,0:T(8,128)S(1)} %get-tuple-element.26), channel_id=1, source_target_pairs={{0,3},{1,2},{2,1},{3,0},{4,7},{5,6},{6,5},{7,4},{8,11},{9,10},{10,... | collective-permute-start | bytes 110600 | tf_op jit(solution)/shard_map/ppermute | solution.py:27
  17.6 0.0 collective-permute-done.2
  17.6 2.5 %collective-permute-done.3 = f32[72,128]{1,0:T(8,128)S(1)} collective-permute-done((f32[72,128]{1,0:T(8,128)S(1)}, f32[72,128]{1,0:T(8,128)S(1)}, u32[]{:S(2)}, u32[]{:S(2)}) %collective-permute-start.3) | collective-permute-done | bytes 36896 | tf_op jit(solution)/shard_map/ppermute | solution.py:27
  20.2 0.0 collective-permute-done.4
  20.2 3.2 %collective-permute-start.7 = (f32[72,128]{1,0:T(8,128)S(1)}, f32[72,128]{1,0:T(8,128)S(1)}, u32[]{:S(2)}, u32[]{:S(2)}) collective-permute-start(f32[72,128]{1,0:T(8,128)S(1)} %add_add_fusion.1), channel_id=1, source_target_pairs={{0,12},{1,13},{2,14},{3,15},{4,8},{5,9},{6,10},{7,11},{8,4},{9,5},... | collective-permute-start | bytes 110600 | tf_op jit(solution)/shard_map/ppermute | solution.py:27
  23.4 0.0 collective-permute-start.6
  23.4 1.3 %collective-permute-start.5 = (f32[72,128]{1,0:T(8,128)S(1)}, f32[72,128]{1,0:T(8,128)S(1)}, u32[]{:S(2)}, u32[]{:S(2)}) collective-permute-start(f32[72,128]{1,0:T(8,128)S(1)} %add_add_fusion.1), channel_id=1, source_target_pairs={{0,4},{1,5},{2,6},{3,7},{4,0},{5,1},{6,2},{7,3},{8,12},{9,13},{10,... | collective-permute-start | bytes 110600 | tf_op jit(solution)/shard_map/ppermute | solution.py:27
  24.6 1.6 %collective-permute-done.7 = f32[72,128]{1,0:T(8,128)S(1)} collective-permute-done((f32[72,128]{1,0:T(8,128)S(1)}, f32[72,128]{1,0:T(8,128)S(1)}, u32[]{:S(2)}, u32[]{:S(2)}) %collective-permute-start.7) | collective-permute-done | bytes 36896 | tf_op jit(solution)/shard_map/ppermute | solution.py:27
  26.2 2.0 %collective-permute-done.6 = f32[72,128]{1,0:T(8,128)S(1)} collective-permute-done((f32[72,128]{1,0:T(8,128)S(1)}, f32[72,128]{1,0:T(8,128)S(1)}, u32[]{:S(2)}, u32[]{:S(2)}) %collective-permute-start.6) | collective-permute-done | bytes 36896 | tf_op jit(solution)/shard_map/ppermute | solution.py:27
  28.2 0.0 collective-permute-done.5
  28.3 0.1 collective-permute-start.10
  28.4 1.4 %collective-permute-start.9 = (f32[72,128]{1,0:T(8,128)S(1)}, f32[72,128]{1,0:T(8,128)S(1)}, u32[]{:S(2)}, u32[]{:S(2)}) collective-permute-start(f32[72,128]{1,0:T(8,128)S(1)} %add_add_fusion.refs_0_), channel_id=1, source_target_pairs={{0,2},{1,3},{2,0},{3,1},{4,6},{5,7},{6,4},{7,5},{8,10},{9,11},{10,... | collective-permute-start | bytes 110600 | tf_op jit(solution)/shard_map/ppermute | solution.py:27
  29.8 0.4 collective-permute-start.8
  30.2 1.9 %collective-permute-done.10.refs_3_ = f32[72,128]{1,0:T(8,128)S(1)} collective-permute-done((f32[72,128]{1,0:T(8,128)S(1)}, f32[72,128]{1,0:T(8,128)S(1)}, u32[]{:S(2)}, u32[]{:S(2)}) %collective-permute-start.10) | collective-permute-done | bytes 36896 | tf_op jit(solution)/shard_map/ppermute | solution.py:27
  32.1 0.4 collective-permute-done.9.refs_2_
  32.5 0.0 collective-permute-done.8.refs_1_
  32.5 10.0 %factor.1 = (f32[256,256]{1,0:T(8,128)}, bf16[256,2,16,128]{3,2,1,0:T(8,128)(2,1)}) custom-call(f32[72,128]{1,0:T(8,128)S(1)} %add_add_fusion.refs_0_, f32[72,128]{1,0:T(8,128)S(1)} %collective-permute-done.8.refs_1_, f32[72,128]{1,0:T(8,128)S(1)} %collective-permute-done.9.refs_2_, f32[72,128]{1,0:T(8,128)S(1)} %collective-permute-done.10.refs_3_, ...), custom_call_target="tpu_custom_call" | custom-call | tf_op jit(solution)/shard_map/factor/pallas_call | solution.py:523
  (2 shorter events, 0.0 us)
Async XLA Ops:
  1.3 1.0 %copy-start = (bf16[64,2,16,128]{3,2,1,0:T(8,128)(2,1)S(1)}, bf16[64,2,16,128]{3,2,1,0:T(8,128)(2,1)}, u32[]{:S(2)}) copy-start(bf16[64,2,16,128]{3,2,1,0:T(8,128)(2,1)} %snap_ref.3) | copy-start | bytes 1572868
  2.4 10.8 %collective-permute-start = (bf16[64,1,16,128]{3,2,1,0:T(8,128)(2,1)S(1)}, bf16[64,1,16,128]{3,2,1,0:T(8,128)(2,1)S(1)}, u32[]{:S(2)}, u32[]{:S(2)}) collective-permute-start(bf16[64,1,16,128]{3,2,1,0:T(8,128)(2,1)S(1)} %get-tuple-element.16), channel_id=1, source_target_pairs={{0,1},{1,2},{2,3},{3,4},{4,5},{5,6},{6,7},{7,8},{8,9},{9,10},{10,1... | collective-permute-start | bytes 786440 | tf_op jit(solution)/shard_map/ppermute | solution.py:556
  2.9 10.3 %collective-permute-start.1 = (bf16[64,1,16,128]{3,2,1,0:T(8,128)(2,1)S(1)}, bf16[64,1,16,128]{3,2,1,0:T(8,128)(2,1)S(1)}, u32[]{:S(2)}, u32[]{:S(2)}) collective-permute-start(bf16[64,1,16,128]{3,2,1,0:T(8,128)(2,1)S(1)} %get-tuple-element.17), channel_id=1, source_target_pairs={{1,0},{2,1},{3,2},{4,3},{5,4},{6,5},{7,6},{8,7},{9,8},{10,9},{11,1... | collective-permute-start | bytes 786440 | tf_op jit(solution)/shard_map/ppermute | solution.py:557
  8.7 1.4 %copy-start.1 = (bf16[192,2,16,128]{3,2,1,0:T(8,128)(2,1)S(1)}, bf16[192,2,16,128]{3,2,1,0:T(8,128)(2,1)}, u32[]{:S(2)}) copy-start(bf16[192,2,16,128]{3,2,1,0:T(8,128)(2,1)} %old_ref.1) | copy-start | bytes 4718596
  10.1 0.7 %copy-start.2 = (f32[192]{0:T(256)S(1)}, f32[192]{0:T(256)}, u32[]{:S(2)}) copy-start(f32[192]{0:T(256)} %param.7) | copy-start | bytes 2308
  15.3 2.4 %collective-permute-start.2 = (f32[72,128]{1,0:T(8,128)S(1)}, f32[72,128]{1,0:T(8,128)S(1)}, u32[]{:S(2)}, u32[]{:S(2)}) collective-permute-start(f32[72,128]{1,0:T(8,128)S(1)} %get-tuple-element.24), channel_id=1, source_target_pairs={{0,1},{1,0},{2,3},{3,2},{4,5},{5,4},{6,7},{7,6},{8,9},{9,8},{10,11... | collective-permute-start | bytes 110600 | tf_op jit(solution)/shard_map/ppermute | solution.py:27
  16.2 4.0 %collective-permute-start.3 = (f32[72,128]{1,0:T(8,128)S(1)}, f32[72,128]{1,0:T(8,128)S(1)}, u32[]{:S(2)}, u32[]{:S(2)}) collective-permute-start(f32[72,128]{1,0:T(8,128)S(1)} %get-tuple-element.25), channel_id=1, source_target_pairs={{0,2},{1,3},{2,0},{3,1},{4,6},{5,7},{6,4},{7,5},{8,10},{9,11},{10,... | collective-permute-start | bytes 110600 | tf_op jit(solution)/shard_map/ppermute | solution.py:27
  16.2 4.0 %collective-permute-start.4 = (f32[72,128]{1,0:T(8,128)S(1)}, f32[72,128]{1,0:T(8,128)S(1)}, u32[]{:S(2)}, u32[]{:S(2)}) collective-permute-start(f32[72,128]{1,0:T(8,128)S(1)} %get-tuple-element.26), channel_id=1, source_target_pairs={{0,3},{1,2},{2,1},{3,0},{4,7},{5,6},{6,5},{7,4},{8,11},{9,10},{10,... | collective-permute-start | bytes 110600 | tf_op jit(solution)/shard_map/ppermute | solution.py:27
  20.2 6.0 %collective-permute-start.7 = (f32[72,128]{1,0:T(8,128)S(1)}, f32[72,128]{1,0:T(8,128)S(1)}, u32[]{:S(2)}, u32[]{:S(2)}) collective-permute-start(f32[72,128]{1,0:T(8,128)S(1)} %add_add_fusion.1), channel_id=1, source_target_pairs={{0,12},{1,13},{2,14},{3,15},{4,8},{5,9},{6,10},{7,11},{8,4},{9,5},... | collective-permute-start | bytes 110600 | tf_op jit(solution)/shard_map/ppermute | solution.py:27
  23.4 4.9 %collective-permute-start.6 = (f32[72,128]{1,0:T(8,128)S(1)}, f32[72,128]{1,0:T(8,128)S(1)}, u32[]{:S(2)}, u32[]{:S(2)}) collective-permute-start(f32[72,128]{1,0:T(8,128)S(1)} %add_add_fusion.1), channel_id=1, source_target_pairs={{0,8},{1,9},{2,10},{3,11},{4,12},{5,13},{6,14},{7,15},{8,0},{9,1},... | collective-permute-start | bytes 110600 | tf_op jit(solution)/shard_map/ppermute | solution.py:27
  23.4 4.9 %collective-permute-start.5 = (f32[72,128]{1,0:T(8,128)S(1)}, f32[72,128]{1,0:T(8,128)S(1)}, u32[]{:S(2)}, u32[]{:S(2)}) collective-permute-start(f32[72,128]{1,0:T(8,128)S(1)} %add_add_fusion.1), channel_id=1, source_target_pairs={{0,4},{1,5},{2,6},{3,7},{4,0},{5,1},{6,2},{7,3},{8,12},{9,13},{10,... | collective-permute-start | bytes 110600 | tf_op jit(solution)/shard_map/ppermute | solution.py:27
  28.3 3.8 %collective-permute-start.10 = (f32[72,128]{1,0:T(8,128)S(1)}, f32[72,128]{1,0:T(8,128)S(1)}, u32[]{:S(2)}, u32[]{:S(2)}) collective-permute-start(f32[72,128]{1,0:T(8,128)S(1)} %add_add_fusion.refs_0_), channel_id=1, source_target_pairs={{0,3},{1,2},{2,1},{3,0},{4,7},{5,6},{6,5},{7,4},{8,11},{9,10},{10,... | collective-permute-start | bytes 110600 | tf_op jit(solution)/shard_map/ppermute | solution.py:27
  28.4 4.1 %collective-permute-start.9 = (f32[72,128]{1,0:T(8,128)S(1)}, f32[72,128]{1,0:T(8,128)S(1)}, u32[]{:S(2)}, u32[]{:S(2)}) collective-permute-start(f32[72,128]{1,0:T(8,128)S(1)} %add_add_fusion.refs_0_), channel_id=1, source_target_pairs={{0,2},{1,3},{2,0},{3,1},{4,6},{5,7},{6,4},{7,5},{8,10},{9,11},{10,... | collective-permute-start | bytes 110600 | tf_op jit(solution)/shard_map/ppermute | solution.py:27
  29.8 2.7 %collective-permute-start.8 = (f32[72,128]{1,0:T(8,128)S(1)}, f32[72,128]{1,0:T(8,128)S(1)}, u32[]{:S(2)}, u32[]{:S(2)}) collective-permute-start(f32[72,128]{1,0:T(8,128)S(1)} %add_add_fusion.refs_0_), channel_id=1, source_target_pairs={{0,1},{1,0},{2,3},{3,2},{4,5},{5,4},{6,7},{7,6},{8,9},{9,8},{10,11... | collective-permute-start | bytes 110600 | tf_op jit(solution)/shard_map/ppermute | solution.py:27

commit v11 on v10

--- a/solution.py
+++ b/solution.py
@@ -7,9 +7,9 @@
 from jax.experimental.pallas import tpu as pltpu
 from jax.sharding import PartitionSpec as P
 
-PANEL = 16
-HALF = 8
-GROUP = 64
+PANEL = 32
+BLOCK = 8
+GROUPS = (64, 64, 64, 32, 32)
 LANES = 128
 SUBS = 8
 SPREAD = 4
@@ -184,7 +184,7 @@
 def filter_kernel(
     before_ref, after_ref, inner_ref, outer_ref, turn_ref, old_ref, oldgram_ref, s_ref, *rest
 ):
-    chunk_refs, packed = rest[:SPREAD], rest[SPREAD]
+    chunk_refs, packed = rest[SPREAD - 1::-1], rest[SPREAD]
     rows, _, rows_y, rows_z = before_ref.shape
     for group in range(rows // rows_y):
         at = slice(group * rows_y, (group + 1) * rows_y)
@@ -290,23 +290,37 @@
     def spread(j, i):
         return jnp.broadcast_to(cols[j, i:i + 1, :], (SUBS, LANES))
 
-    upper, recip = small_factor([[spread(j, i) for j in range(i + 1)] for i in range(HALF)], HALF)
-    below = [cols[j, HALF:, :] for j in range(HALF)]
-    for k in range(HALF):
-        for j in range(k + 1, HALF):
-            below[j] = below[j] - below[k] * upper[j][k]
-    corner = [cols[j, HALF:, :] for j in range(HALF, PANEL)]
-    for k in range(HALF):
-        cols[k, HALF:, :] = below[k] * recip[k]
-    left = [[spread(k, HALF + i) for k in range(HALF)] for i in range(HALF)]
-    for j in range(HALF):
-        for k in range(HALF):
-            corner[j] = corner[j] - below[k] * left[j][k]
-        cols[HALF + j, HALF:, :] = corner[j]
-    entry = [[spread(HALF + j, HALF + i) for j in range(i + 1)] for i in range(HALF)]
-    lower, more = small_factor(entry, HALF)
-    unit = [row + [None] * HALF for row in upper] + [left[i] + lower[i] for i in range(HALF)]
-    return unit, recip + more
+    unit = [[] for _ in range(PANEL)]
+    recip = []
+    open_cols = [cols[j, j // BLOCK * BLOCK:, :] for j in range(PANEL)]
+    for first in range(0, PANEL, BLOCK):
+        end = first + BLOCK
+        if first:
+            for j in range(first, end):
+                cols[j, first:, :] = open_cols[j]
+        entry = [[spread(first + j, first + i) for j in range(i + 1)] for i in range(BLOCK)]
+        upper, some = small_factor(entry, BLOCK)
+        recip += some
+        for i in range(BLOCK):
+            unit[first + i] += upper[i]
+        if end == PANEL:
+            break
+        below = [open_cols[j][BLOCK:] for j in range(first, end)]
+        count = PANEL - end
+        for k in range(BLOCK):
+            for j in range(k + 1, BLOCK):
+                below[j] = below[j] - below[k] * jnp.tile(upper[j][k], (count // SUBS, 1))
+        for k in range(BLOCK):
+            cols[first + k, end:, :] = below[k] * jnp.tile(some[k], (count // SUBS, 1))
+        for i in range(end, PANEL):
+            unit[i] += [spread(first + k, i) for k in range(BLOCK)]
+        for j in range(end, PANEL):
+            skip = j // BLOCK * BLOCK - end
+            height = (count - skip) // SUBS
+            for k in range(BLOCK):
+                part = below[k][skip:] * jnp.tile(unit[j][first + k], (height, 1))
+                open_cols[j] = open_cols[j] - part
+    return unit, recip
 
 
 def left_pieces(panel, t_ref, low, high):
@@ -315,19 +329,25 @@
     lane = lax.broadcasted_iota(jnp.int32, block.shape, 1)
     block = jnp.where((lane >= off) & (lane < off + PANEL), block, 0.0)
     pieces = [piece.astype(jnp.float32) for piece in split_three(block)]
-    left = pieces[LEFT[0]]
-    for k in range(1, len(LEFT)):
-        left = left + pltpu.roll(pieces[LEFT[k]], k * PANEL, axis=1)
-    return left.astype(jnp.bfloat16)
+    slots = LANES // PANEL
+    left = []
+    for k in range(len(LEFT)):
+        piece = pieces[LEFT[k]]
+        if k % slots:
+            left[-1] = left[-1] + pltpu.roll(piece, k % slots * PANEL, axis=1)
+        else:
+            left.append(piece)
+    return jnp.concatenate(left, axis=1).astype(jnp.bfloat16)
 
 
 def right_pieces(panel, v):
     pieces = split_three(v)
     empty = jnp.zeros(v.shape, jnp.bfloat16)
-    slots = [empty] * (LANES // PANEL)
+    slots = LANES // PANEL
+    right = [empty] * (-(-len(RIGHT) // slots) * slots)
     for k in range(len(RIGHT)):
-        slots[(panel + k) % len(slots)] = pieces[RIGHT[k]]
-    return jnp.concatenate(slots, axis=0)
+        right[k // slots * slots + (panel + k) % slots] = pieces[RIGHT[k]]
+    return jnp.concatenate(right, axis=0)
 
 
 def subtract(panel, t_ref, low, high, left, right):
@@ -442,24 +462,27 @@
 
     turn = turn_matrix(rows_y, 0.0)
     steps = rows_y // 2
-    per_group = GROUP // PANEL
     pairs = planes * steps
-    per_panel = pairs // per_group
+    starts = [sum(GROUPS[:k]) for k in range(len(GROUPS))]
 
     def split_rows(group):
-        rows_here = x_ref[group * GROUP:(group + 1) * GROUP, :]
+        size = GROUPS[group]
+        rows_here = x_ref[starts[group]:starts[group] + size, :]
         high = rows_here.astype(jnp.bfloat16)
-        x_pair[group % 2, :GROUP, :] = high
-        x_pair[group % 2, GROUP:, :] = (rows_here - high.astype(jnp.float32)).astype(jnp.bfloat16)
+        x_pair[group, :size, :] = high
+        x_pair[group, size:2 * size, :] = (rows_here - high.astype(jnp.float32)).astype(jnp.bfloat16)
 
     def multiply(group, pair):
-        depth = (group + 1) * GROUP
+        size = GROUPS[group]
+        depth = starts[group] + size
         sums = jnp.dot(
-            x_pair[group % 2, :, :depth], stack[pair, :depth, :], preferred_element_type=jnp.float32
+            x_pair[group, :2 * size, :depth],
+            stack[pair, :depth, :],
+            preferred_element_type=jnp.float32,
         )
-        sums = (sums[:GROUP] + sums[GROUP:]).astype(jnp.bfloat16)
-        sums = sums.reshape(GROUP // rows_y, rows_y, 2 * rows_z)
-        some = slice(group * GROUP // rows_y, (group + 1) * GROUP // rows_y)
+        sums = (sums[:size] + sums[size:]).astype(jnp.bfloat16)
+        sums = sums.reshape(size // rows_y, rows_y, 2 * rows_z)
+        some = slice(starts[group] // rows_y, depth // rows_y)
         for half in (0, 1):
             y = 2 * (pair % steps) + half
             at = slice(y * rows_y, (y + 1) * rows_y)
@@ -477,37 +500,37 @@
             staged[some * rows_y:(some + 1) * rows_y, plane] = part.reshape(rows_y, rows_y, rows_z)
         store(some).start()
 
-    groups = order // GROUP
-    blocks = GROUP // rows_y
-
     def nothing():
         pass
 
     late, outputs = nothing, nothing
-    for group in range(groups):
+    for group in range(len(GROUPS)):
         if group == 1:
             load_new.wait()
             load_old.wait()
-        for step in range(per_group):
-            panel = group * per_group + step
+        panels = GROUPS[group] // PANEL
+        for step in range(panels):
+            panel = starts[group] // PANEL + step
             before = outputs
             late, outputs = factor_panel(panel, t_ref, f_ref, x_ref, cols, rows, late)
             before()
             if group > 0:
                 if step == 0:
                     split_rows(group - 1)
-                for k in range(per_panel):
-                    multiply(group - 1, step * per_panel + k)
-            if group > 1:
-                finish((group - 2) * blocks + step)
+                for pair in range(step * pairs // panels, (step + 1) * pairs // panels):
+                    multiply(group - 1, pair)
+            if group > 1 and step == 0:
+                for some in range(starts[group - 2] // rows_y, starts[group - 1] // rows_y):
+                    finish(some)
     outputs()
-    split_rows(groups - 1)
-    for k in range(blocks):
-        finish((groups - 2) * blocks + k)
+    last = len(GROUPS) - 1
+    split_rows(last)
+    for some in range(starts[last - 1] // rows_y, starts[last] // rows_y):
+        finish(some)
     for pair in range(pairs):
-        multiply(groups - 1, pair)
-    for k in range(blocks):
-        finish((groups - 1) * blocks + k)
+        multiply(last, pair)
+    for some in range(starts[last] // rows_y, order // rows_y):
+        finish(some)
 
     for some in range(order // rows_y):
         store(some).wait()
@@ -534,7 +557,7 @@
             pltpu.VMEM(square, jnp.float32),
             pltpu.VMEM((2, PANEL, PANEL, LANES), jnp.float32),
             pltpu.VMEM((2, 3, PANEL * SUBS, LANES), jnp.float32),
-            pltpu.VMEM((2, 2 * GROUP, order), jnp.bfloat16),
+            pltpu.VMEM((len(GROUPS), 2 * max(GROUPS), order), jnp.bfloat16),
             pltpu.VMEM((pairs, order, 2 * rows_z), jnp.bfloat16),
             pltpu.VMEM((planes, order // rows_y, rows_y * rows_y, rows_z), jnp.bfloat16),
             pltpu.VMEM(shape, jnp.bfloat16),
@@ -559,6 +582,7 @@
         old_modes, snapshots, mode_scales, plane_counts, links
     )
     s_new, *chunks = filtered_rows(before, after, inner, outer, turn, s_old, old_gram)
+    chunks = chunks[::-1]
     sums = sum_chunks(chunks, "blk")
     factor, modes = factor_and_modes(
         sums, s_new, s_old, (order, planes, rows_y, rows_z), peers * planes * rows_y * rows_z

time: 42.7 us -> 44.3 us (1.037)
  Pallas kernels: 14.6 us -> 16 us
    pallas_call x1, Pallas kernels: 10 us -> 11.4 us  [factor_and_modes(): pl.pallas_call(functools.partial(factor_kernel, 1.0 / cell_total), out_sh...]
where the time goes in v11:
time: 44.3 us; the launch traced here: 44.1 us
  Pallas kernels  16 us (36%)
  starting transfers between devices  14.3 us (32%)
  waiting for transfers between devices  8.4 us (19%)
  local copies, waits for them, and re-layouts  3.12 us (7%)
  between operations  1.5 us (3%)
  other arithmetic  0.75 us (2%)
    pallas_call x1, Pallas kernels, factor_and_modes(): pl.pallas_call(functools.partial(factor_kernel, 1.0 / cell_total), out_sh...  11.4 us
    ppermute x9, starting transfers between devices, swap(): return lax.ppermute(x, axis, [(i, i ^ flip) for i in range(peers)])  8.76 us
    ppermute x9, waiting for transfers between devices, swap(): return lax.ppermute(x, axis, [(i, i ^ flip) for i in range(peers)])  8.39 us
    ppermute x1, starting transfers between devices, shards(): after = lax.ppermute(first, 'blk', down)  5.03 us
    unnamed x6, local copies, waits for them, and re-layouts  3.12 us
    pallas_call x1, Pallas kernels, prepared_rows(): pl.pallas_call(scale_kernel, out_shape=[jax.ShapeDtypeStruct((planes * ro...  2.44 us
    pallas_call x1, Pallas kernels, filtered_rows(): pl.pallas_call(filter_kernel, out_shape=[jax.ShapeDtypeStruct((pairs, row...  2.03 us
  transfers between devices with their start and end apart: 11, of which 5 were waited for; matrix products, arithmetic and copies ran while one was open for 2% of the time, Pallas kernels for 6%

profile of v11, /device:TPU:0, one launch (start us, length us, event | category | flops | bytes accessed | tf_op | source)
XLA Modules:
  0.0 44.1 jit_solution(6443018249722336615)
XLA Ops:
  1.3 0.0 copy-start
  1.3 1.0 %copy-done = bf16[64,2,16,128]{3,2,1,0:T(8,128)(2,1)S(1)} copy-done((bf16[64,2,16,128]{3,2,1,0:T(8,128)(2,1)S(1)}, bf16[64,2,16,128]{3,2,1,0:T(8,128)(2,1)}, u32[]{:S(2)}) %copy-start) | copy-done | bytes 524312
  2.3 0.1 edges.1
  2.4 0.5 %collective-permute-start = (bf16[64,1,16,128]{3,2,1,0:T(8,128)(2,1)S(1)}, bf16[64,1,16,128]{3,2,1,0:T(8,128)(2,1)S(1)}, u32[]{:S(2)}, u32[]{:S(2)}) collective-permute-start(bf16[64,1,16,128]{3,2,1,0:T(8,128)(2,1)S(1)} %get-tuple-element.16), channel_id=1, source_target_pairs={{0,1},{1,2},{2,3},{3,4},{4,5},{5,6},{6,7},{7,8},{8,9},{9,10},{10,1... | collective-permute-start | bytes 786440 | tf_op jit(solution)/shard_map/ppermute | solution.py:579
  2.9 5.0 %collective-permute-start.1 = (bf16[64,1,16,128]{3,2,1,0:T(8,128)(2,1)S(1)}, bf16[64,1,16,128]{3,2,1,0:T(8,128)(2,1)S(1)}, u32[]{:S(2)}, u32[]{:S(2)}) collective-permute-start(bf16[64,1,16,128]{3,2,1,0:T(8,128)(2,1)S(1)} %get-tuple-element.17), channel_id=1, source_target_pairs={{1,0},{2,1},{3,2},{4,3},{5,4},{6,5},{7,6},{8,7},{9,8},{10,9},{11,1... | collective-permute-start | bytes 786440 | tf_op jit(solution)/shard_map/ppermute | solution.py:580
  7.9 0.7 %pad_add_fusion.table_ref = s32[3]{0:T(128)S(1)} fusion(s32[2]{0:T(128)} %bitcast.3, s32[1]{0:T(128)S(6)} %copy.7.count_ref), kind=kLoop, calls=%fused_computation.2 | loop fusion | flops 3 | bytes 24 | tf_op jit(solution)/shard_map/concatenate | solution.py:154
  8.7 0.0 copy-start.1
  8.7 1.4 %copy-done.1 = bf16[192,2,16,128]{3,2,1,0:T(8,128)(2,1)S(1)} copy-done((bf16[192,2,16,128]{3,2,1,0:T(8,128)(2,1)S(1)}, bf16[192,2,16,128]{3,2,1,0:T(8,128)(2,1)}, u32[]{:S(2)}) %copy-start.1) | copy-done | bytes 1572888
  10.1 0.0 copy-start.2
  10.1 0.7 %copy-done.2 = f32[192]{0:T(256)S(1)} copy-done((f32[192]{0:T(256)S(1)}, f32[192]{0:T(256)}, u32[]{:S(2)}) %copy-start.2) | copy-done | bytes 792
  10.8 2.4 %prepare.1 = (bf16[16,192,256]{2,1,0:T(8,128)(2,1)S(1)}, f32[192,192]{1,0:T(8,128)S(1)}, f32[4,256,256]{2,1,0:T(8,128)S(1)}, bf16[256,256]{1,0:T(8,128)(2,1)S(1)}, bf16[256,256]{1,0:T(8,128)(2,1)S(1)}) custom-call(s32[3]{0:T(128)S(1)} %pad_add_fusion.table_ref, f32[1,192]{1,0:T(1,128)S(1)} %bitcast.2, bf16[192,2,16,128]{3,2,1,0:T(8,128)(2,1)S(1)} %copy-done.1, ...), custom_call_target="tpu_custom_call" | custom-call | flops 301989888 | bytes 6291456 | tf_op jit(solution)/shard_map/prepare/pallas_call | solution.py:160
  13.2 0.0 collective-permute-done.before_ref
  13.2 0.0 collective-permute-done.1.after_ref
  13.2 2.0 %filter_gram.1 = (bf16[16,64,256]{2,1,0:T(8,128)(2,1)S(1)}, f32[72,128]{1,0:T(8,128)S(1)}, f32[72,128]{1,0:T(8,128)S(1)}, f32[72,128]{1,0:T(8,128)S(1)}, f32[72,128]{1,0:T(8,128)S(1)}) custom-call(bf16[64,1,16,128]{3,2,1,0:T(8,128)(2,1)S(1)} %collective-permute-done.before_ref, bf16[64,1,16,128]{3,2,1,0:T(8,128)(2,1)S(1)} %collective-permute-done.1.after_ref, ...), custom_call_target="tpu_custom_call" | custom-call | flops 134217728 | bytes 2097152 | tf_op jit(solution)/shard_map/filter_gram/pallas_call | solution.py:228
  15.3 1.0 %collective-permute-start.2 = (f32[72,128]{1,0:T(8,128)S(1)}, f32[72,128]{1,0:T(8,128)S(1)}, u32[]{:S(2)}, u32[]{:S(2)}) collective-permute-start(f32[72,128]{1,0:T(8,128)S(1)} %get-tuple-element.24), channel_id=1, source_target_pairs={{0,1},{1,0},{2,3},{3,2},{4,5},{5,4},{6,7},{7,6},{8,9},{9,8},{10,11... | collective-permute-start | bytes 110600 | tf_op jit(solution)/shard_map/ppermute | solution.py:27
  16.2 0.0 collective-permute-start.3
  16.2 1.4 %collective-permute-start.4 = (f32[72,128]{1,0:T(8,128)S(1)}, f32[72,128]{1,0:T(8,128)S(1)}, u32[]{:S(2)}, u32[]{:S(2)}) collective-permute-start(f32[72,128]{1,0:T(8,128)S(1)} %get-tuple-element.26), channel_id=1, source_target_pairs={{0,3},{1,2},{2,1},{3,0},{4,7},{5,6},{6,5},{7,4},{8,11},{9,10},{10,... | collective-permute-start | bytes 110600 | tf_op jit(solution)/shard_map/ppermute | solution.py:27
  17.7 0.0 collective-permute-done.2
  17.7 2.5 %collective-permute-done.3 = f32[72,128]{1,0:T(8,128)S(1)} collective-permute-done((f32[72,128]{1,0:T(8,128)S(1)}, f32[72,128]{1,0:T(8,128)S(1)}, u32[]{:S(2)}, u32[]{:S(2)}) %collective-permute-start.3) | collective-permute-done | bytes 36896 | tf_op jit(solution)/shard_map/ppermute | solution.py:27
  20.2 0.0 collective-permute-done.4
  20.2 3.2 %collective-permute-start.7 = (f32[72,128]{1,0:T(8,128)S(1)}, f32[72,128]{1,0:T(8,128)S(1)}, u32[]{:S(2)}, u32[]{:S(2)}) collective-permute-start(f32[72,128]{1,0:T(8,128)S(1)} %add_add_fusion.1), channel_id=1, source_target_pairs={{0,12},{1,13},{2,14},{3,15},{4,8},{5,9},{6,10},{7,11},{8,4},{9,5},... | collective-permute-start | bytes 110600 | tf_op jit(solution)/shard_map/ppermute | solution.py:27
  23.4 0.0 collective-permute-start.6
  23.4 1.3 %collective-permute-start.5 = (f32[72,128]{1,0:T(8,128)S(1)}, f32[72,128]{1,0:T(8,128)S(1)}, u32[]{:S(2)}, u32[]{:S(2)}) collective-permute-start(f32[72,128]{1,0:T(8,128)S(1)} %add_add_fusion.1), channel_id=1, source_target_pairs={{0,4},{1,5},{2,6},{3,7},{4,0},{5,1},{6,2},{7,3},{8,12},{9,13},{10,... | collective-permute-start | bytes 110600 | tf_op jit(solution)/shard_map/ppermute | solution.py:27
  24.7 1.6 %collective-permute-done.7 = f32[72,128]{1,0:T(8,128)S(1)} collective-permute-done((f32[72,128]{1,0:T(8,128)S(1)}, f32[72,128]{1,0:T(8,128)S(1)}, u32[]{:S(2)}, u32[]{:S(2)}) %collective-permute-start.7) | collective-permute-done | bytes 36896 | tf_op jit(solution)/shard_map/ppermute | solution.py:27
  26.3 2.0 %collective-permute-done.6 = f32[72,128]{1,0:T(8,128)S(1)} collective-permute-done((f32[72,128]{1,0:T(8,128)S(1)}, f32[72,128]{1,0:T(8,128)S(1)}, u32[]{:S(2)}, u32[]{:S(2)}) %collective-permute-start.6) | collective-permute-done | bytes 36896 | tf_op jit(solution)/shard_map/ppermute | solution.py:27
  28.2 0.0 collective-permute-done.5
  28.3 0.1 collective-permute-start.10
  28.4 1.4 %collective-permute-start.9 = (f32[72,128]{1,0:T(8,128)S(1)}, f32[72,128]{1,0:T(8,128)S(1)}, u32[]{:S(2)}, u32[]{:S(2)}) collective-permute-start(f32[72,128]{1,0:T(8,128)S(1)} %add_add_fusion.refs_0_), channel_id=1, source_target_pairs={{0,2},{1,3},{2,0},{3,1},{4,6},{5,7},{6,4},{7,5},{8,10},{9,11},{10,... | collective-permute-start | bytes 110600 | tf_op jit(solution)/shard_map/ppermute | solution.py:27
  29.8 0.4 collective-permute-start.8
  30.2 1.9 %collective-permute-done.10.refs_3_ = f32[72,128]{1,0:T(8,128)S(1)} collective-permute-done((f32[72,128]{1,0:T(8,128)S(1)}, f32[72,128]{1,0:T(8,128)S(1)}, u32[]{:S(2)}, u32[]{:S(2)}) %collective-permute-start.10) | collective-permute-done | bytes 36896 | tf_op jit(solution)/shard_map/ppermute | solution.py:27
  32.1 0.4 collective-permute-done.9.refs_2_
  32.5 0.0 collective-permute-done.8.refs_1_
  32.5 11.4 %factor.1 = (f32[256,256]{1,0:T(8,128)}, bf16[256,2,16,128]{3,2,1,0:T(8,128)(2,1)}) custom-call(f32[72,128]{1,0:T(8,128)S(1)} %add_add_fusion.refs_0_, f32[72,128]{1,0:T(8,128)S(1)} %collective-permute-done.8.refs_1_, f32[72,128]{1,0:T(8,128)S(1)} %collective-permute-done.9.refs_2_, f32[72,128]{1,0:T(8,128)S(1)} %collective-permute-done.10.refs_3_, ...), custom_call_target="tpu_custom_call" | custom-call | tf_op jit(solution)/shard_map/factor/pallas_call | solution.py:546
  (2 shorter events, 0.0 us)
Async XLA Ops:
  1.3 1.0 %copy-start = (bf16[64,2,16,128]{3,2,1,0:T(8,128)(2,1)S(1)}, bf16[64,2,16,128]{3,2,1,0:T(8,128)(2,1)}, u32[]{:S(2)}) copy-start(bf16[64,2,16,128]{3,2,1,0:T(8,128)(2,1)} %snap_ref.3) | copy-start | bytes 1572868
  2.4 10.8 %collective-permute-start = (bf16[64,1,16,128]{3,2,1,0:T(8,128)(2,1)S(1)}, bf16[64,1,16,128]{3,2,1,0:T(8,128)(2,1)S(1)}, u32[]{:S(2)}, u32[]{:S(2)}) collective-permute-start(bf16[64,1,16,128]{3,2,1,0:T(8,128)(2,1)S(1)} %get-tuple-element.16), channel_id=1, source_target_pairs={{0,1},{1,2},{2,3},{3,4},{4,5},{5,6},{6,7},{7,8},{8,9},{9,10},{10,1... | collective-permute-start | bytes 786440 | tf_op jit(solution)/shard_map/ppermute | solution.py:579
  2.9 10.3 %collective-permute-start.1 = (bf16[64,1,16,128]{3,2,1,0:T(8,128)(2,1)S(1)}, bf16[64,1,16,128]{3,2,1,0:T(8,128)(2,1)S(1)}, u32[]{:S(2)}, u32[]{:S(2)}) collective-permute-start(bf16[64,1,16,128]{3,2,1,0:T(8,128)(2,1)S(1)} %get-tuple-element.17), channel_id=1, source_target_pairs={{1,0},{2,1},{3,2},{4,3},{5,4},{6,5},{7,6},{8,7},{9,8},{10,9},{11,1... | collective-permute-start | bytes 786440 | tf_op jit(solution)/shard_map/ppermute | solution.py:580
  8.7 1.4 %copy-start.1 = (bf16[192,2,16,128]{3,2,1,0:T(8,128)(2,1)S(1)}, bf16[192,2,16,128]{3,2,1,0:T(8,128)(2,1)}, u32[]{:S(2)}) copy-start(bf16[192,2,16,128]{3,2,1,0:T(8,128)(2,1)} %old_ref.1) | copy-start | bytes 4718596
  10.1 0.7 %copy-start.2 = (f32[192]{0:T(256)S(1)}, f32[192]{0:T(256)}, u32[]{:S(2)}) copy-start(f32[192]{0:T(256)} %param.7) | copy-start | bytes 2308
  15.3 2.4 %collective-permute-start.2 = (f32[72,128]{1,0:T(8,128)S(1)}, f32[72,128]{1,0:T(8,128)S(1)}, u32[]{:S(2)}, u32[]{:S(2)}) collective-permute-start(f32[72,128]{1,0:T(8,128)S(1)} %get-tuple-element.24), channel_id=1, source_target_pairs={{0,1},{1,0},{2,3},{3,2},{4,5},{5,4},{6,7},{7,6},{8,9},{9,8},{10,11... | collective-permute-start | bytes 110600 | tf_op jit(solution)/shard_map/ppermute | solution.py:27
  16.2 4.0 %collective-permute-start.3 = (f32[72,128]{1,0:T(8,128)S(1)}, f32[72,128]{1,0:T(8,128)S(1)}, u32[]{:S(2)}, u32[]{:S(2)}) collective-permute-start(f32[72,128]{1,0:T(8,128)S(1)} %get-tuple-element.25), channel_id=1, source_target_pairs={{0,2},{1,3},{2,0},{3,1},{4,6},{5,7},{6,4},{7,5},{8,10},{9,11},{10,... | collective-permute-start | bytes 110600 | tf_op jit(solution)/shard_map/ppermute | solution.py:27
  16.2 4.0 %collective-permute-start.4 = (f32[72,128]{1,0:T(8,128)S(1)}, f32[72,128]{1,0:T(8,128)S(1)}, u32[]{:S(2)}, u32[]{:S(2)}) collective-permute-start(f32[72,128]{1,0:T(8,128)S(1)} %get-tuple-element.26), channel_id=1, source_target_pairs={{0,3},{1,2},{2,1},{3,0},{4,7},{5,6},{6,5},{7,4},{8,11},{9,10},{10,... | collective-permute-start | bytes 110600 | tf_op jit(solution)/shard_map/ppermute | solution.py:27
  20.2 6.1 %collective-permute-start.7 = (f32[72,128]{1,0:T(8,128)S(1)}, f32[72,128]{1,0:T(8,128)S(1)}, u32[]{:S(2)}, u32[]{:S(2)}) collective-permute-start(f32[72,128]{1,0:T(8,128)S(1)} %add_add_fusion.1), channel_id=1, source_target_pairs={{0,12},{1,13},{2,14},{3,15},{4,8},{5,9},{6,10},{7,11},{8,4},{9,5},... | collective-permute-start | bytes 110600 | tf_op jit(solution)/shard_map/ppermute | solution.py:27
  23.4 4.9 %collective-permute-start.6 = (f32[72,128]{1,0:T(8,128)S(1)}, f32[72,128]{1,0:T(8,128)S(1)}, u32[]{:S(2)}, u32[]{:S(2)}) collective-permute-start(f32[72,128]{1,0:T(8,128)S(1)} %add_add_fusion.1), channel_id=1, source_target_pairs={{0,8},{1,9},{2,10},{3,11},{4,12},{5,13},{6,14},{7,15},{8,0},{9,1},... | collective-permute-start | bytes 110600 | tf_op jit(solution)/shard_map/ppermute | solution.py:27
  23.4 4.9 %collective-permute-start.5 = (f32[72,128]{1,0:T(8,128)S(1)}, f32[72,128]{1,0:T(8,128)S(1)}, u32[]{:S(2)}, u32[]{:S(2)}) collective-permute-start(f32[72,128]{1,0:T(8,128)S(1)} %add_add_fusion.1), channel_id=1, source_target_pairs={{0,4},{1,5},{2,6},{3,7},{4,0},{5,1},{6,2},{7,3},{8,12},{9,13},{10,... | collective-permute-start | bytes 110600 | tf_op jit(solution)/shard_map/ppermute | solution.py:27
  28.3 3.8 %collective-permute-start.10 = (f32[72,128]{1,0:T(8,128)S(1)}, f32[72,128]{1,0:T(8,128)S(1)}, u32[]{:S(2)}, u32[]{:S(2)}) collective-permute-start(f32[72,128]{1,0:T(8,128)S(1)} %add_add_fusion.refs_0_), channel_id=1, source_target_pairs={{0,3},{1,2},{2,1},{3,0},{4,7},{5,6},{6,5},{7,4},{8,11},{9,10},{10,... | collective-permute-start | bytes 110600 | tf_op jit(solution)/shard_map/ppermute | solution.py:27
  28.4 4.1 %collective-permute-start.9 = (f32[72,128]{1,0:T(8,128)S(1)}, f32[72,128]{1,0:T(8,128)S(1)}, u32[]{:S(2)}, u32[]{:S(2)}) collective-permute-start(f32[72,128]{1,0:T(8,128)S(1)} %add_add_fusion.refs_0_), channel_id=1, source_target_pairs={{0,2},{1,3},{2,0},{3,1},{4,6},{5,7},{6,4},{7,5},{8,10},{9,11},{10,... | collective-permute-start | bytes 110600 | tf_op jit(solution)/shard_map/ppermute | solution.py:27
  29.8 2.7 %collective-permute-start.8 = (f32[72,128]{1,0:T(8,128)S(1)}, f32[72,128]{1,0:T(8,128)S(1)}, u32[]{:S(2)}, u32[]{:S(2)}) collective-permute-start(f32[72,128]{1,0:T(8,128)S(1)} %add_add_fusion.refs_0_), channel_id=1, source_target_pairs={{0,1},{1,0},{2,3},{3,2},{4,5},{5,4},{6,7},{7,6},{8,9},{9,8},{10,11... | collective-permute-start | bytes 110600 | tf_op jit(solution)/shard_map/ppermute | solution.py:27

commit v12 on v10

--- a/solution.py
+++ b/solution.py
@@ -9,7 +9,7 @@
 
 PANEL = 16
 HALF = 8
-GROUP = 64
+GROUPS = (64, 64, 64, 32, 32)
 LANES = 128
 SUBS = 8
 SPREAD = 4
@@ -442,24 +442,27 @@
 
     turn = turn_matrix(rows_y, 0.0)
     steps = rows_y // 2
-    per_group = GROUP // PANEL
     pairs = planes * steps
-    per_panel = pairs // per_group
+    starts = [sum(GROUPS[:k]) for k in range(len(GROUPS))]
 
     def split_rows(group):
-        rows_here = x_ref[group * GROUP:(group + 1) * GROUP, :]
+        size = GROUPS[group]
+        rows_here = x_ref[starts[group]:starts[group] + size, :]
         high = rows_here.astype(jnp.bfloat16)
-        x_pair[group % 2, :GROUP, :] = high
-        x_pair[group % 2, GROUP:, :] = (rows_here - high.astype(jnp.float32)).astype(jnp.bfloat16)
+        x_pair[group, :size, :] = high
+        x_pair[group, size:2 * size, :] = (rows_here - high.astype(jnp.float32)).astype(jnp.bfloat16)
 
     def multiply(group, pair):
-        depth = (group + 1) * GROUP
+        size = GROUPS[group]
+        depth = starts[group] + size
         sums = jnp.dot(
-            x_pair[group % 2, :, :depth], stack[pair, :depth, :], preferred_element_type=jnp.float32
+            x_pair[group, :2 * size, :depth],
+            stack[pair, :depth, :],
+            preferred_element_type=jnp.float32,
         )
-        sums = (sums[:GROUP] + sums[GROUP:]).astype(jnp.bfloat16)
-        sums = sums.reshape(GROUP // rows_y, rows_y, 2 * rows_z)
-        some = slice(group * GROUP // rows_y, (group + 1) * GROUP // rows_y)
+        sums = (sums[:size] + sums[size:]).astype(jnp.bfloat16)
+        sums = sums.reshape(size // rows_y, rows_y, 2 * rows_z)
+        some = slice(starts[group] // rows_y, depth // rows_y)
         for half in (0, 1):
             y = 2 * (pair % steps) + half
             at = slice(y * rows_y, (y + 1) * rows_y)
@@ -477,37 +480,37 @@
             staged[some * rows_y:(some + 1) * rows_y, plane] = part.reshape(rows_y, rows_y, rows_z)
         store(some).start()
 
-    groups = order // GROUP
-    blocks = GROUP // rows_y
-
     def nothing():
         pass
 
     late, outputs = nothing, nothing
-    for group in range(groups):
+    for group in range(len(GROUPS)):
         if group == 1:
             load_new.wait()
             load_old.wait()
-        for step in range(per_group):
-            panel = group * per_group + step
+        panels = GROUPS[group] // PANEL
+        for step in range(panels):
+            panel = starts[group] // PANEL + step
             before = outputs
             late, outputs = factor_panel(panel, t_ref, f_ref, x_ref, cols, rows, late)
             before()
             if group > 0:
                 if step == 0:
                     split_rows(group - 1)
-                for k in range(per_panel):
-                    multiply(group - 1, step * per_panel + k)
-            if group > 1:
-                finish((group - 2) * blocks + step)
+                for pair in range(step * pairs // panels, (step + 1) * pairs // panels):
+                    multiply(group - 1, pair)
+            if group > 1 and step == 0:
+                for some in range(starts[group - 2] // rows_y, starts[group - 1] // rows_y):
+                    finish(some)
     outputs()
-    split_rows(groups - 1)
-    for k in range(blocks):
-        finish((groups - 2) * blocks + k)
+    last = len(GROUPS) - 1
+    split_rows(last)
+    for some in range(starts[last - 1] // rows_y, starts[last] // rows_y):
+        finish(some)
     for pair in range(pairs):
-        multiply(groups - 1, pair)
-    for k in range(blocks):
-        finish((groups - 1) * blocks + k)
+        multiply(last, pair)
+    for some in range(starts[last] // rows_y, order // rows_y):
+        finish(some)
 
     for some in range(order // rows_y):
         store(some).wait()
@@ -534,7 +537,7 @@
             pltpu.VMEM(square, jnp.float32),
             pltpu.VMEM((2, PANEL, PANEL, LANES), jnp.float32),
             pltpu.VMEM((2, 3, PANEL * SUBS, LANES), jnp.float32),
-            pltpu.VMEM((2, 2 * GROUP, order), jnp.bfloat16),
+            pltpu.VMEM((len(GROUPS), 2 * max(GROUPS), order), jnp.bfloat16),
             pltpu.VMEM((pairs, order, 2 * rows_z), jnp.bfloat16),
             pltpu.VMEM((planes, order // rows_y, rows_y * rows_y, rows_z), jnp.bfloat16),
             pltpu.VMEM(shape, jnp.bfloat16),

time: 42.7 us -> 42.8 us (level)
  no operation moved by 1% of the time
where the time goes in v12:
time: 42.8 us; the launch traced here: 42.6 us
  Pallas kernels  14.7 us (34%)
  starting transfers between devices  14.3 us (33%)
  waiting for transfers between devices  8.42 us (20%)
  local copies, waits for them, and re-layouts  3.12 us (7%)
  between operations  1.34 us (3%)
  other arithmetic  0.75 us (2%)
    pallas_call x1, Pallas kernels, factor_and_modes(): pl.pallas_call(functools.partial(factor_kernel, 1.0 / cell_total), out_sh...  10.1 us
    ppermute x9, starting transfers between devices, swap(): return lax.ppermute(x, axis, [(i, i ^ flip) for i in range(peers)])  8.75 us
    ppermute x9, waiting for transfers between devices, swap(): return lax.ppermute(x, axis, [(i, i ^ flip) for i in range(peers)])  8.42 us
    ppermute x1, starting transfers between devices, shards(): after = lax.ppermute(first, 'blk', down)  5.03 us
    unnamed x6, local copies, waits for them, and re-layouts  3.12 us
    pallas_call x1, Pallas kernels, prepared_rows(): pl.pallas_call(scale_kernel, out_shape=[jax.ShapeDtypeStruct((planes * ro...  2.44 us
    pallas_call x1, Pallas kernels, filtered_rows(): pl.pallas_call(filter_kernel, out_shape=[jax.ShapeDtypeStruct((pairs, row...  2.03 us
  transfers between devices with their start and end apart: 11, of which 5 were waited for; matrix products, arithmetic and copies ran while one was open for 2% of the time, Pallas kernels for 6%

profile of v12, /device:TPU:0, one launch (start us, length us, event | category | flops | bytes accessed | tf_op | source)
XLA Modules:
  0.0 42.6 jit_solution(17569890165251463898)
XLA Ops:
  1.3 0.0 copy-start
  1.3 1.0 %copy-done = bf16[64,2,16,128]{3,2,1,0:T(8,128)(2,1)S(1)} copy-done((bf16[64,2,16,128]{3,2,1,0:T(8,128)(2,1)S(1)}, bf16[64,2,16,128]{3,2,1,0:T(8,128)(2,1)}, u32[]{:S(2)}) %copy-start) | copy-done | bytes 524312
  2.3 0.1 edges.1
  2.4 0.5 %collective-permute-start = (bf16[64,1,16,128]{3,2,1,0:T(8,128)(2,1)S(1)}, bf16[64,1,16,128]{3,2,1,0:T(8,128)(2,1)S(1)}, u32[]{:S(2)}, u32[]{:S(2)}) collective-permute-start(bf16[64,1,16,128]{3,2,1,0:T(8,128)(2,1)S(1)} %get-tuple-element.16), channel_id=1, source_target_pairs={{0,1},{1,2},{2,3},{3,4},{4,5},{5,6},{6,7},{7,8},{8,9},{9,10},{10,1... | collective-permute-start | bytes 786440 | tf_op jit(solution)/shard_map/ppermute | solution.py:559
  2.9 5.0 %collective-permute-start.1 = (bf16[64,1,16,128]{3,2,1,0:T(8,128)(2,1)S(1)}, bf16[64,1,16,128]{3,2,1,0:T(8,128)(2,1)S(1)}, u32[]{:S(2)}, u32[]{:S(2)}) collective-permute-start(bf16[64,1,16,128]{3,2,1,0:T(8,128)(2,1)S(1)} %get-tuple-element.17), channel_id=1, source_target_pairs={{1,0},{2,1},{3,2},{4,3},{5,4},{6,5},{7,6},{8,7},{9,8},{10,9},{11,1... | collective-permute-start | bytes 786440 | tf_op jit(solution)/shard_map/ppermute | solution.py:560
  7.9 0.7 %pad_add_fusion.table_ref = s32[3]{0:T(128)S(1)} fusion(s32[2]{0:T(128)} %bitcast.3, s32[1]{0:T(128)S(6)} %copy.7.count_ref), kind=kLoop, calls=%fused_computation.2 | loop fusion | flops 3 | bytes 24 | tf_op jit(solution)/shard_map/concatenate | solution.py:154
  8.7 0.0 copy-start.1
  8.7 1.4 %copy-done.1 = bf16[192,2,16,128]{3,2,1,0:T(8,128)(2,1)S(1)} copy-done((bf16[192,2,16,128]{3,2,1,0:T(8,128)(2,1)S(1)}, bf16[192,2,16,128]{3,2,1,0:T(8,128)(2,1)}, u32[]{:S(2)}) %copy-start.1) | copy-done | bytes 1572888
  10.1 0.0 copy-start.2
  10.1 0.7 %copy-done.2 = f32[192]{0:T(256)S(1)} copy-done((f32[192]{0:T(256)S(1)}, f32[192]{0:T(256)}, u32[]{:S(2)}) %copy-start.2) | copy-done | bytes 792
  10.8 2.4 %prepare.1 = (bf16[16,192,256]{2,1,0:T(8,128)(2,1)S(1)}, f32[192,192]{1,0:T(8,128)S(1)}, f32[4,256,256]{2,1,0:T(8,128)S(1)}, bf16[256,256]{1,0:T(8,128)(2,1)S(1)}, bf16[256,256]{1,0:T(8,128)(2,1)S(1)}) custom-call(s32[3]{0:T(128)S(1)} %pad_add_fusion.table_ref, f32[1,192]{1,0:T(1,128)S(1)} %bitcast.2, bf16[192,2,16,128]{3,2,1,0:T(8,128)(2,1)S(1)} %copy-done.1, ...), custom_call_target="tpu_custom_call" | custom-call | flops 301989888 | bytes 6291456 | tf_op jit(solution)/shard_map/prepare/pallas_call | solution.py:160
  13.2 0.0 collective-permute-done.before_ref
  13.2 0.0 collective-permute-done.1.after_ref
  13.2 2.0 %filter_gram.1 = (bf16[16,64,256]{2,1,0:T(8,128)(2,1)S(1)}, f32[72,128]{1,0:T(8,128)S(1)}, f32[72,128]{1,0:T(8,128)S(1)}, f32[72,128]{1,0:T(8,128)S(1)}, f32[72,128]{1,0:T(8,128)S(1)}) custom-call(bf16[64,1,16,128]{3,2,1,0:T(8,128)(2,1)S(1)} %collective-permute-done.before_ref, bf16[64,1,16,128]{3,2,1,0:T(8,128)(2,1)S(1)} %collective-permute-done.1.after_ref, ...), custom_call_target="tpu_custom_call" | custom-call | flops 134217728 | bytes 2097152 | tf_op jit(solution)/shard_map/filter_gram/pallas_call | solution.py:228
  15.3 0.9 %collective-permute-start.2 = (f32[72,128]{1,0:T(8,128)S(1)}, f32[72,128]{1,0:T(8,128)S(1)}, u32[]{:S(2)}, u32[]{:S(2)}) collective-permute-start(f32[72,128]{1,0:T(8,128)S(1)} %get-tuple-element.24), channel_id=1, source_target_pairs={{0,1},{1,0},{2,3},{3,2},{4,5},{5,4},{6,7},{7,6},{8,9},{9,8},{10,11... | collective-permute-start | bytes 110600 | tf_op jit(solution)/shard_map/ppermute | solution.py:27
  16.2 0.0 collective-permute-start.3
  16.2 1.4 %collective-permute-start.4 = (f32[72,128]{1,0:T(8,128)S(1)}, f32[72,128]{1,0:T(8,128)S(1)}, u32[]{:S(2)}, u32[]{:S(2)}) collective-permute-start(f32[72,128]{1,0:T(8,128)S(1)} %get-tuple-element.26), channel_id=1, source_target_pairs={{0,3},{1,2},{2,1},{3,0},{4,7},{5,6},{6,5},{7,4},{8,11},{9,10},{10,... | collective-permute-start | bytes 110600 | tf_op jit(solution)/shard_map/ppermute | solution.py:27
  17.6 0.0 collective-permute-done.2
  17.6 2.5 %collective-permute-done.3 = f32[72,128]{1,0:T(8,128)S(1)} collective-permute-done((f32[72,128]{1,0:T(8,128)S(1)}, f32[72,128]{1,0:T(8,128)S(1)}, u32[]{:S(2)}, u32[]{:S(2)}) %collective-permute-start.3) | collective-permute-done | bytes 36896 | tf_op jit(solution)/shard_map/ppermute | solution.py:27
  20.2 0.0 collective-permute-done.4
  20.2 3.2 %collective-permute-start.7 = (f32[72,128]{1,0:T(8,128)S(1)}, f32[72,128]{1,0:T(8,128)S(1)}, u32[]{:S(2)}, u32[]{:S(2)}) collective-permute-start(f32[72,128]{1,0:T(8,128)S(1)} %add_add_fusion.1), channel_id=1, source_target_pairs={{0,12},{1,13},{2,14},{3,15},{4,8},{5,9},{6,10},{7,11},{8,4},{9,5},... | collective-permute-start | bytes 110600 | tf_op jit(solution)/shard_map/ppermute | solution.py:27
  23.4 0.0 collective-permute-start.6
  23.4 1.3 %collective-permute-start.5 = (f32[72,128]{1,0:T(8,128)S(1)}, f32[72,128]{1,0:T(8,128)S(1)}, u32[]{:S(2)}, u32[]{:S(2)}) collective-permute-start(f32[72,128]{1,0:T(8,128)S(1)} %add_add_fusion.1), channel_id=1, source_target_pairs={{0,4},{1,5},{2,6},{3,7},{4,0},{5,1},{6,2},{7,3},{8,12},{9,13},{10,... | collective-permute-start | bytes 110600 | tf_op jit(solution)/shard_map/ppermute | solution.py:27
  24.6 1.6 %collective-permute-done.7 = f32[72,128]{1,0:T(8,128)S(1)} collective-permute-done((f32[72,128]{1,0:T(8,128)S(1)}, f32[72,128]{1,0:T(8,128)S(1)}, u32[]{:S(2)}, u32[]{:S(2)}) %collective-permute-start.7) | collective-permute-done | bytes 36896 | tf_op jit(solution)/shard_map/ppermute | solution.py:27
  26.2 2.0 %collective-permute-done.6 = f32[72,128]{1,0:T(8,128)S(1)} collective-permute-done((f32[72,128]{1,0:T(8,128)S(1)}, f32[72,128]{1,0:T(8,128)S(1)}, u32[]{:S(2)}, u32[]{:S(2)}) %collective-permute-start.6) | collective-permute-done | bytes 36896 | tf_op jit(solution)/shard_map/ppermute | solution.py:27
  28.2 0.0 collective-permute-done.5
  28.3 0.1 collective-permute-start.10
  28.4 1.4 %collective-permute-start.9 = (f32[72,128]{1,0:T(8,128)S(1)}, f32[72,128]{1,0:T(8,128)S(1)}, u32[]{:S(2)}, u32[]{:S(2)}) collective-permute-start(f32[72,128]{1,0:T(8,128)S(1)} %add_add_fusion.refs_0_), channel_id=1, source_target_pairs={{0,2},{1,3},{2,0},{3,1},{4,6},{5,7},{6,4},{7,5},{8,10},{9,11},{10,... | collective-permute-start | bytes 110600 | tf_op jit(solution)/shard_map/ppermute | solution.py:27
  29.8 0.4 collective-permute-start.8
  30.2 1.9 %collective-permute-done.10.refs_3_ = f32[72,128]{1,0:T(8,128)S(1)} collective-permute-done((f32[72,128]{1,0:T(8,128)S(1)}, f32[72,128]{1,0:T(8,128)S(1)}, u32[]{:S(2)}, u32[]{:S(2)}) %collective-permute-start.10) | collective-permute-done | bytes 36896 | tf_op jit(solution)/shard_map/ppermute | solution.py:27
  32.1 0.4 collective-permute-done.9.refs_2_
  32.5 0.0 collective-permute-done.8.refs_1_
  32.5 10.1 %factor.1 = (f32[256,256]{1,0:T(8,128)}, bf16[256,2,16,128]{3,2,1,0:T(8,128)(2,1)}) custom-call(f32[72,128]{1,0:T(8,128)S(1)} %add_add_fusion.refs_0_, f32[72,128]{1,0:T(8,128)S(1)} %collective-permute-done.8.refs_1_, f32[72,128]{1,0:T(8,128)S(1)} %collective-permute-done.9.refs_2_, f32[72,128]{1,0:T(8,128)S(1)} %collective-permute-done.10.refs_3_, ...), custom_call_target="tpu_custom_call" | custom-call | tf_op jit(solution)/shard_map/factor/pallas_call | solution.py:526
  (2 shorter events, 0.0 us)
Async XLA Ops:
  1.3 1.0 %copy-start = (bf16[64,2,16,128]{3,2,1,0:T(8,128)(2,1)S(1)}, bf16[64,2,16,128]{3,2,1,0:T(8,128)(2,1)}, u32[]{:S(2)}) copy-start(bf16[64,2,16,128]{3,2,1,0:T(8,128)(2,1)} %snap_ref.3) | copy-start | bytes 1572868
  2.4 10.8 %collective-permute-start = (bf16[64,1,16,128]{3,2,1,0:T(8,128)(2,1)S(1)}, bf16[64,1,16,128]{3,2,1,0:T(8,128)(2,1)S(1)}, u32[]{:S(2)}, u32[]{:S(2)}) collective-permute-start(bf16[64,1,16,128]{3,2,1,0:T(8,128)(2,1)S(1)} %get-tuple-element.16), channel_id=1, source_target_pairs={{0,1},{1,2},{2,3},{3,4},{4,5},{5,6},{6,7},{7,8},{8,9},{9,10},{10,1... | collective-permute-start | bytes 786440 | tf_op jit(solution)/shard_map/ppermute | solution.py:559
  2.9 10.3 %collective-permute-start.1 = (bf16[64,1,16,128]{3,2,1,0:T(8,128)(2,1)S(1)}, bf16[64,1,16,128]{3,2,1,0:T(8,128)(2,1)S(1)}, u32[]{:S(2)}, u32[]{:S(2)}) collective-permute-start(bf16[64,1,16,128]{3,2,1,0:T(8,128)(2,1)S(1)} %get-tuple-element.17), channel_id=1, source_target_pairs={{1,0},{2,1},{3,2},{4,3},{5,4},{6,5},{7,6},{8,7},{9,8},{10,9},{11,1... | collective-permute-start | bytes 786440 | tf_op jit(solution)/shard_map/ppermute | solution.py:560
  8.7 1.4 %copy-start.1 = (bf16[192,2,16,128]{3,2,1,0:T(8,128)(2,1)S(1)}, bf16[192,2,16,128]{3,2,1,0:T(8,128)(2,1)}, u32[]{:S(2)}) copy-start(bf16[192,2,16,128]{3,2,1,0:T(8,128)(2,1)} %old_ref.1) | copy-start | bytes 4718596
  10.1 0.7 %copy-start.2 = (f32[192]{0:T(256)S(1)}, f32[192]{0:T(256)}, u32[]{:S(2)}) copy-start(f32[192]{0:T(256)} %param.7) | copy-start | bytes 2308
  15.3 2.4 %collective-permute-start.2 = (f32[72,128]{1,0:T(8,128)S(1)}, f32[72,128]{1,0:T(8,128)S(1)}, u32[]{:S(2)}, u32[]{:S(2)}) collective-permute-start(f32[72,128]{1,0:T(8,128)S(1)} %get-tuple-element.24), channel_id=1, source_target_pairs={{0,1},{1,0},{2,3},{3,2},{4,5},{5,4},{6,7},{7,6},{8,9},{9,8},{10,11... | collective-permute-start | bytes 110600 | tf_op jit(solution)/shard_map/ppermute | solution.py:27
  16.2 4.0 %collective-permute-start.3 = (f32[72,128]{1,0:T(8,128)S(1)}, f32[72,128]{1,0:T(8,128)S(1)}, u32[]{:S(2)}, u32[]{:S(2)}) collective-permute-start(f32[72,128]{1,0:T(8,128)S(1)} %get-tuple-element.25), channel_id=1, source_target_pairs={{0,2},{1,3},{2,0},{3,1},{4,6},{5,7},{6,4},{7,5},{8,10},{9,11},{10,... | collective-permute-start | bytes 110600 | tf_op jit(solution)/shard_map/ppermute | solution.py:27
  16.2 4.0 %collective-permute-start.4 = (f32[72,128]{1,0:T(8,128)S(1)}, f32[72,128]{1,0:T(8,128)S(1)}, u32[]{:S(2)}, u32[]{:S(2)}) collective-permute-start(f32[72,128]{1,0:T(8,128)S(1)} %get-tuple-element.26), channel_id=1, source_target_pairs={{0,3},{1,2},{2,1},{3,0},{4,7},{5,6},{6,5},{7,4},{8,11},{9,10},{10,... | collective-permute-start | bytes 110600 | tf_op jit(solution)/shard_map/ppermute | solution.py:27
  20.2 6.0 %collective-permute-start.7 = (f32[72,128]{1,0:T(8,128)S(1)}, f32[72,128]{1,0:T(8,128)S(1)}, u32[]{:S(2)}, u32[]{:S(2)}) collective-permute-start(f32[72,128]{1,0:T(8,128)S(1)} %add_add_fusion.1), channel_id=1, source_target_pairs={{0,12},{1,13},{2,14},{3,15},{4,8},{5,9},{6,10},{7,11},{8,4},{9,5},... | collective-permute-start | bytes 110600 | tf_op jit(solution)/shard_map/ppermute | solution.py:27
  23.4 4.9 %collective-permute-start.6 = (f32[72,128]{1,0:T(8,128)S(1)}, f32[72,128]{1,0:T(8,128)S(1)}, u32[]{:S(2)}, u32[]{:S(2)}) collective-permute-start(f32[72,128]{1,0:T(8,128)S(1)} %add_add_fusion.1), channel_id=1, source_target_pairs={{0,8},{1,9},{2,10},{3,11},{4,12},{5,13},{6,14},{7,15},{8,0},{9,1},... | collective-permute-start | bytes 110600 | tf_op jit(solution)/shard_map/ppermute | solution.py:27
  23.4 4.9 %collective-permute-start.5 = (f32[72,128]{1,0:T(8,128)S(1)}, f32[72,128]{1,0:T(8,128)S(1)}, u32[]{:S(2)}, u32[]{:S(2)}) collective-permute-start(f32[72,128]{1,0:T(8,128)S(1)} %add_add_fusion.1), channel_id=1, source_target_pairs={{0,4},{1,5},{2,6},{3,7},{4,0},{5,1},{6,2},{7,3},{8,12},{9,13},{10,... | collective-permute-start | bytes 110600 | tf_op jit(solution)/shard_map/ppermute | solution.py:27
  28.3 3.8 %collective-permute-start.10 = (f32[72,128]{1,0:T(8,128)S(1)}, f32[72,128]{1,0:T(8,128)S(1)}, u32[]{:S(2)}, u32[]{:S(2)}) collective-permute-start(f32[72,128]{1,0:T(8,128)S(1)} %add_add_fusion.refs_0_), channel_id=1, source_target_pairs={{0,3},{1,2},{2,1},{3,0},{4,7},{5,6},{6,5},{7,4},{8,11},{9,10},{10,... | collective-permute-start | bytes 110600 | tf_op jit(solution)/shard_map/ppermute | solution.py:27
  28.4 4.1 %collective-permute-start.9 = (f32[72,128]{1,0:T(8,128)S(1)}, f32[72,128]{1,0:T(8,128)S(1)}, u32[]{:S(2)}, u32[]{:S(2)}) collective-permute-start(f32[72,128]{1,0:T(8,128)S(1)} %add_add_fusion.refs_0_), channel_id=1, source_target_pairs={{0,2},{1,3},{2,0},{3,1},{4,6},{5,7},{6,4},{7,5},{8,10},{9,11},{10,... | collective-permute-start | bytes 110600 | tf_op jit(solution)/shard_map/ppermute | solution.py:27
  29.8 2.7 %collective-permute-start.8 = (f32[72,128]{1,0:T(8,128)S(1)}, f32[72,128]{1,0:T(8,128)S(1)}, u32[]{:S(2)}, u32[]{:S(2)}) collective-permute-start(f32[72,128]{1,0:T(8,128)S(1)} %add_add_fusion.refs_0_), channel_id=1, source_target_pairs={{0,1},{1,0},{2,3},{3,2},{4,5},{5,4},{6,7},{7,6},{8,9},{9,8},{10,11... | collective-permute-start | bytes 110600 | tf_op jit(solution)/shard_map/ppermute | solution.py:27
